TPU v7x, 32 devices: a whole 2x2x4 slice. The times are simulated.
32 devices in a mesh: row: 8 (over y, x, core), col: 4 (over z).
Axes of the slice: x: 2, y: 2, z: 4, core: 2. Of those that a mesh axis runs over, the one named last changes fastest.
Arguments:
- tokens: bfloat16 [8192, 1536], P(('row', 'col')), may hold values from -6 to 6
- attn_gain: bfloat16 [1536], P(('row', 'col')), may hold values from 0.5 to 1.5
- w_query: bfloat16 [1536, 1536], P('row', 'col'), may hold values from -0.15625 to 0.15625
- w_key: bfloat16 [1536, 512], P('row', 'col'), may hold values from -0.15625 to 0.15625
- w_value: bfloat16 [1536, 512], P('row', 'col'), may hold values from -0.15625 to 0.15625
- w_out: bfloat16 [1536, 1536], P('row', 'col'), may hold values from -0.875 to 0.875
- expert_gain: bfloat16 [1536], P(('row', 'col')), may hold values from 0.5 to 1.5
- router: bfloat16 [1536, 8], P('row', 'col'), may hold values from -0.109375 to 0.109375
- w_gate: bfloat16 [8, 1536, 1024], P('row', 'col'), may hold values from -0.15625 to 0.15625
- w_up: bfloat16 [8, 1536, 1024], P('row', 'col'), may hold values from -0.15625 to 0.15625
- w_down: bfloat16 [8, 1024, 1536], P('row', 'col'), may hold values from -0.375 to 0.375
- segment_ids: int32 [32, 256], P(('row', 'col')), may hold values from 0 to 7, never falling along the last dimension, each value on 1 to 128 neighbouring positions
- expert_ids: int32 [8192, 2], P(('row', 'col')), may hold values from 0 to 7, all different within a row; in each aligned block of 256 rows (0 to 255, 256 to 511, ...) at most 128 rows name the same one
- cotangent: bfloat16 [8192, 1536], P(('row', 'col')), may hold values from -6 to 6
Outputs:
- output: bfloat16 [8192, 1536], P(('row', 'col'))
- d_tokens: float32 [8192, 1536], P(('row', 'col'))
- grad_attn_gain: float32 [1536], P(('row', 'col'))
- grad_w_query: float32 [1536, 1536], P('row', 'col')
- grad_w_key: float32 [1536, 512], P('row', 'col')
- grad_w_value: float32 [1536, 512], P('row', 'col')
- grad_w_out: float32 [1536, 1536], P('row', 'col')
- grad_expert_gain: float32 [1536], P(('row', 'col'))
- grad_router: float32 [1536, 8], P('row', 'col')
- grad_w_gate: float32 [8, 1536, 1024], P('row', 'col')
- grad_w_up: float32 [8, 1536, 1024], P('row', 'col')
- grad_w_down: float32 [8, 1024, 1536], P('row', 'col')
Inputs may be any that keep to these rules, and one draw needn't show every extreme that they name: `expert_ids`: each row names 2 different experts. Among the 256 rows of one device no expert is named more than 128 times, and in every draw some device names some expert exactly 128 times. `segment_ids`: within each row the ids never fall and mark 8 documents of 1 to 128 tokens, one of exactly 128 tokens.
All inputs are finite; a program needn't handle non-finite values.
Results may differ from a plain program's by a relative error of at most 0.018.
Values may be sent and summed in bfloat16 or wider, within the bound.
A program may use at most 192 MiB of HBM per device.

v0:
```python
import jax
import jax.numpy as jnp
from jax import lax
from jax.sharding import PartitionSpec as P

KEY_VALUE_HEADS = 8
HEAD_SIZE = 64
TOP = 2
QUERY_PER_KEY = 3


EPSILON = 1e-05
NEGATIVE = -1e30


def rms_factor(rows_in):
    return lax.rsqrt(jnp.mean(rows_in * rows_in, axis=1, keepdims=True) + EPSILON)


def slot_tables(routes, experts, capacity):
    pair_count = routes.shape[0] * routes.shape[1]
    pair_ids = routes.reshape(-1)
    one_hot = (pair_ids[:, None] == jnp.arange(experts, dtype=jnp.int32)[None, :]).astype(jnp.int32)
    before = jnp.sum((jnp.cumsum(one_hot, axis=0) - one_hot) * one_hot, axis=1)
    slot_place = pair_ids * capacity + before
    pair_index = jnp.arange(pair_count, dtype=jnp.int32)
    slot_owner = (
        jnp.full((experts * capacity,), pair_count, jnp.int32).at[slot_place].set(pair_index)
    )
    return (slot_place, slot_owner)


def masked_scores(block_of_query, first_row, heads_of_key, segments, head_scale):
    rows_of_block = block_of_query.shape[0]
    heads_of_query = block_of_query.reshape(
        rows_of_block, KEY_VALUE_HEADS, QUERY_PER_KEY, HEAD_SIZE
    )
    scores = (
        jnp.einsum(
            "qkgd,skd->kgqs", heads_of_query, heads_of_key, preferred_element_type=jnp.float32
        )
        * head_scale
    )
    query_pos = first_row + jnp.arange(rows_of_block, dtype=jnp.int32)
    key_pos = jnp.arange(heads_of_key.shape[0], dtype=jnp.int32)
    allowed = (key_pos[None, :] <= query_pos[:, None]) & (segments[None, :] == segments[:, None])
    return (jnp.where(allowed, scores, NEGATIVE), heads_of_query)


def per_device(
    tokens,
    attn_gain,
    w_query,
    w_key,
    w_value,
    w_out,
    expert_gain,
    router,
    w_gate,
    w_up,
    w_down,
    segment_ids,
    expert_ids,
    cotangent,
):
    sequence_length = tokens.shape[0]
    model = tokens.shape[1]
    row_count = lax.axis_size("row")
    col_count = lax.axis_size("col")
    experts = w_gate.shape[0] * row_count
    capacity = 2 * sequence_length * TOP // experts
    head_scale = HEAD_SIZE ** (-0.5)
    segments = segment_ids.reshape(-1)
    col_full = (
        lax.all_gather(w_query, "col", axis=1, tiled=True),
        lax.all_gather(w_key, "col", axis=1, tiled=True),
        lax.all_gather(w_value, "col", axis=1, tiled=True),
        lax.all_gather(w_out, "col", axis=1, tiled=True),
        lax.all_gather(router, "col", axis=1, tiled=True),
        lax.all_gather(attn_gain.reshape(1, 1, -1), "col", axis=1, tiled=True),
        lax.all_gather(expert_gain.reshape(1, 1, -1), "col", axis=1, tiled=True),
        lax.all_gather(w_gate, "col", axis=1, tiled=True),
        lax.all_gather(w_up, "col", axis=1, tiled=True),
        lax.all_gather(w_down, "col", axis=1, tiled=True),
    )
    row_full = (
        lax.all_gather(col_full[0], "row", axis=0, tiled=True),
        lax.all_gather(col_full[1], "row", axis=0, tiled=True),
        lax.all_gather(col_full[2], "row", axis=0, tiled=True),
        lax.all_gather(col_full[3], "row", axis=0, tiled=True),
        lax.all_gather(col_full[4], "row", axis=0, tiled=True),
        lax.all_gather(col_full[5], "row", axis=0, tiled=True),
        lax.all_gather(col_full[6], "row", axis=0, tiled=True),
    )
    full_query, full_key, full_value, full_out, full_router = (
        row_full[0],
        row_full[1],
        row_full[2],
        row_full[3],
        row_full[4],
    )
    gain_one = row_full[5].reshape(-1).astype(jnp.float32)
    gain_two = row_full[6].reshape(-1).astype(jnp.float32)
    full_gate, full_up, full_down = (col_full[7], col_full[8], col_full[9])
    local_count = full_gate.shape[0]
    rows_f = tokens.astype(jnp.float32)
    factor_one = rms_factor(rows_f)
    normed = (rows_f * factor_one * gain_one).astype(jnp.bfloat16)
    query_rows = jnp.dot(normed, full_query, preferred_element_type=jnp.float32).astype(
        jnp.bfloat16
    )
    rows_of_key = jnp.dot(normed, full_key, preferred_element_type=jnp.float32).astype(jnp.bfloat16)
    rows_of_value = jnp.dot(normed, full_value, preferred_element_type=jnp.float32).astype(
        jnp.bfloat16
    )
    heads_of_key = rows_of_key.reshape(sequence_length, KEY_VALUE_HEADS, HEAD_SIZE)
    heads_of_value = rows_of_value.reshape(sequence_length, KEY_VALUE_HEADS, HEAD_SIZE)
    rows_of_block = min(sequence_length, 512)
    block_count = sequence_length // rows_of_block
    block_starts = jnp.arange(block_count, dtype=jnp.int32) * rows_of_block

    def attend(block_in):
        block_of_query, first_row = block_in
        scores, heads_of_query = masked_scores(
            block_of_query, first_row, heads_of_key, segments, head_scale
        )
        row_max = jnp.max(scores, axis=-1, keepdims=True)
        expo_rows = jnp.exp(scores - row_max)
        totals = jnp.sum(expo_rows, axis=-1, keepdims=True)
        probs_low = (expo_rows / totals).astype(jnp.bfloat16)
        head_mix = jnp.einsum(
            "kgqs,skd->qkgd", probs_low, heads_of_value, preferred_element_type=jnp.float32
        )
        return (
            head_mix.reshape(rows_of_block, -1).astype(jnp.bfloat16),
            (row_max + jnp.log(totals))[..., 0],
        )

    attended, log_totals = lax.map(
        attend, (query_rows.reshape(block_count, rows_of_block, -1), block_starts)
    )
    attended = attended.reshape(sequence_length, -1)
    hidden = rows_f + jnp.dot(attended, full_out, preferred_element_type=jnp.float32)
    factor_two = rms_factor(hidden)
    normed_two = (hidden * factor_two * gain_two).astype(jnp.bfloat16)
    logits = jnp.dot(normed_two, full_router, preferred_element_type=jnp.float32)
    gate_probs = jax.nn.softmax(jnp.take_along_axis(logits, expert_ids, axis=1), axis=1)
    slot_place, slot_owner = slot_tables(expert_ids, experts, capacity)
    send_rows = jnp.take(normed_two, slot_owner // TOP, axis=0, mode="fill", fill_value=0).reshape(
        experts, capacity, model
    )
    arrived = lax.all_to_all(send_rows, "row", split_axis=0, concat_axis=0, tiled=True)
    slot_rows = arrived.shape[1]
    grouped = arrived.reshape(-1, local_count, slot_rows, model)
    gate_pre = jnp.einsum("rlcd,ldh->rlch", grouped, full_gate, preferred_element_type=jnp.float32)
    up_pre = jnp.einsum("rlcd,ldh->rlch", grouped, full_up, preferred_element_type=jnp.float32)
    activation = (jax.nn.silu(gate_pre) * up_pre).astype(jnp.bfloat16)
    produced = jnp.einsum(
        "rlch,lhd->rlcd", activation, full_down, preferred_element_type=jnp.float32
    )
    produced = produced.astype(jnp.bfloat16).reshape(arrived.shape)
    exchanged = (arrived, produced)
    arrived = exchanged[0]
    back_rows = lax.all_to_all(exchanged[-1], "row", split_axis=0, concat_axis=0, tiled=True)
    returned = jnp.take(back_rows.reshape(experts * capacity, model), slot_place, axis=0).reshape(
        sequence_length, TOP, model
    )
    output = (hidden + jnp.sum(returned * gate_probs[:, :, None], axis=1)).astype(jnp.bfloat16)
    upstream = cotangent.astype(jnp.float32)
    gate_grad = jnp.sum(returned * upstream[:, None, :], axis=2)
    slot_gate = jnp.take(gate_probs.reshape(-1), slot_owner, axis=0, mode="fill", fill_value=0.0)
    slot_grad = (
        jnp.take(upstream, slot_owner // TOP, axis=0, mode="fill", fill_value=0.0)
        * slot_gate[:, None]
    )
    slot_grad = slot_grad.astype(jnp.bfloat16).reshape(experts, capacity, model)
    arrived_grad = lax.all_to_all(slot_grad, "row", split_axis=0, concat_axis=0, tiled=True)
    grouped_in = arrived.reshape(-1, local_count, capacity, model)
    grouped_grad = arrived_grad.reshape(-1, local_count, capacity, model)
    gate_pre = jnp.einsum(
        "rlcd,ldh->rlch", grouped_in, full_gate, preferred_element_type=jnp.float32
    )
    up_pre = jnp.einsum("rlcd,ldh->rlch", grouped_in, full_up, preferred_element_type=jnp.float32)
    sigma = jax.nn.sigmoid(gate_pre)
    silu_gate = gate_pre * sigma
    activation = (silu_gate * up_pre).astype(jnp.bfloat16)
    grad_down_local = jnp.einsum(
        "rlch,rlcd->lhd", activation, grouped_grad, preferred_element_type=jnp.float32
    )
    act_grad = jnp.einsum(
        "rlcd,lhd->rlch", grouped_grad, full_down, preferred_element_type=jnp.float32
    )
    up_grad = (act_grad * silu_gate).astype(jnp.bfloat16)
    pre_grad = (act_grad * up_pre * sigma * (1.0 + gate_pre * (1.0 - sigma))).astype(jnp.bfloat16)
    grad_gate_local = jnp.einsum(
        "rlcd,rlch->ldh", grouped_in, pre_grad, preferred_element_type=jnp.float32
    )
    grad_up_local = jnp.einsum(
        "rlcd,rlch->ldh", grouped_in, up_grad, preferred_element_type=jnp.float32
    )
    in_grad = jnp.einsum("rlch,ldh->rlcd", pre_grad, full_gate, preferred_element_type=jnp.float32)
    in_grad = in_grad + jnp.einsum(
        "rlch,ldh->rlcd", up_grad, full_up, preferred_element_type=jnp.float32
    )
    in_grad = in_grad.astype(jnp.bfloat16).reshape(arrived.shape)
    back_grad = lax.all_to_all(in_grad, "row", split_axis=0, concat_axis=0, tiled=True)
    pair_grad = jnp.take(back_grad.reshape(experts * capacity, model), slot_place, axis=0).reshape(
        sequence_length, TOP, model
    )
    normed_two_grad = jnp.sum(pair_grad, axis=1, dtype=jnp.float32)
    pair_mean = jnp.sum(gate_probs * gate_grad, axis=1, keepdims=True)
    pair_logit = gate_probs * (gate_grad - pair_mean)
    expert_range = jnp.arange(experts, dtype=jnp.int32)
    logit_grad = jnp.sum(
        (expert_ids[:, :, None] == expert_range[None, None, :]) * pair_logit[:, :, None], axis=1
    ).astype(jnp.bfloat16)
    grad_router_full = jnp.einsum(
        "sd,se->de", normed_two, logit_grad, preferred_element_type=jnp.float32
    )
    normed_two_grad = normed_two_grad + jnp.einsum(
        "se,de->sd", logit_grad, full_router, preferred_element_type=jnp.float32
    )
    grad_expert_gain_full = jnp.sum(normed_two_grad * hidden * factor_two, axis=0)
    scaled_two = normed_two_grad * gain_two
    hidden_grad = (
        upstream
        + factor_two * scaled_two
        - hidden * factor_two**3 * jnp.mean(scaled_two * hidden, axis=1, keepdims=True)
    )
    branch_grad = hidden_grad.astype(jnp.bfloat16)
    grad_out_full = jnp.einsum(
        "sq,sd->qd", attended, branch_grad, preferred_element_type=jnp.float32
    )
    attended_grad = jnp.einsum(
        "sd,qd->sq", branch_grad, full_out, preferred_element_type=jnp.float32
    ).astype(jnp.bfloat16)

    def attend_back(carry, block_in):
        key_acc, value_acc = carry
        block_of_query, gradient_block, first_row, log_block = block_in
        scores, heads_of_query = masked_scores(
            block_of_query, first_row, heads_of_key, segments, head_scale
        )
        soft_probs = jnp.exp(scores - log_block[..., None])
        probs_low = soft_probs.astype(jnp.bfloat16)
        gradient_heads = gradient_block.reshape(
            rows_of_block, KEY_VALUE_HEADS, QUERY_PER_KEY, HEAD_SIZE
        )
        value_acc = value_acc + jnp.einsum(
            "kgqs,qkgd->skd", probs_low, gradient_heads, preferred_element_type=jnp.float32
        )
        prob_grad = jnp.einsum(
            "qkgd,skd->kgqs", gradient_heads, heads_of_value, preferred_element_type=jnp.float32
        )
        delta_sum = jnp.sum(soft_probs * prob_grad, axis=-1, keepdims=True)
        score_grad = (soft_probs * (prob_grad - delta_sum)).astype(jnp.bfloat16)
        query_grad = (
            jnp.einsum(
                "kgqs,skd->qkgd", score_grad, heads_of_key, preferred_element_type=jnp.float32
            )
            * head_scale
        )
        key_acc = (
            key_acc
            + jnp.einsum(
                "kgqs,qkgd->skd", score_grad, heads_of_query, preferred_element_type=jnp.float32
            )
            * head_scale
        )
        return ((key_acc, value_acc), query_grad.astype(jnp.bfloat16).reshape(rows_of_block, -1))

    heads_zeroed = jnp.zeros((sequence_length, KEY_VALUE_HEADS, HEAD_SIZE), jnp.float32)
    sums_back, query_grad = lax.scan(
        attend_back,
        (heads_zeroed, heads_zeroed),
        (
            query_rows.reshape(block_count, rows_of_block, -1),
            attended_grad.reshape(block_count, rows_of_block, -1),
            block_starts,
            log_totals,
        ),
    )
    query_grad = query_grad.reshape(sequence_length, -1)
    key_grad = sums_back[0].reshape(sequence_length, -1).astype(jnp.bfloat16)
    value_grad = sums_back[1].reshape(sequence_length, -1).astype(jnp.bfloat16)
    grad_query_full = jnp.einsum(
        "sd,sq->dq", normed, query_grad, preferred_element_type=jnp.float32
    )
    grad_key_full = jnp.einsum("sd,sq->dq", normed, key_grad, preferred_element_type=jnp.float32)
    grad_value_full = jnp.einsum(
        "sd,sq->dq", normed, value_grad, preferred_element_type=jnp.float32
    )
    normed_grad = jnp.einsum(
        "sq,dq->sd", query_grad, full_query, preferred_element_type=jnp.float32
    )
    normed_grad = normed_grad + jnp.einsum(
        "sq,dq->sd", key_grad, full_key, preferred_element_type=jnp.float32
    )
    normed_grad = normed_grad + jnp.einsum(
        "sq,dq->sd", value_grad, full_value, preferred_element_type=jnp.float32
    )
    grad_attn_gain_full = jnp.sum(normed_grad * rows_f * factor_one, axis=0)
    scaled_one = normed_grad * gain_one
    d_tokens = (
        hidden_grad
        + factor_one * scaled_one
        - rows_f * factor_one**3 * jnp.mean(scaled_one * rows_f, axis=1, keepdims=True)
    )
    gain_piece = model // (row_count * col_count)
    gain_attn_terms = grad_attn_gain_full.reshape(row_count, col_count, gain_piece)
    gain_expert_terms = grad_expert_gain_full.reshape(row_count, col_count, gain_piece)
    rows_done = (
        lax.psum_scatter(
            grad_query_full.astype(jnp.bfloat16), "row", scatter_dimension=0, tiled=True
        ).astype(jnp.float32),
        lax.psum_scatter(
            grad_key_full.astype(jnp.bfloat16), "row", scatter_dimension=0, tiled=True
        ).astype(jnp.float32),
        lax.psum_scatter(
            grad_value_full.astype(jnp.bfloat16), "row", scatter_dimension=0, tiled=True
        ).astype(jnp.float32),
        lax.psum_scatter(
            grad_out_full.astype(jnp.bfloat16), "row", scatter_dimension=0, tiled=True
        ).astype(jnp.float32),
        lax.psum_scatter(
            grad_router_full.astype(jnp.bfloat16), "row", scatter_dimension=0, tiled=True
        ).astype(jnp.float32),
        lax.psum_scatter(
            gain_attn_terms.astype(jnp.bfloat16), "row", scatter_dimension=0, tiled=True
        ).astype(jnp.float32),
        lax.psum_scatter(
            gain_expert_terms.astype(jnp.bfloat16), "row", scatter_dimension=0, tiled=True
        ).astype(jnp.float32),
    )
    finals = (
        lax.psum_scatter(rows_done[0], "col", scatter_dimension=1, tiled=True),
        lax.psum_scatter(rows_done[1], "col", scatter_dimension=1, tiled=True),
        lax.psum_scatter(rows_done[2], "col", scatter_dimension=1, tiled=True),
        lax.psum_scatter(rows_done[3], "col", scatter_dimension=1, tiled=True),
        lax.psum_scatter(rows_done[4], "col", scatter_dimension=1, tiled=True),
        lax.psum_scatter(rows_done[5], "col", scatter_dimension=1, tiled=True),
        lax.psum_scatter(rows_done[6], "col", scatter_dimension=1, tiled=True),
        lax.psum_scatter(grad_gate_local, "col", scatter_dimension=1, tiled=True),
        lax.psum_scatter(grad_up_local, "col", scatter_dimension=1, tiled=True),
        lax.psum_scatter(grad_down_local, "col", scatter_dimension=1, tiled=True),
    )
    return (
        output,
        d_tokens,
        finals[5].reshape(-1),
        finals[0],
        finals[1],
        finals[2],
        finals[3],
        finals[6].reshape(-1),
        finals[4],
        finals[7],
        finals[8],
        finals[9],
    )


def solution(mesh):
    in_specs = (
        P(("row", "col"), None),
        P(("row", "col")),
        P("row", "col"),
        P("row", "col"),
        P("row", "col"),
        P("row", "col"),
        P(("row", "col")),
        P("row", "col"),
        P("row", "col", None),
        P("row", "col", None),
        P("row", "col", None),
        P(("row", "col"), None),
        P(("row", "col"), None),
        P(("row", "col"), None),
    )
    out_specs = (
        P(("row", "col"), None),
        P(("row", "col"), None),
        P(("row", "col")),
        P("row", "col"),
        P("row", "col"),
        P("row", "col"),
        P("row", "col"),
        P(("row", "col")),
        P("row", "col"),
        P("row", "col", None),
        P("row", "col", None),
        P("row", "col", None),
    )
    return jax.shard_map(
        per_device, mesh=mesh, in_specs=in_specs, out_specs=out_specs, check_vma=False
    )
```

profile of v0, /device:TPU:0, one launch (start us, length us, event | category | flops | bytes accessed | tf_op | source)
XLA Modules:
  0.0 1266.3 jit_solution(5466588651172880569)
XLA Ops:
  7.3 16.2 %all_gather.55 = bf16[192,512]{1,0:T(8,128)(2,1)} all-gather(bf16[192,128]{1,0:T(8,128)(2,1)} %param.19), channel_id=1, replica_groups=mesh['row'=8,'col'=4] {'col'}, dimensions={1}, use_global_device_ids=true | all-gather | bytes 245760 | tf_op jit(solution)/shard_map/all_gather | solution.py:76
  23.6 13.4 %all_gather.53 = bf16[192,512]{1,0:T(8,128)(2,1)} all-gather(bf16[192,128]{1,0:T(8,128)(2,1)} %param.20), channel_id=1, replica_groups=mesh['row'=8,'col'=4] {'col'}, dimensions={1}, use_global_device_ids=true | all-gather | bytes 245760 | tf_op jit(solution)/shard_map/all_gather | solution.py:77
  37.0 17.1 %all_gather.57 = bf16[192,1536]{1,0:T(8,128)(2,1)} all-gather(bf16[192,384]{1,0:T(8,128)(2,1)} %param.18), channel_id=1, replica_groups=mesh['row'=8,'col'=4] {'col'}, dimensions={1}, use_global_device_ids=true | all-gather | bytes 737280 | tf_op jit(solution)/shard_map/all_gather | solution.py:75
  54.2 16.8 %all_gather.59 = bf16[192,1536]{1,0:T(8,128)(2,1)} all-gather(bf16[192,384]{1,0:T(8,128)(2,1)} %param.21), channel_id=1, replica_groups=mesh['row'=8,'col'=4] {'col'}, dimensions={1}, use_global_device_ids=true | all-gather | bytes 737280 | tf_op jit(solution)/shard_map/all_gather | solution.py:78
  78.7 10.4 all-reduce.9
  89.2 8.9 all_gather.52
  99.2 8.9 all_gather.62
  125.7 31.6 %all-gather.18.cloned.1.call-done = bf16[1536,1536]{1,0:T(8,128)(2,1)} async-done(((bf16[192,1536]{1,0:T(8,128)(2,1)}), bf16[1536,1536]{1,0:T(8,128)(2,1)}) %all-gather.18.cloned.1.call-update) | async-done | bytes 4718608 | tf_op jit(solution)/shard_map/all_gather | solution.py:90
  177.2 45.0 %all-gather.22.cloned.1.call-done = bf16[1,1536,1024]{2,1,0:T(8,128)(2,1)} async-done(((bf16[1,384,1024]{2,1,0:T(8,128)(2,1)}), bf16[1,1536,1024]{2,1,0:T(8,128)(2,1)}) %all-gather.22.cloned.1.call-update) | async-done | bytes 3145744 | tf_op jit(solution)/shard_map/all_gather | solution.py:83
  222.2 8.3 fusion.20
  230.5 55.3 %all-gather.20.cloned.1.call-done = bf16[1,1536,1024]{2,1,0:T(8,128)(2,1)} async-done(((bf16[1,384,1024]{2,1,0:T(8,128)(2,1)}), bf16[1,1536,1024]{2,1,0:T(8,128)(2,1)}) %all-gather.20.cloned.1.call-update) | async-done | bytes 3145744 | tf_op jit(solution)/shard_map/all_gather | solution.py:82
  297.0 52.6 %all-gather.24.cloned.1.call-done = bf16[1,1024,1536]{2,1,0:T(8,128)(2,1)} async-done(((bf16[1,256,1536]{2,1,0:T(8,128)(2,1)}), bf16[1,1024,1536]{2,1,0:T(8,128)(2,1)}) %all-gather.24.cloned.1.call-update) | async-done | bytes 3145744 | tf_op jit(solution)/shard_map/all_gather | solution.py:84
  349.5 7.6 convolution_convert_fusion.2
  369.7 8.3 all-gather.2
  378.0 24.8 %all-gather.3 = bf16[8,192,8]{1,2,0:T(8,128)(2,1)S(1)} all-gather(bf16[1,192,8]{1,2,0:T(8,128)(2,1)S(1)} %bitcast.245), channel_id=1, replica_groups=mesh['row'=8,'col'=4] {'row'}, dimensions={0}, use_global_device_ids=true | all-gather | bytes 27648 | tf_op jit(solution)/shard_map/all_gather | solution.py:91
  432.8 40.7 %all_to_all.20 = bf16[8,128,1536]{2,1,0:T(8,128)(2,1)S(1)} all-to-all(bf16[8,128,1536]{2,1,0:T(8,128)(2,1)S(1)} %multiply_convert_fusion), channel_id=1, replica_groups=mesh['row'=8,'col'=4] {'row'}, dimensions={0} | all-to-all | bytes 6291456 | tf_op jit(solution)/shard_map/all_to_all | solution.py:177
  495.6 37.2 %all-to-all-done.3 = bf16[8,128,1536]{2,1,0:T(8,128)(2,1)} async-done(((bf16[8,128,1536]{2,1,0:T(8,128)(2,1)}), bf16[8,128,1536]{2,1,0:T(8,128)(2,1)}, u32[]{:S(2)}, u32[]{:S(2)}) %all-to-all-start.3) | async-done | bytes 3145760 | tf_op jit(solution)/shard_map/all_to_all | solution.py:206
  549.2 7.6 multiply_reduce_fusion.1
  562.0 6.9 reduce_sum.148
  620.3 40.6 %reduce-scatter.21.cloned.1.call-done = bf16[192,512]{1,0:T(8,128)(2,1)} async-done(((bf16[1536,512]{1,0:T(8,128)(2,1)}), bf16[192,512]{1,0:T(8,128)(2,1)}) %reduce-scatter.21.cloned.1.call-update) | async-done | bytes 196624 | tf_op jit(solution)/shard_map/reduce_scatter | solution.py:316
  662.7 55.4 %reduce-scatter.17.cloned.1.call-done = bf16[192,1536]{1,0:T(8,128)(2,1)} async-done(((bf16[1536,1536]{1,0:T(8,128)(2,1)}), bf16[192,1536]{1,0:T(8,128)(2,1)}) %reduce-scatter.17.cloned.1.call-update) | async-done | bytes 589840 | tf_op jit(solution)/shard_map/reduce_scatter | solution.py:313
  720.4 55.5 %reduce-scatter.29.cloned.1.call-done = bf16[192,1536]{1,0:T(8,128)(2,1)} async-done(((bf16[1536,1536]{1,0:T(8,128)(2,1)}), bf16[192,1536]{1,0:T(8,128)(2,1)}) %reduce-scatter.29.cloned.1.call-update) | async-done | bytes 589840 | tf_op jit(solution)/shard_map/reduce_scatter | solution.py:322
  778.2 8.6 convolution_bitcast_fusion
  787.2 8.7 convolution_bitcast_fusion.2
  796.0 8.6 convolution_bitcast_fusion.1
  821.1 22.9 %all-reduce.8 = (bf16[8,4,48]{2,1,0:T(4,128)(2,1)S(1)}, bf16[8,4,48]{2,1,0:T(4,128)(2,1)S(1)}) all-reduce(bf16[8,4,48]{2,1,0:T(4,128)(2,1)S(1)} %convert_element_type.241, bf16[8,4,48]{2,1,0:T(4,128)(2,1)S(1)} %convert_element_type.252), channel_id=4, replica_groups=mesh['row'=8,'col'=4] {'row'}, use_global_device_ids=true, to_apply=%region_19.21.clone | all-reduce | flops 3072 | bytes 12288
  844.6 18.8 %all-reduce.7 = (f32[1,4,48]{2,1,0:T(4,128)S(1)}, f32[1,4,48]{2,1,0:T(4,128)S(1)}, f32[192,8]{0,1:T(8,128)S(1)}) all-reduce(f32[1,4,48]{2,1,0:T(4,128)S(1)} %get-tuple-element.105, f32[1,4,48]{2,1,0:T(4,128)S(1)} %get-tuple-element.106, bf16[192,8]{0,1:T(8,128)(2,1)S(1)} %copy.143), channel_id=5, replica_groups=mesh['row'=8,'col'=4] {'col'}, use_global_device_ids=true, to_apply=%region_20.22.clone | all-reduce | flops 1920 | bytes 12288
  869.3 18.9 %reduce-scatter.19.cloned.1.call-done = f32[192,384]{1,0:T(8,128)} async-done(((f32[192,1536]{1,0:T(8,128)}), f32[192,384]{1,0:T(8,128)}) %reduce-scatter.19.cloned.1.call-update) | async-done | bytes 294928 | tf_op jit(solution)/shard_map/reduce_scatter | solution.py:336
  888.2 30.7 %reduce-scatter.31.cloned.1.call-done = f32[192,384]{1,0:T(8,128)} async-done(((f32[192,1536]{1,0:T(8,128)}), f32[192,384]{1,0:T(8,128)}) %reduce-scatter.31.cloned.1.call-update) | async-done | bytes 294928 | tf_op jit(solution)/shard_map/reduce_scatter | solution.py:339
  918.9 112.2 %reduce-scatter.37.cloned.1.call-done = f32[1,256,1536]{2,1,0:T(8,128)} async-done(((f32[1,1024,1536]{2,1,0:T(8,128)}), f32[1,256,1536]{2,1,0:T(8,128)}) %reduce-scatter.37.cloned.1.call-update) | async-done | bytes 1572880 | tf_op jit(solution)/shard_map/reduce_scatter | solution.py:345
  1031.1 114.0 %reduce-scatter.33.cloned.1.call-done = f32[1,384,1024]{2,1,0:T(8,128)} async-done(((f32[1,1536,1024]{2,1,0:T(8,128)}), f32[1,384,1024]{2,1,0:T(8,128)}) %reduce-scatter.33.cloned.1.call-update) | async-done | bytes 1572880 | tf_op jit(solution)/shard_map/reduce_scatter | solution.py:343
  1145.1 114.2 %reduce-scatter.35.cloned.1.call-done = f32[1,384,1024]{2,1,0:T(8,128)} async-done(((f32[1,1536,1024]{2,1,0:T(8,128)}), f32[1,384,1024]{2,1,0:T(8,128)}) %reduce-scatter.35.cloned.1.call-update) | async-done | bytes 1572880 | tf_op jit(solution)/shard_map/reduce_scatter | solution.py:344
  (257 shorter events, 223.3 us)
Async XLA Ops:
  7.2 69.8 %copy-start.34 = (u32[32]{0:T(128)S(1)}, u32[32]{0:T(128)}, u32[]{:S(2)}) copy-start(u32[32]{0:T(128)} %constant.178) | copy-start | bytes 388
  7.2 65.0 %copy-start.31 = (s32[256,2]{0,1:T(2,128)S(1)}, s32[256,2]{0,1:T(2,128)}, u32[]{:S(2)}) copy-start(s32[256,2]{0,1:T(2,128)} %param.28) | copy-start | bytes 6148
  7.2 71.0 %copy-start.39 = (bf16[48]{0:T(256)(128)(2,1)S(1)}, bf16[48]{0:T(256)(128)(2,1)}, u32[]{:S(2)}) copy-start(bf16[48]{0:T(256)(128)(2,1)} %param.17) | copy-start | bytes 292
  7.2 71.3 %copy-start.40 = (bf16[48]{0:T(256)(128)(2,1)S(1)}, bf16[48]{0:T(256)(128)(2,1)}, u32[]{:S(2)}) copy-start(bf16[48]{0:T(256)(128)(2,1)} %param.22) | copy-start | bytes 292
  7.2 91.0 %copy-start.1 = (bf16[256,1536]{1,0:T(8,128)(2,1)S(1)}, bf16[256,1536]{1,0:T(8,128)(2,1)}, u32[]{:S(2)}) copy-start(bf16[256,1536]{1,0:T(8,128)(2,1)} %param.16) | copy-start | bytes 2359300
  7.2 100.9 %all-gather.14.cloned.1.call-start = ((), (), s32[]{:S(2)}) async-start(), calls=%async_computation.17 | async-start | bytes 1769472 | tf_op jit(solution)/shard_map/all_gather | solution.py:88
  23.5 75.5 %copy-start.32 = (s32[1,256]{1,0:T(1,128)S(1)}, s32[1,256]{1,0:T(1,128)}, u32[]{:S(2)}) copy-start(s32[1,256]{1,0:T(1,128)} %param.27) | copy-start | bytes 3076
  23.5 86.8 %all-gather.12.cloned.1.call-start = ((), (), s32[]{:S(2)}) async-start(), calls=%async_computation.16 | async-start | bytes 1769472 | tf_op jit(solution)/shard_map/all_gather | solution.py:89
  37.0 79.6 %all-gather.16.cloned.1.call-start = ((), (), s32[]{:S(2)}) async-start(), calls=%async_computation.18 | async-start | bytes 5308416 | tf_op jit(solution)/shard_map/all_gather | solution.py:87
  54.2 103.1 %all-gather.18.cloned.1.call-start = ((), (), s32[]{:S(2)}) async-start(), calls=%async_computation.19 | async-start | bytes 5308416 | tf_op jit(solution)/shard_map/all_gather | solution.py:90
  71.0 151.2 %all-gather.22.cloned.1.call-start = ((), (), s32[]{:S(2)}) async-start(), calls=%async_computation.21 | async-start | bytes 3932160 | tf_op jit(solution)/shard_map/all_gather | solution.py:83
  71.6 214.2 %all-gather.20.cloned.1.call-start = ((), (), s32[]{:S(2)}) async-start(), calls=%async_computation.20 | async-start | bytes 3932160 | tf_op jit(solution)/shard_map/all_gather | solution.py:82
  171.9 50.3 %all-to-all-start = ((bf16[8,128,1536]{2,1,0:T(8,128)(2,1)}), bf16[8,128,1536]{2,1,0:T(8,128)(2,1)}, u32[]{:S(2)}, u32[]{:S(2)}) async-start(bf16[8,128,1536]{2,1,0:T(8,128)(2,1)} %broadcast_select_fusion), calls=%async_computation | async-start | bytes 6291456 | tf_op jit(solution)/shard_map/all_to_all | solution.py:152
  176.4 173.1 %all-gather.24.cloned.1.call-start = ((), (), s32[]{:S(2)}) async-start(), calls=%async_computation.22 | async-start | bytes 3932160 | tf_op jit(solution)/shard_map/all_gather | solution.py:84
  357.1 56.6 %all-to-all-start.1 = ((bf16[8,128,1536]{2,1,0:T(8,128)(2,1)}), bf16[8,128,1536]{2,1,0:T(8,128)(2,1)}, u32[]{:S(2)}, u32[]{:S(2)}) async-start(bf16[8,128,1536]{2,1,0:T(8,128)(2,1)} %convolution_convert_fusion.2), calls=%async_computation.1 | async-start | bytes 6291456 | tf_op jit(solution)/shard_map/all_to_all | solution.py:164
  429.4 44.1 %copy-start.15 = (f32[8,128,1024]{2,1,0:T(8,128)S(1)}, f32[8,128,1024]{2,1,0:T(8,128)}, u32[]{:S(2)}) copy-start(f32[8,128,1024]{2,1,0:T(8,128)} %copy-done.14) | copy-start | bytes 12582916
  429.4 44.1 %copy-start.38 = (bf16[1,1024,1536]{2,1,0:T(8,128)(2,1)S(1)}, bf16[1,1024,1536]{2,1,0:T(8,128)(2,1)}, u32[]{:S(2)}) copy-start(bf16[1,1024,1536]{2,1,0:T(8,128)(2,1)} %all-gather.24.cloned.1.call-done) | copy-start | bytes 9437188
  432.8 40.7 %copy-start.13 = (f32[8,128,1024]{2,1,0:T(8,128)S(1)}, f32[8,128,1024]{2,1,0:T(8,128)}, u32[]{:S(2)}) copy-start(f32[8,128,1024]{2,1,0:T(8,128)} %fusion.20) | copy-start | bytes 12582916
  490.4 42.4 %all-to-all-start.3 = ((bf16[8,128,1536]{2,1,0:T(8,128)(2,1)}), bf16[8,128,1536]{2,1,0:T(8,128)(2,1)}, u32[]{:S(2)}, u32[]{:S(2)}) async-start(bf16[8,128,1536]{2,1,0:T(8,128)(2,1)} %add_convert_fusion), calls=%async_computation.3 | async-start | bytes 6291456 | tf_op jit(solution)/shard_map/all_to_all | solution.py:206
  494.9 123.6 %reduce-scatter.25.cloned.1.call-start = ((), (), s32[]{:S(2)}) async-start(), calls=%async_computation.27 | async-start | bytes 1769472 | tf_op jit(solution)/shard_map/reduce_scatter | solution.py:319
  583.0 77.9 %reduce-scatter.21.cloned.1.call-start = ((), (), s32[]{:S(2)}) async-start(), calls=%async_computation.25 | async-start | bytes 1769472 | tf_op jit(solution)/shard_map/reduce_scatter | solution.py:316
  597.0 121.1 %reduce-scatter.17.cloned.1.call-start = ((), (), s32[]{:S(2)}) async-start(), calls=%async_computation.23 | async-start | bytes 5308416 | tf_op jit(solution)/shard_map/reduce_scatter | solution.py:313
  604.3 171.6 %reduce-scatter.29.cloned.1.call-start = ((), (), s32[]{:S(2)}) async-start(), calls=%async_computation.29 | async-start | bytes 5308416 | tf_op jit(solution)/shard_map/reduce_scatter | solution.py:322
  610.4 202.2 %reduce-scatter.39.cloned.1.call-start = ((), (), s32[]{:S(2)}) async-start(), calls=%async_computation.34 | async-start | bytes 442368
  611.6 257.7 %reduce-scatter.27.cloned.1.call-start = ((), (), s32[]{:S(2)}) async-start(), calls=%async_computation.28 | async-start | bytes 491520 | tf_op jit(solution)/shard_map/reduce_scatter | solution.py:338
  620.3 249.0 %reduce-scatter.23.cloned.1.call-start = ((), (), s32[]{:S(2)}) async-start(), calls=%async_computation.26 | async-start | bytes 491520 | tf_op jit(solution)/shard_map/reduce_scatter | solution.py:337
  662.7 225.6 %reduce-scatter.19.cloned.1.call-start = ((), (), s32[]{:S(2)}) async-start(), calls=%async_computation.24 | async-start | bytes 1474560 | tf_op jit(solution)/shard_map/reduce_scatter | solution.py:336
  720.3 198.6 %reduce-scatter.31.cloned.1.call-start = ((), (), s32[]{:S(2)}) async-start(), calls=%async_computation.30 | async-start | bytes 1474560 | tf_op jit(solution)/shard_map/reduce_scatter | solution.py:339
  778.2 252.9 %reduce-scatter.37.cloned.1.call-start = ((), (), s32[]{:S(2)}) async-start(), calls=%async_computation.33 | async-start | bytes 7864320 | tf_op jit(solution)/shard_map/reduce_scatter | solution.py:345
  786.9 358.2 %reduce-scatter.33.cloned.1.call-start = ((), (), s32[]{:S(2)}) async-start(), calls=%async_computation.31 | async-start | bytes 7864320 | tf_op jit(solution)/shard_map/reduce_scatter | solution.py:343
  795.9 463.4 %reduce-scatter.35.cloned.1.call-start = ((), (), s32[]{:S(2)}) async-start(), calls=%async_computation.32 | async-start | bytes 7864320 | tf_op jit(solution)/shard_map/reduce_scatter | solution.py:344
  818.9 47.5 %copy-start.33 = (f32[256]{0:T(256)S(1)}, f32[256]{0:T(256)}, u32[]{:S(2)}) copy-start(f32[256]{0:T(256)} %get-tuple-element.89) | copy-start | bytes 3076
  (35 other events, 218.9 us)
Sparse Core Ops, SparseCore 0:
  23.6 24.3 all-gather.13
  49.9 25.6 all-gather.11
  77.5 38.9 all-gather.15
  118.3 38.8 all-gather.17
  158.6 63.4 all-gather.21
  223.6 62.1 all-gather.19
  287.3 62.1 all-gather.23
  583.1 35.3 reduce-scatter.24
  622.4 38.4 reduce-scatter.20
  664.2 53.8 reduce-scatter.16
  721.9 53.8 reduce-scatter.28
  778.8 33.8 reduce-scatter.38
  815.5 20.5 reduce-scatter.26
  838.9 19.0 reduce-scatter.22
  860.8 27.4 reduce-scatter.18
  891.0 27.8 reduce-scatter.30
  921.6 109.4 reduce-scatter.36
  1033.8 111.2 reduce-scatter.32
  1148.0 111.2 reduce-scatter.34
where the time goes:
time: 1280 us; the launch traced here: 1270 us
  waiting for transfers between devices  782 us (61%)
  blocking collectives  207 us (16%)
  matrix products  114 us (9%)
  local copies, waits for them, and re-layouts  76.1 us (6%)
  other arithmetic  55.4 us (4%)
  between operations  16.6 us (1%)
  starting transfers between devices  15.3 us (1%)
    reduce_scatter x1, waiting for transfers between devices, per_device(): lax.psum_scatter(grad_up_local, 'col', scatter_dimension=1, tiled=True)  114 us
    reduce_scatter x1, waiting for transfers between devices, per_device(): lax.psum_scatter(grad_gate_local, 'col', scatter_dimension=1, tiled=True)  114 us
    reduce_scatter x1, waiting for transfers between devices, per_device(): lax.psum_scatter(grad_down_local, 'col', scatter_dimension=1, tiled=True)  112 us
    reduce_scatter x1, waiting for transfers between devices, per_device(): lax.psum_scatter(grad_out_full.astype(jnp.bfloat16), 'row', scatter_dimen...  55.5 us
    reduce_scatter x1, waiting for transfers between devices, per_device(): lax.psum_scatter(grad_query_full.astype(jnp.bfloat16), 'row', scatter_dim...  55.4 us
    all_gather x1, waiting for transfers between devices, per_device(): lax.all_gather(w_gate, 'col', axis=1, tiled=True)  55.3 us
    all_gather x1, waiting for transfers between devices, per_device(): lax.all_gather(w_down, 'col', axis=1, tiled=True)  52.6 us
    unnamed x3, blocking collectives  52.1 us
  transfers between devices with their start and end apart: 22, of which 16 were waited for; matrix products, arithmetic and copies ran while one was open for 11% of the time, Pallas kernels for 0%

commit v1 on v0

v1 whole, which is shorter than its diff:
```python
import functools

import jax
import jax.numpy as jnp
from jax import lax
from jax.experimental import pallas as pl
from jax.experimental.pallas import tpu as pltpu
from jax.sharding import PartitionSpec as P

KEY_VALUE_HEADS = 8
HEAD_SIZE = 64
TOP = 2
QUERY_PER_KEY = 3


EPSILON = 1e-05
NEGATIVE = -1e30


MESH = pl.DeviceIdType.MESH
ANY = pl.BlockSpec(memory_space=pl.ANY)


def row_at(row, flip):
    y, x, core = row // 4, (row // 2) % 2, row % 2
    return (
        (y + flip // 4) % 2 * 4 + (x + (flip // 2) % 2) % 2 * 2 + (core + flip % 2) % 2
    )


def remote(source, target, send, receive, device):
    return pltpu.make_async_remote_copy(
        source, target, send, receive, device_id=device, device_id_type=MESH
    )


def greet(row_flips, col_steps):
    row, col = lax.axis_index("row"), lax.axis_index("col")
    sem = pltpu.get_barrier_semaphore()
    for flip in row_flips:
        pl.semaphore_signal(
            sem, inc=1, device_id={"row": row_at(row, flip)}, device_id_type=MESH
        )
    for step in col_steps:
        pl.semaphore_signal(
            sem, inc=1, device_id={"col": (col + step) % 4}, device_id_type=MESH
        )
    pl.semaphore_wait(sem, len(row_flips) + len(col_steps))


def unit_order(col, k):
    table = ((0, 1, 2, 3), (1, 0, 2, 3), (2, 3, 1, 0), (3, 2, 1, 0))
    out = table[3][k]
    for c in (2, 1, 0):
        out = jnp.where(col == c, table[c][k], out)
    return out


X, Y, SIB = 2, 4, 1


def plane_send(view, row, ss, rs):
    for i, flip in enumerate((X, Y, SIB)):
        remote(view(row), view(row), ss(i), rs(i), {"row": row_at(row, flip)}).start()


def plane_forward(view, halves, row, ss, rs):
    first, second = halves
    from_x, from_y = row_at(row, X), row_at(row, Y)
    sib = {"row": row_at(row, SIB)}
    remote(view(from_x), view(from_x), ss(0), rs(0), sib).wait_recv()
    remote(first(from_x), first(from_x), ss(3), rs(3), {"row": from_y}).start()
    remote(view(from_x), view(from_x), ss(5), rs(5), sib).start()
    remote(view(from_y), view(from_y), ss(1), rs(1), sib).wait_recv()
    remote(second(from_y), second(from_y), ss(4), rs(4), {"row": from_x}).start()
    remote(view(from_y), view(from_y), ss(6), rs(6), sib).start()


def plane_last(view, halves, row, ss, rs):
    first, second = halves
    diag = row_at(row, X + Y)
    sib = {"row": row_at(row, SIB)}
    remote(first(diag), first(diag), ss(3), rs(3), sib).wait_recv()
    remote(first(diag), first(diag), ss(7), rs(7), sib).start()
    remote(second(diag), second(diag), ss(4), rs(4), sib).wait_recv()
    remote(second(diag), second(diag), ss(8), rs(8), sib).start()


def plane_finish(view, halves, row, ss, rs):
    first, second = halves
    sib_row = row_at(row, SIB)
    sib = {"row": sib_row}
    whole = view(sib_row)
    remote(whole, whole, ss(2), rs(2), sib).wait_recv()
    for i, flip in ((5, X), (6, Y)):
        block = view(row_at(sib_row, flip))
        remote(block, block, ss(i), rs(i), sib).wait_recv()
    far = row_at(sib_row, X + Y)
    remote(first(far), first(far), ss(7), rs(7), sib).wait_recv()
    remote(second(far), second(far), ss(8), rs(8), sib).wait_recv()
    for i in range(9):
        block = view(row) if i in (0, 1, 2, 5, 6) else (first(row) if i in (3, 7) else second(row))
        remote(block, block, ss(i), rs(i), sib).wait_send()


def pick(ref, cols, halves_rows):
    block, cut = halves_rows

    def at(start, size):
        def view(r):
            rows = pl.ds(pl.multiple_of(r * block + start, 16), size)
            if cols is None:
                return ref.at[rows, :]
            return ref.at[rows, pl.ds(pl.multiple_of(cols[0], 128), cols[1])]

        return view

    return at(0, block), (at(0, cut), at(cut, block - cut))


def gather_kernel(own_a, own_b, own_s, own_c, full_a, full_b, full_s, full_c,
                  zss, zrs, ass, ars, bss, brs, css, crs, s_zs, s_zr, s_ps, s_pr, loc):
    row, col = lax.axis_index("row"), lax.axis_index("col")
    greet(range(1, 6), (1, 2, 3)) if False else greet(range(1, 8), (1, 2, 3))
    block = own_a.shape[0]
    width_a, width_b = own_a.shape[1], own_b.shape[1]
    rows_c = own_c.shape[0]
    cut = block // 2

    def views(c):
        va = pick(full_a, (c * width_a, width_a), (block, cut))
        vb = pick(full_b, (c * width_b, width_b), (block, cut))
        return va, vb

    for i, step in enumerate((1, 2, 3)):
        remote(own_s, full_s.at[col, row], s_zs.at[i], s_zr.at[i], {"col": (col + step) % 4}).start()
    (view_a, _), (view_b, _) = views(col)
    copies = [
        pltpu.make_async_copy(own_a, view_a(row), loc.at[0]),
        pltpu.make_async_copy(own_b, view_b(row), loc.at[1]),
        pltpu.make_async_copy(own_s, full_s.at[col, row], loc.at[2]),
        pltpu.make_async_copy(own_c, full_c.at[pl.ds(row * rows_c, rows_c), :], loc.at[3]),
    ]
    for copy in copies:
        copy.start()

    def along(c, source_a, source_b, right, left):
        (va, _), (vb, _) = views(c)
        for d, (cond, step) in enumerate(((right, 1), (left, 3))):
            @pl.when(cond)
            def _():
                there = {"col": (col + step) % 4}
                remote(source_a, va(row), zss.at[0, c, d], zrs.at[0, c], there).start()
                remote(source_b, vb(row), zss.at[1, c, d], zrs.at[1, c], there).start()

    along(col, own_a, own_b, col < 3, col > 0)
    for copy in copies:
        copy.wait()
    for k in range(4):
        c = unit_order(col, k)
        (va, ha), (vb, hb) = views(c)
        if k > 0:
            remote(va(row), va(row), zss.at[0, c, 0], zrs.at[0, c], {"col": (col + 1) % 4}).wait_recv()
            remote(vb(row), vb(row), zss.at[1, c, 0], zrs.at[1, c], {"col": (col + 1) % 4}).wait_recv()
            along(c, va(row), vb(row), (c < col) & (col < 3), (c > col) & (col > 0))
        plane_send(va, row, lambda i: ass.at[c, i], lambda i: ars.at[c, i])
        plane_send(vb, row, lambda i: bss.at[c, i], lambda i: brs.at[c, i])
        if k > 0:
            p = unit_order(col, k - 1)
            (va, ha), (vb, hb) = views(p)
            plane_forward(va, ha, row, lambda i: ass.at[p, i], lambda i: ars.at[p, i])
            plane_forward(vb, hb, row, lambda i: bss.at[p, i], lambda i: brs.at[p, i])
        if k > 1:
            q = unit_order(col, k - 2)
            (va, ha), (vb, hb) = views(q)
            plane_last(va, ha, row, lambda i: ass.at[q, i], lambda i: ars.at[q, i])
            plane_last(vb, hb, row, lambda i: bss.at[q, i], lambda i: brs.at[q, i])
        if k == 0:
            for i, step in enumerate((3, 2, 1)):
                remote(own_s, full_s.at[(col + step) % 4, row], s_zs.at[i], s_zr.at[i], {"col": (col + 1) % 4}).wait()
            for i in range(1, 8):
                remote(full_s.at[:, row], full_s.at[:, row], s_ps.at[i - 1], s_pr.at[i - 1], {"row": row_at(row, i)}).start()
    vc, hc = pick(full_c, None, (rows_c, rows_c // 2))
    csv, crv = (lambda i: css.at[i]), (lambda i: crs.at[i])
    plane_send(vc, row, csv, crv)
    for k in (3,):
        p = unit_order(col, k)
        (va, ha), (vb, hb) = views(p)
        plane_forward(va, ha, row, lambda i: ass.at[p, i], lambda i: ars.at[p, i])
        plane_forward(vb, hb, row, lambda i: bss.at[p, i], lambda i: brs.at[p, i])
    for k in (2, 3):
        p = unit_order(col, k)
        (va, ha), (vb, hb) = views(p)
        plane_last(va, ha, row, lambda i: ass.at[p, i], lambda i: ars.at[p, i])
        plane_last(vb, hb, row, lambda i: bss.at[p, i], lambda i: brs.at[p, i])
    plane_forward(vc, hc, row, csv, crv)
    plane_last(vc, hc, row, csv, crv)
    for c in range(4):
        (va, ha), (vb, hb) = views(c)
        plane_finish(va, ha, row, lambda i: ass.at[c, i], lambda i: ars.at[c, i])
        plane_finish(vb, hb, row, lambda i: bss.at[c, i], lambda i: brs.at[c, i])
    plane_finish(vc, hc, row, csv, crv)
    for i in range(1, 8):
        there = row_at(row, i)
        remote(full_s.at[:, there], full_s.at[:, there], s_ps.at[i - 1], s_pr.at[i - 1], {"row": there}).wait()
    for k in range(4):
        c = unit_order(col, k)
        (va, ha), (vb, hb) = views(c)
        right = (c <= col) & (col < 3)
        left = (c >= col) & (col > 0)
        for d, cond in enumerate((right, left)):
            @pl.when(cond)
            def _():
                there = {"col": (col + 1) % 4}
                remote(va(row), va(row), zss.at[0, c, d], zrs.at[0, c], there).wait_send()
                remote(vb(row), vb(row), zss.at[1, c, d], zrs.at[1, c], there).wait_send()


def gather_attention(own_a, own_b, own_s, own_c):
    sems = pltpu.SemaphoreType.DMA
    block, rows_c = own_a.shape[0], own_c.shape[0]
    return pl.pallas_call(
        gather_kernel,
        out_shape=(
            jax.ShapeDtypeStruct((block * 8, own_a.shape[1] * 4), own_a.dtype),
            jax.ShapeDtypeStruct((block * 8, own_b.shape[1] * 4), own_b.dtype),
            jax.ShapeDtypeStruct((4, 8) + own_s.shape, own_s.dtype),
            jax.ShapeDtypeStruct((8 * rows_c, own_c.shape[1]), own_c.dtype),
        ),
        in_specs=[ANY] * 4,
        out_specs=(ANY,) * 4,
        scratch_shapes=[
            sems((2, 4, 2)), sems((2, 4)),
            sems((4, 9)), sems((4, 9)), sems((4, 9)), sems((4, 9)),
            sems((9,)), sems((9,)),
            sems((3,)), sems((3,)), sems((7,)), sems((7,)), sems((4,)),
        ],
        compiler_params=pltpu.CompilerParams(collective_id=0, has_side_effects=True),
        cost_estimate=pl.CostEstimate(flops=0, bytes_accessed=200_000_000, transcendentals=0),
    )(own_a, own_b, own_s, own_c)


def spread_kernel(own_c, own_g, full_c, full_g, css, crs, gss, grs, loc):
    row = lax.axis_index("row")
    greet(range(1, 8), ())
    rows_c = own_c.shape[0]
    copies = [
        pltpu.make_async_copy(own_c, full_c.at[pl.ds(row * rows_c, rows_c), :], loc.at[0]),
        pltpu.make_async_copy(own_g, full_g.at[row], loc.at[1]),
    ]
    for copy in copies:
        copy.start()
    for i in range(1, 8):
        remote(own_g, full_g.at[row], gss.at[i - 1], grs.at[i - 1], {"row": row_at(row, i)}).start()
    for copy in copies:
        copy.wait()
    vc, hc = pick(full_c, None, (rows_c, rows_c // 2))
    csv, crv = (lambda i: css.at[i]), (lambda i: crs.at[i])
    plane_send(vc, row, csv, crv)
    plane_forward(vc, hc, row, csv, crv)
    plane_last(vc, hc, row, csv, crv)
    plane_finish(vc, hc, row, csv, crv)
    for i in range(1, 8):
        there = row_at(row, i)
        remote(own_g, full_g.at[there], gss.at[i - 1], grs.at[i - 1], {"row": there}).wait()


def spread_tokens(own_c, own_g):
    sems = pltpu.SemaphoreType.DMA
    return pl.pallas_call(
        spread_kernel,
        out_shape=(
            jax.ShapeDtypeStruct((8 * own_c.shape[0], own_c.shape[1]), own_c.dtype),
            jax.ShapeDtypeStruct((8,) + own_g.shape, own_g.dtype),
        ),
        in_specs=[ANY] * 2,
        out_specs=(ANY,) * 2,
        scratch_shapes=[sems((9,)), sems((9,)), sems((7,)), sems((7,)), sems((2,))],
        compiler_params=pltpu.CompilerParams(collective_id=1, has_side_effects=True),
        cost_estimate=pl.CostEstimate(flops=0, bytes_accessed=100_000_000, transcendentals=0),
    )(own_c, own_g)


def add_into(target, term):
    target[...] = (target[...].astype(jnp.float32) + term[...].astype(jnp.float32)).astype(target.dtype)


def reduce_kernel(grad_a, grad_b, grad_s, sum_a, sum_b, sum_s,
                  own, rec_sib, rec_one, rec_two, rec_z, s_own, s_rec, s_mid, s_zrec,
                  lss, lrs, ss1, rs1, ss2, rs2, zss, zrs, lo, s_ss, s_rs, sz_ss, sz_rs):
    row, col = lax.axis_index("row"), lax.axis_index("col")
    core = row % 2
    chip = row // 2
    cy, cx = chip // 2, chip % 2
    block, width = own.shape[2], own.shape[3]
    width_a = sum_a.shape[1]
    width_b = width - width_a
    cut = block // 2
    greet(range(1, 8), (1, 2, 3))
    sib = {"row": row_at(row, SIB)}
    to_x, to_y = {"row": row_at(row, X)}, {"row": row_at(row, Y)}

    def parts(c, q, of_core):
        rows = pl.ds(pl.multiple_of((q * 2 + of_core) * block, 16), block)
        return (
            grad_a.at[rows, pl.ds(pl.multiple_of(c * width_a, 128), width_a)],
            grad_b.at[rows, pl.ds(pl.multiple_of(c * width_b, 128), width_b)],
        )

    for i in range(1, 8):
        there = row_at(row, i)
        remote(grad_s.at[there], s_rec.at[i - 1], s_ss.at[i - 1], s_rs.at[i - 1], {"row": there}).start()
    def start_first(c, carry):
        for q in range(4):
            pa, pb = parts(c, q, 1 - core)
            remote(pa, rec_sib.at[c, q, :, pl.ds(0, width_a)], ss1.at[c, q, 0], rs1.at[c, q, 0], sib).start()
            remote(pb, rec_sib.at[c, q, :, pl.ds(width_a, width_b)], ss1.at[c, q, 1], rs1.at[c, q, 1], sib).start()
            pa, pb = parts(c, q, core)
            pltpu.make_async_copy(pa, own.at[c, q, :, pl.ds(0, width_a)], lss.at[c, q, 0]).start()
            pltpu.make_async_copy(pb, own.at[c, q, :, pl.ds(width_a, width_b)], lss.at[c, q, 1]).start()
        return carry
    lax.fori_loop(0, 4, start_first, 0)
    own_small = pltpu.make_async_copy(grad_s.at[row], s_own, lo.at[0])
    own_small.start()

    def chip_sum(c):
        for q in range(4):
            pa, pb = parts(c, q, core)
            for i, (p, off, w) in enumerate(((pa, 0, width_a), (pb, width_a, width_b))):
                pltpu.make_async_copy(p, own.at[c, q, :, pl.ds(off, w)], lss.at[c, q, i]).wait()
                remote(p, rec_sib.at[c, q, :, pl.ds(off, w)], ss1.at[c, q, i], rs1.at[c, q, i], sib).wait_recv()
            add_into(own.at[c, q], rec_sib.at[c, q])

    top, low = pl.ds(0, cut), pl.ds(cut, block - cut)

    def one(c):
        for j in range(2):
            yield remote(own.at[c, j * 2 + 1 - cx, top, :], rec_one.at[c, 0, j], ss2.at[c, 0, j], rs2.at[c, 0, j], to_x)
            yield remote(own.at[c, (1 - cy) * 2 + j, low, :], rec_one.at[c, 1, j], ss2.at[c, 1, j], rs2.at[c, 1, j], to_y)

    def one_sum(c):
        for copy in one(c):
            copy.wait_recv()
        for j in range(2):
            add_into(own.at[c, j * 2 + cx, top, :], rec_one.at[c, 0, j])
            add_into(own.at[c, cy * 2 + j, low, :], rec_one.at[c, 1, j])

    def two(c):
        yield remote(own.at[c, (1 - cy) * 2 + cx, top, :], rec_two.at[c, 0], ss2.at[c, 0, 2], rs2.at[c, 0, 2], to_y)
        yield remote(own.at[c, cy * 2 + 1 - cx, low, :], rec_two.at[c, 1], ss2.at[c, 1, 2], rs2.at[c, 1, 2], to_x)

    def two_sum(c):
        for copy in two(c):
            copy.wait_recv()
        add_into(own.at[c, chip, top, :], rec_two.at[c, 0])
        add_into(own.at[c, chip, low, :], rec_two.at[c, 1])

    def column(step):
        there = (col + step) % 4
        return remote(own.at[there, chip], rec_z.at[step - 1], zss.at[step - 1], zrs.at[step - 1], {"col": there})

    def stages(k, carry):
        @pl.when(k < 4)
        def _():
            chip_sum(k)
            for copy in one(k):
                copy.start()
        @pl.when((k >= 1) & (k < 5))
        def _():
            one_sum(k - 1)
            for copy in two(k - 1):
                copy.start()
        @pl.when(k >= 2)
        def _():
            two_sum(k - 2)
        for step in (1, 2, 3):
            @pl.when((k >= 2) & ((col + step) % 4 == k - 2))
            def _():
                column(step).start()
        return carry
    lax.fori_loop(0, 6, stages, 0)

    own_small.wait()
    total = s_own[...]
    for i in range(1, 8):
        there = row_at(row, i)
        remote(grad_s.at[there], s_rec.at[i - 1], s_ss.at[i - 1], s_rs.at[i - 1], {"row": there}).wait()
        total = total + s_rec[i - 1]
    s_mid[...] = total

    def small(step):
        there = (col + step) % 4
        return remote(s_mid.at[there], s_zrec.at[step - 1], sz_ss.at[step - 1], sz_rs.at[step - 1], {"col": there})

    for step in (1, 2, 3):
        small(step).start()
    for step in (1, 2, 3):
        small(step).wait()
    sum_s[...] = s_mid[col] + s_zrec[0] + s_zrec[1] + s_zrec[2]
    for step in (1, 2, 3):
        column(step).wait_recv()
    for start in range(0, block, 32):
        rows = pl.ds(start, 32)
        total = own[col, chip, rows, :].astype(jnp.float32)
        for step in range(3):
            total = total + rec_z[step, rows, :].astype(jnp.float32)
        sum_a[rows, :] = total[:, :width_a]
        sum_b[rows, :] = total[:, width_a:]
    for step in (1, 2, 3):
        column(step).wait_send()

    def sent(c, carry):
        for q in range(4):
            pa, pb = parts(c, q, 1 - core)
            remote(pa, rec_sib.at[c, q, :, pl.ds(0, width_a)], ss1.at[c, q, 0], rs1.at[c, q, 0], sib).wait_send()
            remote(pb, rec_sib.at[c, q, :, pl.ds(width_a, width_b)], ss1.at[c, q, 1], rs1.at[c, q, 1], sib).wait_send()
        for copy in one(c):
            copy.wait_send()
        for copy in two(c):
            copy.wait_send()
        return carry
    lax.fori_loop(0, 4, sent, 0)


def reduce_attention(grad_a, grad_b, grad_s):
    sems = pltpu.SemaphoreType.DMA
    block = grad_a.shape[0] // 8
    width_a, width_b = grad_a.shape[1] // 4, grad_b.shape[1] // 4
    width = width_a + width_b
    cut = block // 2
    low = grad_a.dtype
    vm = pl.BlockSpec(memory_space=pltpu.VMEM)
    small = grad_s.shape[1:]
    return pl.pallas_call(
        reduce_kernel,
        out_shape=(
            jax.ShapeDtypeStruct((block, width_a), jnp.float32),
            jax.ShapeDtypeStruct((block, width_b), jnp.float32),
            jax.ShapeDtypeStruct(small[1:], jnp.float32),
        ),
        in_specs=[ANY] * 3,
        out_specs=(vm,) * 3,
        scratch_shapes=[
            pltpu.VMEM((4, 4, block, width), low),
            pltpu.VMEM((4, 4, block, width), low),
            pltpu.VMEM((4, 2, 2, cut, width), low),
            pltpu.VMEM((4, 2, cut, width), low),
            pltpu.VMEM((3, block, width), low),
            pltpu.VMEM(small, jnp.float32),
            pltpu.VMEM((7,) + small, jnp.float32),
            pltpu.VMEM(small, jnp.float32),
            pltpu.VMEM((3,) + small[1:], jnp.float32),
            sems((4, 4, 2)), sems((1,)),
            sems((4, 4, 2)), sems((4, 4, 2)),
            sems((4, 2, 3)), sems((4, 2, 3)),
            sems((3,)), sems((3,)), sems((1,)),
            sems((7,)), sems((7,)), sems((3,)), sems((3,)),
        ],
        compiler_params=pltpu.CompilerParams(
            collective_id=2, has_side_effects=True, vmem_limit_bytes=48 * 2**20
        ),
        cost_estimate=pl.CostEstimate(flops=0, bytes_accessed=250_000_000, transcendentals=0),
    )(grad_a, grad_b, grad_s)


def rms_factor(rows_in):
    return lax.rsqrt(jnp.mean(rows_in * rows_in, axis=1, keepdims=True) + EPSILON)


def dot(a, b):
    return jnp.dot(a, b, preferred_element_type=jnp.float32)


def dot_t(a, b):
    return lax.dot_general(a, b, (((1,), (1,)), ((), ())), preferred_element_type=jnp.float32)


def t_dot(a, b):
    return lax.dot_general(a, b, (((0,), (0,)), ((), ())), preferred_element_type=jnp.float32)


def on_small_slice():
    return lax.axis_size("row") == 8 and lax.axis_size("col") == 4


def gather_all(own_a, own_b, own_s, own_c):
    if on_small_slice():
        return gather_attention(own_a, own_b, own_s, own_c)
    col_a = lax.all_gather(own_a, "col", axis=1, tiled=True)
    col_b = lax.all_gather(own_b, "col", axis=1, tiled=True)
    small = lax.all_gather(lax.all_gather(own_s, "col", axis=0), "row", axis=1)
    return (
        lax.all_gather(col_a, "row", axis=0, tiled=True),
        lax.all_gather(col_b, "row", axis=0, tiled=True),
        small,
        lax.all_gather(own_c, "row", axis=0, tiled=True),
    )


def spread(own_c, own_g):
    if on_small_slice():
        return spread_tokens(own_c, own_g)
    return (
        lax.all_gather(own_c, "row", axis=0, tiled=True),
        lax.all_gather(own_g, "row", axis=0),
    )


def reduce_all(grad_a, grad_b, grad_s):
    if on_small_slice():
        return reduce_attention(grad_a, grad_b, grad_s)

    def both(g):
        plane = lax.psum_scatter(g, "row", scatter_dimension=0, tiled=True).astype(jnp.float32)
        return lax.psum_scatter(plane, "col", scatter_dimension=1, tiled=True)

    small = lax.psum_scatter(grad_s, "row", scatter_dimension=0, tiled=False)
    return both(grad_a), both(grad_b), lax.psum_scatter(small, "col", scatter_dimension=0, tiled=False)


def masked_scores(queries, heads_of_key, segments, head_scale):
    length = queries.shape[0]
    heads_of_query = queries.reshape(length, KEY_VALUE_HEADS, QUERY_PER_KEY, HEAD_SIZE)
    scores = (
        jnp.einsum("qkgd,skd->kgqs", heads_of_query, heads_of_key, preferred_element_type=jnp.float32)
        * head_scale
    )
    pos = jnp.arange(length, dtype=jnp.int32)
    allowed = (pos[None, :] <= pos[:, None]) & (segments[None, :] == segments[:, None])
    return jnp.where(allowed, scores, NEGATIVE), heads_of_query


def per_device(
    tokens,
    attn_gain,
    w_query,
    w_key,
    w_value,
    w_out,
    expert_gain,
    router,
    w_gate,
    w_up,
    w_down,
    segment_ids,
    expert_ids,
    cotangent,
):
    length, model = tokens.shape
    rows, cols = lax.axis_size("row"), lax.axis_size("col")
    experts = w_gate.shape[0] * rows
    capacity = 2 * length * TOP // experts
    head_scale = HEAD_SIZE ** (-0.5)
    segments = segment_ids.reshape(-1)
    block, width_q = w_query.shape
    width_k = w_key.shape[1]
    width_a = width_q + 2 * width_k
    piece = attn_gain.shape[0]
    router_cols = router.shape[1]

    full_gate = lax.all_gather(w_gate, "col", axis=1, tiled=True)[0]
    full_up = lax.all_gather(w_up, "col", axis=1, tiled=True)[0]
    full_down = lax.all_gather(w_down, "col", axis=1, tiled=True)[0]

    lane = 256

    def row_of(v):
        return jnp.pad(v, ((0, 0), (0, lane - v.shape[1])))

    own_s = jnp.concatenate(
        [row_of(router.T), row_of(attn_gain[None]), row_of(expert_gain[None])], axis=0
    )
    own_s = jnp.pad(own_s, ((0, 16 - own_s.shape[0]), (0, 0)))
    own_a = jnp.concatenate([w_query, w_key, w_value], axis=1)
    full_a, full_out, small, plane_upstream = gather_all(own_a, w_out, own_s, cotangent)
    full_router = small[:, :, :router_cols, :block].transpose(1, 3, 0, 2).reshape(model, experts)
    gain_one = small[:, :, router_cols, :piece].transpose(1, 0, 2).reshape(model).astype(jnp.float32)
    gain_two = small[:, :, router_cols + 1, :piece].transpose(1, 0, 2).reshape(model).astype(jnp.float32)

    rows_f = tokens.astype(jnp.float32)
    factor_one = rms_factor(rows_f)
    normed = (rows_f * factor_one * gain_one).astype(jnp.bfloat16)
    qkv = dot(normed, full_a).astype(jnp.bfloat16).reshape(length, cols, width_a)
    query_rows = qkv[:, :, :width_q].reshape(length, -1)
    rows_of_key = qkv[:, :, width_q : width_q + width_k].reshape(length, -1)
    rows_of_value = qkv[:, :, width_q + width_k :].reshape(length, -1)
    heads_of_key = rows_of_key.reshape(length, KEY_VALUE_HEADS, HEAD_SIZE)
    heads_of_value = rows_of_value.reshape(length, KEY_VALUE_HEADS, HEAD_SIZE)

    scores, heads_of_query = masked_scores(query_rows, heads_of_key, segments, head_scale)
    row_max = jnp.max(scores, axis=-1, keepdims=True)
    expo_rows = jnp.exp(scores - row_max)
    totals = jnp.sum(expo_rows, axis=-1, keepdims=True)
    soft_probs = expo_rows / totals
    probs_low = soft_probs.astype(jnp.bfloat16)
    attended = (
        jnp.einsum("kgqs,skd->qkgd", probs_low, heads_of_value, preferred_element_type=jnp.float32)
        .reshape(length, -1)
        .astype(jnp.bfloat16)
    )
    hidden = rows_f + dot(attended, full_out)
    factor_two = rms_factor(hidden)
    normed_two = (hidden * factor_two * gain_two).astype(jnp.bfloat16)
    logits = dot(normed_two, full_router)

    named = expert_ids[:, :, None] == jnp.arange(experts, dtype=jnp.int32)[None, None, :]
    chosen = jnp.sum(jnp.where(named, logits[:, None, :], 0.0), axis=2)
    gate_probs = jax.nn.softmax(chosen, axis=1)
    gate_table = jnp.sum(jnp.where(named, gate_probs[:, :, None], 0.0), axis=1)
    gate_table = jnp.where(jnp.any(named, axis=1), gate_table, -1.0)
    plane_normed, plane_gate = spread(normed_two, gate_table.T)
    plane_normed = plane_normed.reshape(rows, length, model)
    plane_upstream = plane_upstream.reshape(rows, length, model)
    mine = lax.dynamic_index_in_dim(plane_gate, lax.axis_index("row"), axis=1, keepdims=False)
    routed = mine >= 0.0
    place = jnp.cumsum(routed.astype(jnp.int32), axis=1) - 1
    slots = jnp.arange(capacity, dtype=jnp.int32)
    chosen_rows = (
        (place[:, None, :] == slots[None, :, None]) & routed[:, None, :]
    ).astype(jnp.bfloat16)
    grouped = jnp.einsum(
        "rct,rtd->rcd", chosen_rows, plane_normed, preferred_element_type=jnp.float32
    ).astype(jnp.bfloat16).reshape(rows * capacity, model)
    weighted = (plane_upstream.astype(jnp.float32) * mine[:, :, None]).astype(jnp.bfloat16)
    grouped_grad = jnp.einsum(
        "rct,rtd->rcd", chosen_rows, weighted, preferred_element_type=jnp.float32
    ).astype(jnp.bfloat16).reshape(rows * capacity, model)

    gate_pre = dot(grouped, full_gate)
    up_pre = dot(grouped, full_up)
    sigma = jax.nn.sigmoid(gate_pre)
    silu_gate = gate_pre * sigma
    activation = (silu_gate * up_pre).astype(jnp.bfloat16)
    grad_down_local = t_dot(activation, grouped_grad).astype(jnp.bfloat16)
    grad_down = lax.psum_scatter(grad_down_local, "col", scatter_dimension=0, tiled=True)
    produced = dot(activation, full_down).astype(jnp.bfloat16)
    back_rows = lax.all_to_all(
        produced.reshape(rows, capacity, model), "row", split_axis=0, concat_axis=0, tiled=True
    ).reshape(experts * capacity, model)
    act_grad = dot_t(grouped_grad, full_down)
    up_grad = (act_grad * silu_gate).astype(jnp.bfloat16)
    pre_grad = (act_grad * up_pre * sigma * (1.0 + gate_pre * (1.0 - sigma))).astype(jnp.bfloat16)
    in_grad = (dot_t(pre_grad, full_gate) + dot_t(up_grad, full_up)).astype(jnp.bfloat16)
    back_grad = lax.all_to_all(
        in_grad.reshape(rows, capacity, model), "row", split_axis=0, concat_axis=0, tiled=True
    ).reshape(experts * capacity, model)
    grad_gate_local = t_dot(grouped, pre_grad).astype(jnp.bfloat16)
    grad_gate = lax.psum_scatter(grad_gate_local, "col", scatter_dimension=0, tiled=True)
    grad_up_local = t_dot(grouped, up_grad).astype(jnp.bfloat16)
    grad_up = lax.psum_scatter(grad_up_local, "col", scatter_dimension=0, tiled=True)

    any_named = jnp.any(named, axis=1)
    before = jnp.cumsum(any_named.astype(jnp.int32), axis=0) - 1
    slot_of = jnp.sum(
        jnp.where(named, before[:, None, :] + jnp.arange(experts, dtype=jnp.int32) * capacity, 0),
        axis=2,
    )
    all_slots = jnp.arange(experts * capacity, dtype=jnp.int32)
    from_slot = (slot_of.T[:, :, None] == all_slots[None, None, :]).astype(jnp.bfloat16)
    returned = [dot(from_slot[k], back_rows) for k in range(TOP)]
    upstream = cotangent.astype(jnp.float32)
    output = (
        hidden + sum(returned[k] * gate_probs[:, k : k + 1] for k in range(TOP))
    ).astype(jnp.bfloat16)
    gate_grad = jnp.stack([jnp.sum(returned[k] * upstream, axis=1) for k in range(TOP)], axis=1)
    normed_two_grad = dot(from_slot[0] + from_slot[1], back_grad)
    pair_mean = jnp.sum(gate_probs * gate_grad, axis=1, keepdims=True)
    pair_logit = gate_probs * (gate_grad - pair_mean)
    logit_grad = jnp.sum(jnp.where(named, pair_logit[:, :, None], 0.0), axis=1).astype(jnp.bfloat16)
    grad_router = t_dot(normed_two, logit_grad)
    normed_two_grad = normed_two_grad + dot_t(logit_grad, full_router)
    grad_expert_gain = jnp.sum(normed_two_grad * hidden * factor_two, axis=0)
    scaled_two = normed_two_grad * gain_two
    hidden_grad = (
        upstream
        + factor_two * scaled_two
        - hidden * factor_two**3 * jnp.mean(scaled_two * hidden, axis=1, keepdims=True)
    )
    branch_grad = hidden_grad.astype(jnp.bfloat16)
    grad_out_full = t_dot(attended, branch_grad).astype(jnp.bfloat16)
    attended_grad = dot_t(branch_grad, full_out).astype(jnp.bfloat16)

    gradient_heads = attended_grad.reshape(length, KEY_VALUE_HEADS, QUERY_PER_KEY, HEAD_SIZE)
    value_grad = jnp.einsum(
        "kgqs,qkgd->skd", probs_low, gradient_heads, preferred_element_type=jnp.float32
    )
    prob_grad = jnp.einsum(
        "qkgd,skd->kgqs", gradient_heads, heads_of_value, preferred_element_type=jnp.float32
    )
    delta_sum = jnp.sum(soft_probs * prob_grad, axis=-1, keepdims=True)
    score_grad = (soft_probs * (prob_grad - delta_sum)).astype(jnp.bfloat16)
    query_grad = (
        jnp.einsum("kgqs,skd->qkgd", score_grad, heads_of_key, preferred_element_type=jnp.float32)
        * head_scale
    )
    key_grad = (
        jnp.einsum("kgqs,qkgd->skd", score_grad, heads_of_query, preferred_element_type=jnp.float32)
        * head_scale
    )
    qkv_grad = jnp.concatenate(
        [
            query_grad.astype(jnp.bfloat16).reshape(length, cols, width_q),
            key_grad.astype(jnp.bfloat16).reshape(length, cols, width_k),
            value_grad.astype(jnp.bfloat16).reshape(length, cols, width_k),
        ],
        axis=2,
    ).reshape(length, cols * width_a)
    grad_a_full = t_dot(normed, qkv_grad).astype(jnp.bfloat16)
    normed_grad = dot_t(qkv_grad, full_a)
    grad_attn_gain = jnp.sum(normed_grad * rows_f * factor_one, axis=0)
    scaled_one = normed_grad * gain_one
    d_tokens = (
        hidden_grad
        + factor_one * scaled_one
        - rows_f * factor_one**3 * jnp.mean(scaled_one * rows_f, axis=1, keepdims=True)
    )
    grad_s = jnp.concatenate(
        [
            jnp.pad(
                grad_router.reshape(rows, block, cols, router_cols).transpose(0, 2, 3, 1),
                ((0, 0), (0, 0), (0, 0), (0, lane - block)),
            ),
            jnp.pad(
                jnp.stack([grad_attn_gain, grad_expert_gain])
                .reshape(2, rows, cols, piece)
                .transpose(1, 2, 0, 3),
                ((0, 0), (0, 0), (0, 6 - router_cols), (0, lane - piece)),
            ),
        ],
        axis=2,
    )
    sum_a, sum_out, sum_s = reduce_all(grad_a_full, grad_out_full, grad_s)
    return (
        output,
        d_tokens,
        sum_s[router_cols, :piece],
        sum_a[:, :width_q],
        sum_a[:, width_q : width_q + width_k],
        sum_a[:, width_q + width_k :],
        sum_out,
        sum_s[router_cols + 1, :piece],
        sum_s[:router_cols, :block].T,
        grad_gate.astype(jnp.float32)[None],
        grad_up.astype(jnp.float32)[None],
        grad_down.astype(jnp.float32)[None],
    )


def solution(mesh):
    in_specs = (
        P(("row", "col"), None),
        P(("row", "col")),
        P("row", "col"),
        P("row", "col"),
        P("row", "col"),
        P("row", "col"),
        P(("row", "col")),
        P("row", "col"),
        P("row", "col", None),
        P("row", "col", None),
        P("row", "col", None),
        P(("row", "col"), None),
        P(("row", "col"), None),
        P(("row", "col"), None),
    )
    out_specs = (
        P(("row", "col"), None),
        P(("row", "col"), None),
        P(("row", "col")),
        P("row", "col"),
        P("row", "col"),
        P("row", "col"),
        P("row", "col"),
        P(("row", "col")),
        P("row", "col"),
        P("row", "col", None),
        P("row", "col", None),
        P("row", "col", None),
    )
    return jax.shard_map(
        per_device, mesh=mesh, in_specs=in_specs, out_specs=out_specs, check_vma=False
    )
```

time: 1280 us -> 530 us (0.41)
  waiting for transfers between devices: 782 us -> 47.3 us
  Pallas kernels: 0 us -> 282 us
  blocking collectives: 207 us -> 0 us
  local copies, waits for them, and re-layouts: 76.1 us -> 14 us
  other arithmetic: 55.4 us -> 20.8 us
  matrix products: 114 us -> 131 us
    reduce_scatter x11 -> x3, waiting for transfers between devices: 548 us -> 0.01 us  [the longest x1 0.01 us: per_device(): lax.psum_scatter(grad_up_local, 'col', scatter_dimension=0, tiled=True)]
    pallas_call x0 -> x3, Pallas kernels: none -> 282 us  [the longest x1 135 us: gather_attention(): pl.pallas_call(gather_kernel, out_shape=(jax.ShapeDtypeStruct((block * 8,...]
    all_gather x7 -> x3, waiting for transfers between devices: 188 us -> 0.01 us  [the longest x1 0.01 us: per_device(): full_up = lax.all_gather(w_up, 'col', axis=1, tiled=True)[0]]
    all_gather x8 -> x0, blocking collectives: 114 us -> none  [the longest x1 24.8 us: per_device(): lax.all_gather(col_full[4], 'row', axis=0, tiled=True)]
    unnamed x3 -> x0, blocking collectives: 52.1 us -> none
    all_to_all x1 -> x0, blocking collectives: 40.7 us -> none  [per_device(): lax.all_to_all(slot_grad, 'row', split_axis=0, concat_axis=0, tiled=True)]
    gather x8 -> x0, local copies, waits for them, and re-layouts: 34.9 us -> none  [the longest x1 6.87 us: per_device(): jnp.take(gate_probs.reshape(-1), slot_owner, axis=0, mode='fill', fill_va...]
    reduce_sum x7 -> x5, other arithmetic: 18.3 us -> 0.11 us  [the longest x1 0.05 us: per_device(): chosen = jnp.sum(jnp.where(named, logits[:, None, :], 0.0), axis=2)]
  transfers between devices with their start and end apart: 22 -> 8, of which waited for: 16 -> 2; matrix products, arithmetic and copies ran while one was open for 11% -> 27% of each run, Pallas kernels for 0% -> 54%
where the time goes in v1:
time: 530 us; the launch traced here: 519 us
  Pallas kernels  282 us (53%)
  matrix products  131 us (25%)
  waiting for transfers between devices  47.3 us (9%)
  other arithmetic  20.8 us (4%)
  between operations  15.2 us (3%)
  local copies, waits for them, and re-layouts  14 us (3%)
  starting transfers between devices  9.38 us (2%)
    pallas_call x1, Pallas kernels, gather_attention(): pl.pallas_call(gather_kernel, out_shape=(jax.ShapeDtypeStruct((block * 8,...  135 us
    pallas_call x1, Pallas kernels, reduce_attention(): pl.pallas_call(reduce_kernel, out_shape=(jax.ShapeDtypeStruct((block, wid...  88.6 us
    pallas_call x1, Pallas kernels, spread_tokens(): pl.pallas_call(spread_kernel, out_shape=(jax.ShapeDtypeStruct((8 * own_c....  58.6 us
    dot_general x9, matrix products, dot(): return jnp.dot(a, b, preferred_element_type=jnp.float32)  45.1 us
    dot_general x6, matrix products, dot_t(): lax.dot_general(a, b, (((1,), (1,)), ((), ())), preferred_element_type=jn...  29.9 us
    dot_general x6, matrix products, t_dot(): lax.dot_general(a, b, (((0,), (0,)), ((), ())), preferred_element_type=jn...  28.9 us
    all_to_all x1, waiting for transfers between devices, per_device(): lax.all_to_all(produced.reshape(rows, capacity, model), 'row', split_axis...  25.8 us
    all_to_all x1, waiting for transfers between devices, per_device(): lax.all_to_all(in_grad.reshape(rows, capacity, model), 'row', split_axis=...  19.4 us
  transfers between devices with their start and end apart: 8, of which 2 were waited for; matrix products, arithmetic and copies ran while one was open for 27% of the time, Pallas kernels for 54%

profile of v1, /device:TPU:0, one launch (start us, length us, event | category | flops | bytes accessed | tf_op | source)
XLA Modules:
  0.0 519.4 jit_solution(1748648068609307293)
XLA Ops:
  12.5 134.8 %shard_map.229 = (bf16[1536,2560]{1,0:T(8,128)(2,1)}, bf16[1536,1536]{1,0:T(8,128)(2,1)}, bf16[4,8,16,256]{3,2,1,0:T(8,128)(2,1)}, bf16[2048,1536]{1,0:T(8,128)(2,1)}) custom-call(bf16[192,640]{1,0:T(8,128)(2,1)} %pad_maximum_fusion.1.own_a, bf16[192,384]{1,0:T(8,128)(2,1)} %own_b.1, bf16[16,256]{1,0:T(8,128)(2,1)} %pad.26.own_s, bf16[256,1536]{1,0:T(8,128)(2,1)} %own_c.1), custom_call_target="tpu_custom_call" | custom-call | bytes 200000000 | tf_op jit(solution)/shard_map/pallas_call | solution.py:222
  149.2 5.5 %convolution_convert_fusion.2 = bf16[256,2560]{1,0:T(8,128)(2,1)S(1)} fusion(bf16[1536,2560]{1,0:T(8,128)(2,1)} %get-tuple-element.22, bf16[256,1536]{1,0:T(8,128)(2,1)S(1)} %copy-done, f32[1536]{0:T(1024)S(1)} %reshape.306, f32[256]{0:T(256)S(1)} %get-tuple-element.55), kind=kOutput, calls=%fused_computation.21 | convolution fusion | flops 2015494144 | bytes 9968640 | tf_op jit(solution)/shard_map/dot_general | solution.py:471
  159.2 4.6 fusion.92
  163.9 3.5 fusion.41
  167.4 4.1 multiply_reduce_fusion.2
  173.0 58.6 %shard_map.230 = (bf16[2048,1536]{1,0:T(8,128)(2,1)}, f32[8,8,256]{2,1,0:T(8,128)}) custom-call(bf16[256,1536]{1,0:T(8,128)(2,1)} %copy-done.4, f32[8,256]{1,0:T(8,128)} %select_bitcast_fusion.own_g), custom_call_target="tpu_custom_call" | custom-call | bytes 100000000 | tf_op jit(solution)/shard_map/pallas_call | solution.py:270
  233.9 5.5 %convolution_convert_fusion.3 = bf16[8,128,1536]{2,1,0:T(8,128)(2,1)} fusion(bf16[8,256,1536]{2,1,0:T(8,128)(2,1)} %bitcast.202, s32[8,256]{1,0:T(8,128)S(1)} %add_bitcast_fusion, pred[8,256]{1,0:T(8,128)(4,1)S(1)} %bitcast.232), kind=kOutput, calls=%fused_computation.23 | convolution fusion | flops 807403520 | bytes 9447424 | tf_op jit(solution)/shard_map/rct,rtd->rcd/dot_general | solution.py:621
  239.3 6.0 %fusion.10 = bf16[8,128,1536]{2,1,0:T(8,128)(2,1)} fusion(bf16[8,256,1536]{2,1,0:T(8,128)(2,1)} %bitcast.213, f32[8,256]{1,0:T(8,128)S(1)} %bitcast.237, s32[8,256]{1,0:T(8,128)S(1)} %add_bitcast_fusion, pred[8,256]{1,0:T(8,128)(4,1)S(1)} %bitcast.233), kind=kOutput, calls=%fused_computation.22 | convolution fusion | flops 816840704 | bytes 9455616 | tf_op jit(solution)/shard_map/rct,rtd->rcd/dot_general | solution.py:625
  245.4 8.2 %fusion.17 = f32[1024,1024]{1,0:T(8,128)} fusion(bf16[1024,1536]{1,0:T(8,128)(2,1)} %bitcast.205, bf16[1,1536,1024]{2,1,0:T(8,128)(2,1)} %all-gather.6.cloned.1.call-done), kind=kOutput, calls=%fused_computation.38 | convolution fusion | flops 3221225472 | bytes 10485760 | tf_op jit(solution)/shard_map/dot_general | solution.py:471
  253.6 8.2 %fusion.21 = f32[1024,1024]{1,0:T(8,128)} fusion(bf16[1024,1536]{1,0:T(8,128)(2,1)} %bitcast.206, bf16[1,1536,1024]{2,1,0:T(8,128)(2,1)} %all-gather.4.cloned.1.call-done), kind=kOutput, calls=%fused_computation.42 | convolution fusion | flops 3221225472 | bytes 10485760 | tf_op jit(solution)/shard_map/dot_general | solution.py:471
  261.8 12.3 %multiply_convert_fusion = (bf16[1024,1024]{1,0:T(8,128)(2,1)S(1)}, bf16[1024,1024]{1,0:T(8,128)(2,1)}, bf16[1024,1024]{1,0:T(8,128)(2,1)}) fusion(f32[1024,1024]{1,0:T(8,128)} %fusion.21, f32[1024,1024]{1,0:T(8,128)} %fusion.17, bf16[1024,1536]{1,0:T(8,128)(2,1)} %bitcast.221, bf16[1,1024,1536]{2,1,0:T(8,128)(2,1)} %all-gather.8.cloned.1.call-done), kind=kOutput, calls=%fused_computation.16 | convolution fusion | flops 3236954112 | bytes 20971520 | tf_op jit(solution)/shard_map/dot_general | solution.py:475
  275.3 5.0 convolution_convert_fusion.5
  280.4 7.6 %convolution_convert_fusion.4 = bf16[1024,1536]{1,0:T(8,128)(2,1)} fusion(bf16[1024,1024]{1,0:T(8,128)(2,1)} %get-tuple-element.40, bf16[1024,1536]{1,0:T(8,128)(2,1)} %bitcast.222), kind=kOutput, calls=%fused_computation.24 | convolution fusion | flops 3222798336 | bytes 8388608 | tf_op jit(solution)/shard_map/dot_general | solution.py:479
  288.1 7.6 %convolution_convert_fusion.7 = bf16[1024,1536]{1,0:T(8,128)(2,1)} fusion(bf16[1024,1024]{1,0:T(8,128)(2,1)} %get-tuple-element.40, bf16[1,1024,1536]{2,1,0:T(8,128)(2,1)} %all-gather.8.cloned.1.call-done), kind=kOutput, calls=%fused_computation.27 | convolution fusion | flops 3222798336 | bytes 8388608 | tf_op jit(solution)/shard_map/dot_general | solution.py:471
  295.7 4.5 all-to-all-start
  301.1 6.2 %fusion.19 = f32[1024,1536]{1,0:T(8,128)S(1)} fusion(bf16[1024,1024]{1,0:T(8,128)(2,1)} %get-tuple-element.39, bf16[1,1536,1024]{2,1,0:T(8,128)(2,1)} %all-gather.4.cloned.1.call-done), kind=kOutput, calls=%fused_computation.40 | convolution fusion | flops 3221225472 | bytes 11534336 | tf_op jit(solution)/shard_map/dot_general | solution.py:475
  307.3 5.0 add_convert_fusion
  312.3 25.8 %all-to-all-done = bf16[8,128,1536]{2,1,0:T(8,128)(2,1)} async-done(((bf16[8,128,1536]{2,1,0:T(8,128)(2,1)}), bf16[8,128,1536]{2,1,0:T(8,128)(2,1)}, u32[]{:S(2)}, u32[]{:S(2)}) %all-to-all-start) | async-done | bytes 3145760 | tf_op jit(solution)/shard_map/all_to_all | solution.py:637
  338.0 4.5 all-to-all-start.1
  344.4 7.7 %convolution_convert_fusion.6 = bf16[1536,1024]{1,0:T(8,128)(2,1)} fusion(bf16[1024,1536]{1,0:T(8,128)(2,1)} %bitcast.207, bf16[1024,1024]{1,0:T(8,128)(2,1)} %get-tuple-element.39), kind=kOutput, calls=%fused_computation.26 | convolution fusion | flops 3222798336 | bytes 8388608 | tf_op jit(solution)/shard_map/dot_general | solution.py:479
  352.1 3.1 fusion.55
  355.3 4.1 fusion.26
  361.0 19.4 %all-to-all-done.1 = bf16[8,128,1536]{2,1,0:T(8,128)(2,1)} async-done(((bf16[8,128,1536]{2,1,0:T(8,128)(2,1)}), bf16[8,128,1536]{2,1,0:T(8,128)(2,1)}, u32[]{:S(2)}, u32[]{:S(2)}) %all-to-all-start.1) | async-done | bytes 3145760 | tf_op jit(solution)/shard_map/all_to_all | solution.py:644
  380.4 4.0 multiply_reduce_fusion
  387.8 4.1 fusion.4
  398.8 3.5 fusion.36
  402.9 2.6 convolution_convert_fusion.1.grad_b
  405.6 5.7 %convolution_convert_fusion.grad_a = bf16[1536,2560]{1,0:T(8,128)(2,1)} fusion(bf16[256,2560]{0,1:T(8,128)(2,1)S(1)} %bitcast.215, bf16[256,1536]{1,0:T(8,128)(2,1)S(1)} %copy-done, f32[1536]{0:T(1024)S(1)} %reshape.306, f32[256]{0:T(256)S(1)} %get-tuple-element.55), kind=kOutput, calls=%fused_computation.3 | convolution fusion | flops 2018770944 | bytes 9968640 | tf_op jit(solution)/shard_map/dot_general | solution.py:479
  411.3 88.6 %shard_map.231 = (f32[192,640]{1,0:T(8,128)S(1)}, f32[192,384]{1,0:T(8,128)S(1)}, f32[8,256]{1,0:T(8,128)S(1)}) custom-call(bf16[1536,2560]{1,0:T(8,128)(2,1)} %convolution_convert_fusion.grad_a, bf16[1536,1536]{1,0:T(8,128)(2,1)S(1)} %convolution_convert_fusion.1.grad_b, f32[8,4,8,256]{3,2,1,0:T(8,128)S(1)} %select_maximum_fusion.grad_s), custom_call_target="tpu_custom_call" | custom-call | bytes 250000000 | tf_op jit(solution)/shard_map/pallas_call | solution.py:434
  504.0 2.5 bitcast_convert_fusion.1
  506.5 2.5 bitcast_convert_fusion
  508.9 2.5 bitcast_convert_fusion.2
  (154 shorter events, 36.6 us)
Async XLA Ops:
  7.2 141.2 %copy-start = (bf16[256,1536]{1,0:T(8,128)(2,1)S(1)}, bf16[256,1536]{1,0:T(8,128)(2,1)}, u32[]{:S(2)}) copy-start(bf16[256,1536]{1,0:T(8,128)(2,1)} %param.14) | copy-start | bytes 2359300
  7.2 238.2 %all-gather.6.cloned.1.call-start = ((), (), s32[]{:S(2)}) async-start(), calls=%async_computation.6 | async-start | bytes 3932160 | tf_op jit(solution)/shard_map/all_gather | solution.py:562
  7.9 245.6 %all-gather.4.cloned.1.call-start = ((), (), s32[]{:S(2)}) async-start(), calls=%async_computation.5 | async-start | bytes 3932160 | tf_op jit(solution)/shard_map/all_gather | solution.py:561
  8.7 253.1 %all-gather.8.cloned.1.call-start = ((), (), s32[]{:S(2)}) async-start(), calls=%async_computation.7 | async-start | bytes 3932160 | tf_op jit(solution)/shard_map/all_gather | solution.py:563
  9.4 494.6 %reduce-scatter.6.cloned.1.call-start = ((), (), s32[]{:S(2)}) async-start(), calls=%async_computation.9 | async-start | bytes 3932160 | tf_op jit(solution)/shard_map/reduce_scatter | solution.py:650
  154.7 4.2 copy-start.17
  158.9 5.0 copy-start.10
  159.2 4.7 copy-start.15
  167.4 4.1 copy-start.7
  261.7 13.6 %copy-start.6 = (bf16[8,128,1536]{2,1,0:T(8,128)(2,1)S(1)}, bf16[8,128,1536]{2,1,0:T(8,128)(2,1)}, u32[]{:S(2)}) copy-start(bf16[8,128,1536]{2,1,0:T(8,128)(2,1)} %convolution_convert_fusion.3) | copy-start | bytes 9437188
  274.0 1.3 copy-start.20
  280.4 226.1 %reduce-scatter.8.cloned.1.call-start = ((), (), s32[]{:S(2)}) async-start(), calls=%async_computation.10 | async-start | bytes 3932160 | tf_op jit(solution)/shard_map/reduce_scatter | solution.py:635
  295.7 42.4 %all-to-all-start = ((bf16[8,128,1536]{2,1,0:T(8,128)(2,1)}), bf16[8,128,1536]{2,1,0:T(8,128)(2,1)}, u32[]{:S(2)}, u32[]{:S(2)}) async-start(bf16[8,128,1536]{2,1,0:T(8,128)(2,1)} %bitcast.219), calls=%async_computation | async-start | bytes 6291456 | tf_op jit(solution)/shard_map/all_to_all | solution.py:637
  301.1 6.2 %copy-start.19 = (bf16[1,1536,1024]{2,1,0:T(8,128)(2,1)S(1)}, bf16[1,1536,1024]{2,1,0:T(8,128)(2,1)}, u32[]{:S(2)}) copy-start(bf16[1,1536,1024]{2,1,0:T(8,128)(2,1)} %all-gather.6.cloned.1.call-done) | copy-start | bytes 9437188
  301.1 6.2 %copy-start.21 = (bf16[1024,1024]{1,0:T(8,128)(2,1)S(1)}, bf16[1024,1024]{1,0:T(8,128)(2,1)}, u32[]{:S(2)}) copy-start(bf16[1024,1024]{1,0:T(8,128)(2,1)} %copy-done.20) | copy-start | bytes 6291460
  338.0 42.4 %all-to-all-start.1 = ((bf16[8,128,1536]{2,1,0:T(8,128)(2,1)}), bf16[8,128,1536]{2,1,0:T(8,128)(2,1)}, u32[]{:S(2)}, u32[]{:S(2)}) async-start(bf16[8,128,1536]{2,1,0:T(8,128)(2,1)} %bitcast.218), calls=%async_computation.1 | async-start | bytes 6291456 | tf_op jit(solution)/shard_map/all_to_all | solution.py:644
  342.5 166.4 %reduce-scatter.4.cloned.1.call-start = ((), (), s32[]{:S(2)}) async-start(), calls=%async_computation.8 | async-start | bytes 3932160 | tf_op jit(solution)/shard_map/reduce_scatter | solution.py:648
  352.1 3.1 copy-start.12
  352.1 3.1 copy-start.14
  380.4 5.7 %slice-start = ((s8[4718592]{0:T(1024)(128)(4,1)}), s8[4194304]{0:T(1024)(128)(4,1)S(1)}, s32[]{:S(2)}) async-start(s8[4718592]{0:T(1024)(128)(4,1)} %bitcast.203), calls=%async_computation.11 | async-start | bytes 8388608
  380.4 5.7 %slice-start.1 = ((s8[4718592]{0:T(1024)(128)(4,1)}), s8[524288]{0:T(1024)(128)(4,1)S(1)}, s32[]{:S(2)}) async-start(s8[4718592]{0:T(1024)(128)(4,1)} %bitcast.203), calls=%async_computation.12 | async-start | bytes 1048576
  387.8 4.2 slice-start.2
  387.8 4.8 slice-start.3
  394.2 3.6 slice-start.4
  396.6 2.1 slice-start.5
  397.8 4.4 copy-start.8
  398.7 3.7 copy-start.5
  398.8 4.2 copy-start.2
  402.9 2.7 copy-start.9
  411.3 91.1 %copy-start.3 = (f32[256,1536]{1,0:T(8,128)S(1)}, f32[256,1536]{1,0:T(8,128)}, u32[]{:S(2)}) copy-start(f32[256,1536]{1,0:T(8,128)} %copy-done.1) | copy-start | bytes 4718596
  411.3 91.1 %copy-start.13 = (f32[256,1536]{1,0:T(8,128)S(1)}, f32[256,1536]{1,0:T(8,128)}, u32[]{:S(2)}) copy-start(f32[256,1536]{1,0:T(8,128)} %get-tuple-element.65) | copy-start | bytes 4718596
  411.3 91.1 %copy-start.18 = (f32[256]{0:T(256)S(1)}, f32[256]{0:T(256)}, u32[]{:S(2)}) copy-start(f32[256]{0:T(256)} %get-tuple-element.54) | copy-start | bytes 3076
  (4 other events, 4.1 us)
Sparse Core Ops, SparseCore 0:
  9.6 79.2 all-gather.5
  90.5 61.9 all-gather.3
  154.1 62.1 all-gather.7
  280.5 59.0 reduce-scatter.5
  341.8 60.2 reduce-scatter.7
  404.2 85.2 reduce-scatter.3

commit v2 on v1

--- a/solution.py
+++ b/solution.py
@@ -59,9 +59,10 @@
 X, Y, SIB = 2, 4, 1
 
 
-def plane_send(view, row, ss, rs):
+def plane_send(view, row, ss, rs, source=None):
+    source = view(row) if source is None else source
     for i, flip in enumerate((X, Y, SIB)):
-        remote(view(row), view(row), ss(i), rs(i), {"row": row_at(row, flip)}).start()
+        remote(source, view(row), ss(i), rs(i), {"row": row_at(row, flip)}).start()
 
 
 def plane_forward(view, halves, row, ss, rs):
@@ -118,147 +119,181 @@
     return at(0, block), (at(0, cut), at(cut, block - cut))
 
 
-def gather_kernel(own_a, own_b, own_s, own_c, full_a, full_b, full_s, full_c,
-                  zss, zrs, ass, ars, bss, brs, css, crs, s_zs, s_zr, s_ps, s_pr, loc):
+def through(source, middle, target, sem):
+    return pltpu.make_async_copy(source, middle, sem), pltpu.make_async_copy(middle, target, sem)
+
+
+def through(source, middle, target, sem):
+    return pltpu.make_async_copy(source, middle, sem), pltpu.make_async_copy(middle, target, sem)
+
+
+def line_kernel(own_a, own_b, own_s, own_c, line_a, line_b, full_s, full_c, mid_a, mid_b, mid_c,
+                zss, zrs, css, crs, s_zs, s_zr, s_ps, s_pr, loc):
     row, col = lax.axis_index("row"), lax.axis_index("col")
-    greet(range(1, 6), (1, 2, 3)) if False else greet(range(1, 8), (1, 2, 3))
-    block = own_a.shape[0]
     width_a, width_b = own_a.shape[1], own_b.shape[1]
     rows_c = own_c.shape[0]
-    cut = block // 2
-
-    def views(c):
-        va = pick(full_a, (c * width_a, width_a), (block, cut))
-        vb = pick(full_b, (c * width_b, width_b), (block, cut))
-        return va, vb
-
-    for i, step in enumerate((1, 2, 3)):
-        remote(own_s, full_s.at[col, row], s_zs.at[i], s_zr.at[i], {"col": (col + step) % 4}).start()
-    (view_a, _), (view_b, _) = views(col)
+    vc, hc = pick(full_c, None, (rows_c, rows_c // 2))
+    csv, crv = (lambda i: css.at[i]), (lambda i: crs.at[i])
+
+    def of_a(c):
+        return line_a.at[:, pl.ds(pl.multiple_of(c * width_a, 128), width_a)]
+
+    def of_b(c):
+        return line_b.at[:, pl.ds(pl.multiple_of(c * width_b, 128), width_b)]
+
     copies = [
-        pltpu.make_async_copy(own_a, view_a(row), loc.at[0]),
-        pltpu.make_async_copy(own_b, view_b(row), loc.at[1]),
-        pltpu.make_async_copy(own_s, full_s.at[col, row], loc.at[2]),
-        pltpu.make_async_copy(own_c, full_c.at[pl.ds(row * rows_c, rows_c), :], loc.at[3]),
+        through(own_a, mid_a, of_a(col), loc.at[0]),
+        through(own_b, mid_b, of_b(col), loc.at[1]),
+        through(own_c, mid_c, vc(row), loc.at[2]),
     ]
-    for copy in copies:
+    for copy, _ in copies:
         copy.start()
+    small_copy = pltpu.make_async_copy(own_s, full_s.at[col, row], loc.at[3])
+    small_copy.start()
+    greet(range(1, 8), (1, 2, 3))
 
     def along(c, source_a, source_b, right, left):
-        (va, _), (vb, _) = views(c)
         for d, (cond, step) in enumerate(((right, 1), (left, 3))):
             @pl.when(cond)
             def _():
                 there = {"col": (col + step) % 4}
-                remote(source_a, va(row), zss.at[0, c, d], zrs.at[0, c], there).start()
-                remote(source_b, vb(row), zss.at[1, c, d], zrs.at[1, c], there).start()
+                remote(source_a, of_a(c), zss.at[0, c, d], zrs.at[0, c], there).start()
+                remote(source_b, of_b(c), zss.at[1, c, d], zrs.at[1, c], there).start()
+
+    def arrived(k):
+        c = unit_order(col, k)
+        there = {"col": (col + 1) % 4}
+        remote(of_a(c), of_a(c), zss.at[0, c, 0], zrs.at[0, c], there).wait_recv()
+        remote(of_b(c), of_b(c), zss.at[1, c, 0], zrs.at[1, c], there).wait_recv()
+        along(c, of_a(c), of_b(c), (c < col) & (col < 3), (c > col) & (col > 0))
 
     along(col, own_a, own_b, col < 3, col > 0)
-    for copy in copies:
-        copy.wait()
-    for k in range(4):
-        c = unit_order(col, k)
-        (va, ha), (vb, hb) = views(c)
-        if k > 0:
-            remote(va(row), va(row), zss.at[0, c, 0], zrs.at[0, c], {"col": (col + 1) % 4}).wait_recv()
-            remote(vb(row), vb(row), zss.at[1, c, 0], zrs.at[1, c], {"col": (col + 1) % 4}).wait_recv()
-            along(c, va(row), vb(row), (c < col) & (col < 3), (c > col) & (col > 0))
-        plane_send(va, row, lambda i: ass.at[c, i], lambda i: ars.at[c, i])
-        plane_send(vb, row, lambda i: bss.at[c, i], lambda i: brs.at[c, i])
-        if k > 0:
-            p = unit_order(col, k - 1)
-            (va, ha), (vb, hb) = views(p)
-            plane_forward(va, ha, row, lambda i: ass.at[p, i], lambda i: ars.at[p, i])
-            plane_forward(vb, hb, row, lambda i: bss.at[p, i], lambda i: brs.at[p, i])
-        if k > 1:
-            q = unit_order(col, k - 2)
-            (va, ha), (vb, hb) = views(q)
-            plane_last(va, ha, row, lambda i: ass.at[q, i], lambda i: ars.at[q, i])
-            plane_last(vb, hb, row, lambda i: bss.at[q, i], lambda i: brs.at[q, i])
-        if k == 0:
-            for i, step in enumerate((3, 2, 1)):
-                remote(own_s, full_s.at[(col + step) % 4, row], s_zs.at[i], s_zr.at[i], {"col": (col + 1) % 4}).wait()
-            for i in range(1, 8):
-                remote(full_s.at[:, row], full_s.at[:, row], s_ps.at[i - 1], s_pr.at[i - 1], {"row": row_at(row, i)}).start()
-    vc, hc = pick(full_c, None, (rows_c, rows_c // 2))
-    csv, crv = (lambda i: css.at[i]), (lambda i: crs.at[i])
-    plane_send(vc, row, csv, crv)
-    for k in (3,):
-        p = unit_order(col, k)
-        (va, ha), (vb, hb) = views(p)
-        plane_forward(va, ha, row, lambda i: ass.at[p, i], lambda i: ars.at[p, i])
-        plane_forward(vb, hb, row, lambda i: bss.at[p, i], lambda i: brs.at[p, i])
-    for k in (2, 3):
-        p = unit_order(col, k)
-        (va, ha), (vb, hb) = views(p)
-        plane_last(va, ha, row, lambda i: ass.at[p, i], lambda i: ars.at[p, i])
-        plane_last(vb, hb, row, lambda i: bss.at[p, i], lambda i: brs.at[p, i])
+    for i, step in enumerate((1, 2, 3)):
+        remote(own_s, full_s.at[col, row], s_zs.at[i], s_zr.at[i], {"col": (col + step) % 4}).start()
+    plane_send(vc, row, csv, crv, own_c)
+    for first, second in copies:
+        first.wait()
+        second.start()
+    small_copy.wait()
+    arrived(1)
+    for i, step in enumerate((3, 2, 1)):
+        remote(own_s, full_s.at[(col + step) % 4, row], s_zs.at[i], s_zr.at[i], {"col": (col + 1) % 4}).wait()
+    for i in range(1, 8):
+        remote(full_s.at[:, row], full_s.at[:, row], s_ps.at[i - 1], s_pr.at[i - 1], {"row": row_at(row, i)}).start()
+    arrived(2)
     plane_forward(vc, hc, row, csv, crv)
+    arrived(3)
     plane_last(vc, hc, row, csv, crv)
-    for c in range(4):
-        (va, ha), (vb, hb) = views(c)
-        plane_finish(va, ha, row, lambda i: ass.at[c, i], lambda i: ars.at[c, i])
-        plane_finish(vb, hb, row, lambda i: bss.at[c, i], lambda i: brs.at[c, i])
+    for _, second in copies:
+        second.wait()
     plane_finish(vc, hc, row, csv, crv)
     for i in range(1, 8):
         there = row_at(row, i)
         remote(full_s.at[:, there], full_s.at[:, there], s_ps.at[i - 1], s_pr.at[i - 1], {"row": there}).wait()
     for k in range(4):
         c = unit_order(col, k)
-        (va, ha), (vb, hb) = views(c)
         right = (c <= col) & (col < 3)
         left = (c >= col) & (col > 0)
         for d, cond in enumerate((right, left)):
             @pl.when(cond)
             def _():
                 there = {"col": (col + 1) % 4}
-                remote(va(row), va(row), zss.at[0, c, d], zrs.at[0, c], there).wait_send()
-                remote(vb(row), vb(row), zss.at[1, c, d], zrs.at[1, c], there).wait_send()
-
-
-def gather_attention(own_a, own_b, own_s, own_c):
+                remote(of_a(c), of_a(c), zss.at[0, c, d], zrs.at[0, c], there).wait_send()
+                remote(of_b(c), of_b(c), zss.at[1, c, d], zrs.at[1, c], there).wait_send()
+
+
+def gather_line(own_a, own_b, own_s, own_c):
     sems = pltpu.SemaphoreType.DMA
-    block, rows_c = own_a.shape[0], own_c.shape[0]
+    rows_c = own_c.shape[0]
     return pl.pallas_call(
-        gather_kernel,
+        line_kernel,
         out_shape=(
-            jax.ShapeDtypeStruct((block * 8, own_a.shape[1] * 4), own_a.dtype),
-            jax.ShapeDtypeStruct((block * 8, own_b.shape[1] * 4), own_b.dtype),
+            jax.ShapeDtypeStruct((own_a.shape[0], own_a.shape[1] * 4), own_a.dtype),
+            jax.ShapeDtypeStruct((own_b.shape[0], own_b.shape[1] * 4), own_b.dtype),
             jax.ShapeDtypeStruct((4, 8) + own_s.shape, own_s.dtype),
             jax.ShapeDtypeStruct((8 * rows_c, own_c.shape[1]), own_c.dtype),
         ),
         in_specs=[ANY] * 4,
         out_specs=(ANY,) * 4,
         scratch_shapes=[
+            pltpu.VMEM(own_a.shape, own_a.dtype),
+            pltpu.VMEM(own_b.shape, own_b.dtype),
+            pltpu.VMEM(own_c.shape, own_c.dtype),
             sems((2, 4, 2)), sems((2, 4)),
-            sems((4, 9)), sems((4, 9)), sems((4, 9)), sems((4, 9)),
             sems((9,)), sems((9,)),
             sems((3,)), sems((3,)), sems((7,)), sems((7,)), sems((4,)),
         ],
         compiler_params=pltpu.CompilerParams(collective_id=0, has_side_effects=True),
-        cost_estimate=pl.CostEstimate(flops=0, bytes_accessed=200_000_000, transcendentals=0),
+        cost_estimate=pl.CostEstimate(flops=0, bytes_accessed=1_000_000, transcendentals=0),
     )(own_a, own_b, own_s, own_c)
 
 
-def spread_kernel(own_c, own_g, full_c, full_g, css, crs, gss, grs, loc):
+def plane_kernel(count, *refs):
     row = lax.axis_index("row")
+    owns, fulls, mids = refs[:count], refs[count : 2 * count], refs[2 * count : 3 * count]
+    ss, rs, loc = refs[3 * count :]
+    views, copies = [], []
+    for i in range(count):
+        block = owns[i].shape[0]
+        views.append(pick(fulls[i], None, (block, block // 2)))
+        copies.append(through(owns[i], mids[i], views[i][0](row), loc.at[i]))
+        copies[i][0].start()
     greet(range(1, 8), ())
+
+    def sems_of(i):
+        return (lambda j: ss.at[i, j]), (lambda j: rs.at[i, j])
+
+    for i in range(count):
+        plane_send(views[i][0], row, *sems_of(i), owns[i])
+    for first, second in copies:
+        first.wait()
+        second.start()
+    for i in range(count):
+        plane_forward(*views[i], row, *sems_of(i))
+    for i in range(count):
+        plane_last(*views[i], row, *sems_of(i))
+    for _, second in copies:
+        second.wait()
+    for i in range(count):
+        plane_finish(*views[i], row, *sems_of(i))
+
+
+def gather_plane(collective, owns):
+    sems = pltpu.SemaphoreType.DMA
+    count = len(owns)
+    return pl.pallas_call(
+        functools.partial(plane_kernel, count),
+        out_shape=tuple(
+            jax.ShapeDtypeStruct((8 * own.shape[0], own.shape[1]), own.dtype) for own in owns
+        ),
+        in_specs=[ANY] * count,
+        out_specs=(ANY,) * count,
+        scratch_shapes=[pltpu.VMEM(own.shape, own.dtype) for own in owns]
+        + [sems((count, 9)), sems((count, 9)), sems((count,))],
+        compiler_params=pltpu.CompilerParams(collective_id=collective, has_side_effects=True),
+        cost_estimate=pl.CostEstimate(flops=0, bytes_accessed=1_000_000, transcendentals=0),
+    )(*owns)
+
+
+def spread_kernel(own_c, own_g, full_c, full_g, mid_c, css, crs, gss, grs, loc):
+    row = lax.axis_index("row")
     rows_c = own_c.shape[0]
-    copies = [
-        pltpu.make_async_copy(own_c, full_c.at[pl.ds(row * rows_c, rows_c), :], loc.at[0]),
-        pltpu.make_async_copy(own_g, full_g.at[row], loc.at[1]),
-    ]
-    for copy in copies:
-        copy.start()
+    vc, hc = pick(full_c, None, (rows_c, rows_c // 2))
+    csv, crv = (lambda i: css.at[i]), (lambda i: crs.at[i])
+    first, second = through(own_c, mid_c, vc(row), loc.at[0])
+    first.start()
+    own_copy = pltpu.make_async_copy(own_g, full_g.at[row], loc.at[1])
+    own_copy.start()
+    greet(range(1, 8), ())
+    plane_send(vc, row, csv, crv, own_c)
     for i in range(1, 8):
         remote(own_g, full_g.at[row], gss.at[i - 1], grs.at[i - 1], {"row": row_at(row, i)}).start()
-    for copy in copies:
-        copy.wait()
-    vc, hc = pick(full_c, None, (rows_c, rows_c // 2))
-    csv, crv = (lambda i: css.at[i]), (lambda i: crs.at[i])
-    plane_send(vc, row, csv, crv)
+    first.wait()
+    second.start()
     plane_forward(vc, hc, row, csv, crv)
     plane_last(vc, hc, row, csv, crv)
+    second.wait()
+    own_copy.wait()
     plane_finish(vc, hc, row, csv, crv)
     for i in range(1, 8):
         there = row_at(row, i)
@@ -275,9 +310,12 @@
         ),
         in_specs=[ANY] * 2,
         out_specs=(ANY,) * 2,
-        scratch_shapes=[sems((9,)), sems((9,)), sems((7,)), sems((7,)), sems((2,))],
+        scratch_shapes=[
+            pltpu.VMEM(own_c.shape, own_c.dtype),
+            sems((9,)), sems((9,)), sems((7,)), sems((7,)), sems((2,)),
+        ],
         compiler_params=pltpu.CompilerParams(collective_id=1, has_side_effects=True),
-        cost_estimate=pl.CostEstimate(flops=0, bytes_accessed=100_000_000, transcendentals=0),
+        cost_estimate=pl.CostEstimate(flops=0, bytes_accessed=1_000_000, transcendentals=0),
     )(own_c, own_g)
 
 
@@ -310,7 +348,8 @@
     for i in range(1, 8):
         there = row_at(row, i)
         remote(grad_s.at[there], s_rec.at[i - 1], s_ss.at[i - 1], s_rs.at[i - 1], {"row": there}).start()
-    def start_first(c, carry):
+    def start_first(k, carry):
+        c = (col + 1 + k) % 4
         for q in range(4):
             pa, pb = parts(c, q, 1 - core)
             remote(pa, rec_sib.at[c, q, :, pl.ds(0, width_a)], ss1.at[c, q, 0], rs1.at[c, q, 0], sib).start()
@@ -359,22 +398,25 @@
         there = (col + step) % 4
         return remote(own.at[there, chip], rec_z.at[step - 1], zss.at[step - 1], zrs.at[step - 1], {"col": there})
 
+    def nth(k):
+        return (col + 1 + k) % 4
+
     def stages(k, carry):
         @pl.when(k < 4)
         def _():
-            chip_sum(k)
-            for copy in one(k):
+            chip_sum(nth(k))
+            for copy in one(nth(k)):
                 copy.start()
         @pl.when((k >= 1) & (k < 5))
         def _():
-            one_sum(k - 1)
-            for copy in two(k - 1):
+            one_sum(nth(k - 1))
+            for copy in two(nth(k - 1)):
                 copy.start()
         @pl.when(k >= 2)
         def _():
-            two_sum(k - 2)
+            two_sum(nth(k - 2))
         for step in (1, 2, 3):
-            @pl.when((k >= 2) & ((col + step) % 4 == k - 2))
+            @pl.when(k == step + 1)
             def _():
                 column(step).start()
         return carry
@@ -459,7 +501,7 @@
         compiler_params=pltpu.CompilerParams(
             collective_id=2, has_side_effects=True, vmem_limit_bytes=48 * 2**20
         ),
-        cost_estimate=pl.CostEstimate(flops=0, bytes_accessed=250_000_000, transcendentals=0),
+        cost_estimate=pl.CostEstimate(flops=0, bytes_accessed=1_000_000, transcendentals=0),
     )(grad_a, grad_b, grad_s)
 
 
@@ -484,8 +526,6 @@
 
 
 def gather_all(own_a, own_b, own_s, own_c):
-    if on_small_slice():
-        return gather_attention(own_a, own_b, own_s, own_c)
     col_a = lax.all_gather(own_a, "col", axis=1, tiled=True)
     col_b = lax.all_gather(own_b, "col", axis=1, tiled=True)
     small = lax.all_gather(lax.all_gather(own_s, "col", axis=0), "row", axis=1)
@@ -558,9 +598,9 @@
     piece = attn_gain.shape[0]
     router_cols = router.shape[1]
 
-    full_gate = lax.all_gather(w_gate, "col", axis=1, tiled=True)[0]
-    full_up = lax.all_gather(w_up, "col", axis=1, tiled=True)[0]
-    full_down = lax.all_gather(w_down, "col", axis=1, tiled=True)[0]
+    hidden_units = w_gate.shape[2]
+    own_gu = jnp.concatenate([w_gate[0], w_up[0]], axis=1)
+    own_down = w_down[0]
 
     lane = 256
 
@@ -572,7 +612,16 @@
     )
     own_s = jnp.pad(own_s, ((0, 16 - own_s.shape[0]), (0, 0)))
     own_a = jnp.concatenate([w_query, w_key, w_value], axis=1)
-    full_a, full_out, small, plane_upstream = gather_all(own_a, w_out, own_s, cotangent)
+    if on_small_slice():
+        line_a, line_out, small, plane_upstream = gather_line(own_a, w_out, own_s, cotangent)
+        own_gu, own_down, line_a, line_out = lax.optimization_barrier(
+            (own_gu, own_down, line_a, line_out)
+        )
+        full_a, full_out = gather_plane(3, (line_a, line_out))
+    else:
+        full_a, full_out, small, plane_upstream = gather_all(own_a, w_out, own_s, cotangent)
+    full_gu = lax.all_gather(own_gu, "col", axis=0, tiled=True)
+    full_down = lax.all_gather(own_down, "col", axis=0, tiled=True)
     full_router = small[:, :, :router_cols, :block].transpose(1, 3, 0, 2).reshape(model, experts)
     gain_one = small[:, :, router_cols, :piece].transpose(1, 0, 2).reshape(model).astype(jnp.float32)
     gain_two = small[:, :, router_cols + 1, :piece].transpose(1, 0, 2).reshape(model).astype(jnp.float32)
@@ -621,33 +670,46 @@
     grouped = jnp.einsum(
         "rct,rtd->rcd", chosen_rows, plane_normed, preferred_element_type=jnp.float32
     ).astype(jnp.bfloat16).reshape(rows * capacity, model)
-    weighted = (plane_upstream.astype(jnp.float32) * mine[:, :, None]).astype(jnp.bfloat16)
-    grouped_grad = jnp.einsum(
-        "rct,rtd->rcd", chosen_rows, weighted, preferred_element_type=jnp.float32
-    ).astype(jnp.bfloat16).reshape(rows * capacity, model)
-
-    gate_pre = dot(grouped, full_gate)
-    up_pre = dot(grouped, full_up)
+    slot_gate = jnp.sum(
+        jnp.where(chosen_rows > 0, mine[:, None, :], 0.0), axis=2
+    ).reshape(rows * capacity, 1)
+    grouped_up = jnp.einsum(
+        "rct,rtd->rcd", chosen_rows, plane_upstream, preferred_element_type=jnp.float32
+    ).reshape(rows * capacity, model)
+    grouped_grad = (grouped_up * slot_gate).astype(jnp.bfloat16)
+
+    both_pre = dot(grouped, full_gu)
+    gate_pre, up_pre = both_pre[:, :hidden_units], both_pre[:, hidden_units:]
     sigma = jax.nn.sigmoid(gate_pre)
     silu_gate = gate_pre * sigma
     activation = (silu_gate * up_pre).astype(jnp.bfloat16)
     grad_down_local = t_dot(activation, grouped_grad).astype(jnp.bfloat16)
     grad_down = lax.psum_scatter(grad_down_local, "col", scatter_dimension=0, tiled=True)
-    produced = dot(activation, full_down).astype(jnp.bfloat16)
+    later_grad, _ = lax.optimization_barrier((grouped_grad, grad_down_local))
+    act_grad = dot_t(later_grad, full_down)
+    both_grad = jnp.concatenate(
+        [
+            (act_grad * up_pre * sigma * (1.0 + gate_pre * (1.0 - sigma))).astype(jnp.bfloat16),
+            (act_grad * silu_gate).astype(jnp.bfloat16),
+        ],
+        axis=1,
+    )
+    in_grad = dot_t(both_grad, full_gu).astype(jnp.bfloat16)
+    back_grad = lax.all_to_all(
+        in_grad.reshape(rows, capacity, model), "row", split_axis=0, concat_axis=0, tiled=True
+    ).reshape(experts * capacity, model)
+    later_act, _ = lax.optimization_barrier((activation, in_grad))
+    produced = dot(later_act, full_down).astype(jnp.bfloat16)
+    slot_gate_grad = jnp.sum(produced.astype(jnp.float32) * grouped_up, axis=1)
+    back_gate_grad = lax.all_to_all(
+        slot_gate_grad.reshape(rows, 1, capacity), "row", split_axis=0, concat_axis=0, tiled=True
+    ).reshape(experts * capacity)
+    grad_gu_local = t_dot(grouped, both_grad).astype(jnp.bfloat16)
+    grad_gu = lax.psum_scatter(grad_gu_local, "col", scatter_dimension=0, tiled=True)
+    produced, back_grad = lax.optimization_barrier((produced, back_grad))
     back_rows = lax.all_to_all(
         produced.reshape(rows, capacity, model), "row", split_axis=0, concat_axis=0, tiled=True
     ).reshape(experts * capacity, model)
-    act_grad = dot_t(grouped_grad, full_down)
-    up_grad = (act_grad * silu_gate).astype(jnp.bfloat16)
-    pre_grad = (act_grad * up_pre * sigma * (1.0 + gate_pre * (1.0 - sigma))).astype(jnp.bfloat16)
-    in_grad = (dot_t(pre_grad, full_gate) + dot_t(up_grad, full_up)).astype(jnp.bfloat16)
-    back_grad = lax.all_to_all(
-        in_grad.reshape(rows, capacity, model), "row", split_axis=0, concat_axis=0, tiled=True
-    ).reshape(experts * capacity, model)
-    grad_gate_local = t_dot(grouped, pre_grad).astype(jnp.bfloat16)
-    grad_gate = lax.psum_scatter(grad_gate_local, "col", scatter_dimension=0, tiled=True)
-    grad_up_local = t_dot(grouped, up_grad).astype(jnp.bfloat16)
-    grad_up = lax.psum_scatter(grad_up_local, "col", scatter_dimension=0, tiled=True)
 
     any_named = jnp.any(named, axis=1)
     before = jnp.cumsum(any_named.astype(jnp.int32), axis=0) - 1
@@ -656,13 +718,14 @@
         axis=2,
     )
     all_slots = jnp.arange(experts * capacity, dtype=jnp.int32)
-    from_slot = (slot_of.T[:, :, None] == all_slots[None, None, :]).astype(jnp.bfloat16)
+    is_slot = slot_of.T[:, :, None] == all_slots[None, None, :]
+    from_slot = is_slot.astype(jnp.bfloat16)
+    gate_grad = jnp.sum(jnp.where(is_slot, back_gate_grad[None, None, :], 0.0), axis=2).T
     returned = [dot(from_slot[k], back_rows) for k in range(TOP)]
     upstream = cotangent.astype(jnp.float32)
     output = (
         hidden + sum(returned[k] * gate_probs[:, k : k + 1] for k in range(TOP))
     ).astype(jnp.bfloat16)
-    gate_grad = jnp.stack([jnp.sum(returned[k] * upstream, axis=1) for k in range(TOP)], axis=1)
     normed_two_grad = dot(from_slot[0] + from_slot[1], back_grad)
     pair_mean = jnp.sum(gate_probs * gate_grad, axis=1, keepdims=True)
     pair_logit = gate_probs * (gate_grad - pair_mean)
@@ -729,6 +792,10 @@
         ],
         axis=2,
     )
+    grad_down = grad_down.astype(jnp.float32)[None]
+    grad_a_full, d_tokens, output, grad_down = lax.optimization_barrier(
+        (grad_a_full, d_tokens, output, grad_down)
+    )
     sum_a, sum_out, sum_s = reduce_all(grad_a_full, grad_out_full, grad_s)
     return (
         output,
@@ -740,9 +807,9 @@
         sum_out,
         sum_s[router_cols + 1, :piece],
         sum_s[:router_cols, :block].T,
-        grad_gate.astype(jnp.float32)[None],
-        grad_up.astype(jnp.float32)[None],
-        grad_down.astype(jnp.float32)[None],
+        grad_gu[:, :hidden_units].astype(jnp.float32)[None],
+        grad_gu[:, hidden_units:].astype(jnp.float32)[None],
+        grad_down,
     )
 
 

time: 530 us -> 460 us (0.87); the launches traced: 519 us -> 456 us
  Pallas kernels: 282 us -> 200 us
  matrix products: 131 us -> 119 us
  waiting for transfers between devices: 47.3 us -> 56.8 us
  blocking collectives: 0 us -> 8.1 us
  local copies, waits for them, and re-layouts: 14 us -> 20.9 us
  other arithmetic: 20.8 us -> 26.9 us
    pallas_call x1 -> x2, Pallas kernels: 135 us -> 95.7 us  [the longest x1 56.4 us: gather_plane(): pl.pallas_call(functools.partial(plane_kernel, count), out_shape=tuple((j...]
    all_gather x3 -> x2, waiting for transfers between devices: 0.01 us -> 28.7 us  [the longest x1 28.7 us: per_device(): full_down = lax.all_gather(own_down, 'col', axis=0, tiled=True)]
    pallas_call x1, Pallas kernels: 58.6 us -> 33.4 us  [spread_tokens(): pl.pallas_call(spread_kernel, out_shape=(jax.ShapeDtypeStruct((8 * own_c....]
    all_to_all x1, waiting for transfers between devices: 25.8 us -> 6.25 us  [per_device(): lax.all_to_all(produced.reshape(rows, capacity, model), 'row', split_axis...]
    pallas_call x1, Pallas kernels: 88.6 us -> 71.2 us  [reduce_attention(): pl.pallas_call(reduce_kernel, out_shape=(jax.ShapeDtypeStruct((block, wid...]
    all_to_all x0 -> x1, blocking collectives: none -> 8.1 us  [per_device(): lax.all_to_all(slot_gate_grad.reshape(rows, 1, capacity), 'row', split_ax...]
    dot_general x9 -> x8, matrix products: 45.1 us -> 37.5 us  [dot(): return jnp.dot(a, b, preferred_element_type=jnp.float32)]
    unnamed x59 -> x81, local copies, waits for them, and re-layouts: 5.26 us -> 10.8 us
  transfers between devices with their start and end apart: 8 -> 6, of which waited for: 2 -> 3; matrix products, arithmetic and copies ran while one was open for 27% -> 32% of each run, Pallas kernels for 54% -> 35%
where the time goes in v2:
time: 460 us; the launch traced here: 456 us
  Pallas kernels  200 us (43%)
  matrix products  119 us (26%)
  waiting for transfers between devices  56.8 us (12%)
  other arithmetic  26.9 us (6%)
  local copies, waits for them, and re-layouts  20.9 us (5%)
  between operations  14.7 us (3%)
  starting transfers between devices  9.25 us (2%)
  blocking collectives  8.1 us (2%)
    pallas_call x1, Pallas kernels, reduce_attention(): pl.pallas_call(reduce_kernel, out_shape=(jax.ShapeDtypeStruct((block, wid...  71.2 us
    pallas_call x1, Pallas kernels, gather_plane(): pl.pallas_call(functools.partial(plane_kernel, count), out_shape=tuple((j...  56.4 us
    pallas_call x1, Pallas kernels, gather_line(): pl.pallas_call(line_kernel, out_shape=(jax.ShapeDtypeStruct((own_a.shape[...  39.3 us
    dot_general x8, matrix products, dot(): return jnp.dot(a, b, preferred_element_type=jnp.float32)  37.5 us
    pallas_call x1, Pallas kernels, spread_tokens(): pl.pallas_call(spread_kernel, out_shape=(jax.ShapeDtypeStruct((8 * own_c....  33.4 us
    dot_general x5, matrix products, dot_t(): lax.dot_general(a, b, (((1,), (1,)), ((), ())), preferred_element_type=jn...  28.8 us
    all_gather x1, waiting for transfers between devices, per_device(): full_down = lax.all_gather(own_down, 'col', axis=0, tiled=True)  28.7 us
    dot_general x5, matrix products, t_dot(): lax.dot_general(a, b, (((0,), (0,)), ((), ())), preferred_element_type=jn...  28 us
  transfers between devices with their start and end apart: 6, of which 3 were waited for; matrix products, arithmetic and copies ran while one was open for 32% of the time, Pallas kernels for 35%

profile of v2, /device:TPU:0, one launch (start us, length us, event | category | flops | bytes accessed | tf_op | source)
XLA Modules:
  0.0 455.9 jit_solution(9181220511370811149)
XLA Ops:
  8.6 2.7 pad_maximum_fusion.3
  12.1 39.3 %shard_map.229 = (bf16[192,2560]{1,0:T(8,128)(2,1)}, bf16[192,1536]{1,0:T(8,128)(2,1)}, bf16[4,8,16,256]{3,2,1,0:T(8,128)(2,1)}, bf16[2048,1536]{1,0:T(8,128)(2,1)}) custom-call(bf16[192,640]{1,0:T(8,128)(2,1)} %pad_maximum_fusion.5.own_a, bf16[192,384]{1,0:T(8,128)(2,1)} %own_b.1, bf16[16,256]{1,0:T(8,128)(2,1)} %pad.26.own_s, bf16[256,1536]{1,0:T(8,128)(2,1)} %own_c.1), custom_call_target="tpu_custom_call" | custom-call | bytes 1000000 | tf_op jit(solution)/shard_map/pallas_call | solution.py:208
  53.5 56.4 %shard_map.230 = (bf16[1536,2560]{1,0:T(8,128)(2,1)}, bf16[1536,1536]{1,0:T(8,128)(2,1)}) custom-call(bf16[192,2560]{1,0:T(8,128)(2,1)} %get-tuple-element.38.refs_0_, bf16[192,1536]{1,0:T(8,128)(2,1)} %get-tuple-element.39.refs_1_), custom_call_target="tpu_custom_call" | custom-call | bytes 1000000 | tf_op jit(solution)/shard_map/pallas_call | solution.py:264
  109.9 5.5 %convolution_convert_fusion.3 = bf16[256,2560]{1,0:T(8,128)(2,1)S(1)} fusion(bf16[1536,2560]{1,0:T(8,128)(2,1)} %get-tuple-element.40, bf16[256,1536]{1,0:T(8,128)(2,1)S(1)} %copy-done.2, f32[1536]{0:T(1024)S(1)} %reshape.253, f32[256]{0:T(256)S(1)} %get-tuple-element.81), kind=kOutput, calls=%fused_computation.22 | convolution fusion | flops 2015494144 | bytes 9968640 | tf_op jit(solution)/shard_map/dot_general | solution.py:513
  120.2 4.7 %fusion.83 = (f32[8,3,256]{2,1,0:T(4,128)S(1)}, f32[8,3,256,256]{2,3,1,0:T(8,128)}) fusion(pred[256,256]{0,1:T(8,128)(4,1)S(1)} %fusion.56, bf16[256,8,64,1]{0,2,3,1:T(8,128)(2,1)S(1)} %bitcast.222, bf16[256,8,3,64]{0,3,2,1:T(8,128)(2,1)S(1)} %bitcast.216), kind=kOutput, calls=%fused_computation.162 | convolution fusion | flops 207618304 | bytes 7430144 | tf_op jit(solution)/shard_map/sub | solution.py:641
  125.0 3.5 fusion.26
  128.5 4.1 multiply_reduce_fusion.2
  134.1 33.4 %shard_map.231 = (bf16[2048,1536]{1,0:T(8,128)(2,1)}, f32[8,8,256]{2,1,0:T(8,128)}) custom-call(bf16[256,1536]{1,0:T(8,128)(2,1)} %copy-done.5, f32[8,256]{1,0:T(8,128)} %select_bitcast_fusion.own_g), custom_call_target="tpu_custom_call" | custom-call | bytes 1000000 | tf_op jit(solution)/shard_map/pallas_call | solution.py:305
  169.7 4.2 fusion.40
  175.2 2.6 convolution_convert_fusion.5
  179.9 9.7 %fusion.85 = f32[1024,2048]{1,0:T(8,128)S(1)} fusion(bf16[1024,1536]{1,0:T(8,128)(2,1)} %bitcast.208, bf16[1536,2048]{1,0:T(8,128)(2,1)} %all-gather.3.cloned.1.call-done), kind=kOutput, calls=%fused_computation.164 | convolution fusion | flops 6442450944 | bytes 17825792 | tf_op jit(solution)/shard_map/dot_general | solution.py:513
  194.9 5.3 %convolution_convert_fusion.7 = bf16[1024,1536]{1,0:T(8,128)(2,1)} fusion(bf16[1024,1024]{1,0:T(8,128)(2,1)S(1)} %multiply_convert_fusion.2, bf16[1024,1536]{1,0:T(8,128)(2,1)S(1)} %copy-done.14), kind=kOutput, calls=%fused_computation.26 | convolution fusion | flops 3222798336 | bytes 8388608 | tf_op jit(solution)/shard_map/dot_general | solution.py:521
  200.2 28.7 %all-gather.5.cloned.1.call-done = bf16[1024,1536]{1,0:T(8,128)(2,1)} async-done(((bf16[256,1536]{1,0:T(8,128)(2,1)}), bf16[1024,1536]{1,0:T(8,128)(2,1)}) %all-gather.5.cloned.1.call-update) | async-done | bytes 3145744 | tf_op jit(solution)/shard_map/all_gather | solution.py:624
  228.9 9.9 %multiply_convert_fusion.1 = (bf16[1024,1024]{1,0:T(8,128)(2,1)S(1)}, bf16[1024,1024]{1,0:T(8,128)(2,1)S(1)}) fusion(f32[1024,2048]{1,0:T(8,128)} %copy-done.9, bf16[1024,1536]{1,0:T(8,128)(2,1)} %fusion.4, bf16[1024,1536]{1,0:T(8,128)(2,1)} %all-gather.5.cloned.1.call-done), kind=kOutput, calls=%fused_computation.18 | convolution fusion | flops 3234856960 | bytes 18874368 | tf_op jit(solution)/shard_map/dot_general | solution.py:517
  238.9 11.5 %convolution_convert_fusion.4 = bf16[1024,1536]{1,0:T(8,128)(2,1)} fusion(bf16[1536,2048]{1,0:T(8,128)(2,1)} %all-gather.3.cloned.1.call-done, bf16[1024,1024]{1,0:T(8,128)(2,1)S(1)} %get-tuple-element.65, bf16[1024,1024]{1,0:T(8,128)(2,1)S(1)} %get-tuple-element.64), kind=kOutput, calls=%fused_computation.23 | convolution fusion | flops 6452412416 | bytes 13631488 | tf_op jit(solution)/shard_map/dot_general | solution.py:517
  250.5 6.7 %fusion.5 = (f32[1024]{0:T(1024)S(1)}, bf16[1024,1536]{1,0:T(8,128)(2,1)}) fusion(f32[8,128,1536]{2,1,0:T(8,128)} %copy-done.1, bf16[1024,1024]{1,0:T(8,128)(2,1)S(1)} %copy-done.17, bf16[1024,1536]{1,0:T(8,128)(2,1)S(1)} %copy-done.28), kind=kOutput, calls=%fused_computation.12 | convolution fusion | flops 3227515904 | bytes 14684160 | tf_op jit(solution)/shard_map/dot_general | solution.py:513
  257.2 8.1 %all_to_all.15 = f32[8,1,128]{2,1,0:T(1,128)S(1)} all-to-all(f32[8,1,128]{2,1,0:T(1,128)S(1)} %bitcast.246), channel_id=1, replica_groups=mesh['row'=8,'col'=4] {'row'}, dimensions={0} | all-to-all | bytes 8192 | tf_op jit(solution)/shard_map/all_to_all | solution.py:704
  265.3 4.5 all-to-all-start
  269.8 11.8 %convolution_convert_fusion.1 = bf16[1536,2048]{1,0:T(8,128)(2,1)} fusion(bf16[1024,1536]{1,0:T(8,128)(2,1)} %bitcast.209, bf16[1024,1024]{1,0:T(8,128)(2,1)} %copy-done.30, bf16[1024,1024]{1,0:T(8,128)(2,1)} %copy-done.29), kind=kOutput, calls=%fused_computation.2 | convolution fusion | flops 6453985280 | bytes 13631488 | tf_op jit(solution)/shard_map/dot_general | solution.py:521
  286.5 21.1 %all-to-all-done = bf16[8,128,1536]{2,1,0:T(8,128)(2,1)} async-done(((bf16[8,128,1536]{2,1,0:T(8,128)(2,1)}), bf16[8,128,1536]{2,1,0:T(8,128)(2,1)}, u32[]{:S(2)}, u32[]{:S(2)}) %all-to-all-start) | async-done | bytes 3145760 | tf_op jit(solution)/shard_map/all_to_all | solution.py:698
  307.6 4.0 multiply_reduce_fusion
  317.0 4.6 %all-to-all-start.2 = ((bf16[8,128,1536]{2,1,0:T(8,128)(2,1)}), bf16[8,128,1536]{2,1,0:T(8,128)(2,1)}, u32[]{:S(2)}, u32[]{:S(2)}) async-start(bf16[8,128,1536]{2,1,0:T(8,128)(2,1)} %bitcast.218), calls=%async_computation.2 | async-start | bytes 6291456 | tf_op jit(solution)/shard_map/all_to_all | solution.py:710
  321.6 6.7 %fusion.1 = (f32[8,3,256]{2,1,0:T(4,128)S(1)}, f32[8,256,256,3]{2,1,3,0:T(8,128)}) fusion(f32[8,3,256,256]{2,3,1,0:T(8,128)} %get-tuple-element.85, f32[8,3,256]{2,1,0:T(4,128)S(1)} %copy-done.26, bf16[256,8,64,1]{0,2,3,1:T(8,128)(2,1)} %bitcast.231, bf16[256,8,3,64]{0,3,2,1:T(8,128)(2,1)S(1)} %bitcast.225), kind=kOutput, calls=%fused_computation.6 | convolution fusion | flops 206039040 | bytes 13680640 | tf_op jit(solution)/shard_map/qkgd,skd->kgqs/dot_general | solution.py:750
  328.4 4.3 fusion.3
  337.0 3.5 fusion.21
  340.8 5.1 %convolution_convert_fusion.2.grad_b = bf16[1536,1536]{1,0:T(8,128)(2,1)} fusion(bf16[256,1536]{0,1:T(8,128)(2,1)S(1)} %bitcast.211, f32[256,1536]{1,0:T(8,128)} %copy-done.3), kind=kOutput, calls=%fused_computation.3 | convolution fusion | flops 1210712064 | bytes 7077888 | tf_op jit(solution)/shard_map/dot_general | solution.py:521
  346.0 5.5 %convolution_convert_fusion.grad_a = bf16[1536,2560]{1,0:T(8,128)(2,1)} fusion(bf16[256,2560]{0,1:T(8,128)(2,1)S(1)} %bitcast.215, bf16[256,1536]{1,0:T(8,128)(2,1)S(1)} %copy-done.2, f32[1536]{0:T(1024)S(1)} %reshape.253, f32[256]{0:T(256)S(1)} %get-tuple-element.81), kind=kOutput, calls=%fused_computation.1 | convolution fusion | flops 2018770944 | bytes 9968640 | tf_op jit(solution)/shard_map/dot_general | solution.py:521
  353.1 6.2 %all-to-all-done.2 = bf16[8,128,1536]{2,1,0:T(8,128)(2,1)} async-done(((bf16[8,128,1536]{2,1,0:T(8,128)(2,1)}), bf16[8,128,1536]{2,1,0:T(8,128)(2,1)}, u32[]{:S(2)}, u32[]{:S(2)}) %all-to-all-start.2) | async-done | bytes 3145760 | tf_op jit(solution)/shard_map/all_to_all | solution.py:710
  359.3 3.2 convolution_multiply_fusion
  362.5 3.9 fusion.13
  371.3 71.2 %shard_map.232 = (f32[192,640]{1,0:T(8,128)S(1)}, f32[192,384]{1,0:T(8,128)S(1)}, f32[8,256]{1,0:T(8,128)S(1)}) custom-call(bf16[1536,2560]{1,0:T(8,128)(2,1)} %convolution_convert_fusion.grad_a, bf16[1536,1536]{1,0:T(8,128)(2,1)S(1)} %copy-done, f32[8,4,8,256]{3,2,1,0:T(8,128)S(1)} %select_maximum_fusion.grad_s), custom_call_target="tpu_custom_call" | custom-call | bytes 1000000 | tf_op jit(solution)/shard_map/pallas_call | solution.py:476
  445.0 3.4 fusion.43
  (174 shorter events, 45.5 us)
Async XLA Ops:
  7.2 4.2 copy-start.21
  7.2 4.2 copy-start.24
  7.2 4.2 copy-start.23
  7.2 172.7 %all-gather.3.cloned.1.call-start = ((), (), s32[]{:S(2)}) async-start(), calls=%async_computation.5 | async-start | bytes 7864320 | tf_op jit(solution)/shard_map/all_gather | solution.py:623
  8.6 44.7 %copy-start.2 = (bf16[256,1536]{1,0:T(8,128)(2,1)S(1)}, bf16[256,1536]{1,0:T(8,128)(2,1)}, u32[]{:S(2)}) copy-start(bf16[256,1536]{1,0:T(8,128)(2,1)} %param.14) | copy-start | bytes 2359300
  51.5 177.5 %all-gather.5.cloned.1.call-start = ((), (), s32[]{:S(2)}) async-start(), calls=%async_computation.6 | async-start | bytes 3932160 | tf_op jit(solution)/shard_map/all_gather | solution.py:624
  52.2 314.3 %reduce-scatter.3.cloned.1.call-start = ((), (), s32[]{:S(2)}) async-start(), calls=%async_computation.7 | async-start | bytes 3932160 | tf_op jit(solution)/shard_map/reduce_scatter | solution.py:687
  115.5 4.5 copy-start.27
  119.9 5.0 %copy-start.12 = (bf16[256,4,384]{0,2,1:T(8,128)(2,1)}, bf16[256,4,384]{0,2,1:T(8,128)(2,1)S(1)}, u32[]{:S(2)}) copy-start(bf16[256,4,384]{0,2,1:T(8,128)(2,1)S(1)} %copy.64) | copy-start | bytes 2359300
  120.2 4.7 %copy-start.20 = (bf16[256,4,128]{0,2,1:T(8,128)(2,1)}, bf16[256,4,128]{0,2,1:T(8,128)(2,1)S(1)}, u32[]{:S(2)}) copy-start(bf16[256,4,128]{0,2,1:T(8,128)(2,1)S(1)} %copy.65) | copy-start | bytes 786436
  128.5 4.1 copy-start.7
  128.5 4.4 copy-start.22
  169.7 4.5 slice-start
  169.7 5.5 %slice-start.1 = ((s8[6291456]{0:T(1024)(128)(4,1)}), s8[2097152]{0:T(1024)(128)(4,1)S(1)}, s32[]{:S(2)}) async-start(s8[6291456]{0:T(1024)(128)(4,1)} %bitcast.202), calls=%async_computation.10 | async-start | bytes 4194304
  189.6 5.3 %copy-start.14 = (bf16[1024,1536]{1,0:T(8,128)(2,1)S(1)}, bf16[1024,1536]{1,0:T(8,128)(2,1)}, u32[]{:S(2)}) copy-start(bf16[1024,1536]{1,0:T(8,128)(2,1)} %fusion.4) | copy-start | bytes 9437188
  238.9 11.6 %copy-start.29 = (bf16[1024,1024]{1,0:T(8,128)(2,1)}, bf16[1024,1024]{1,0:T(8,128)(2,1)S(1)}, u32[]{:S(2)}) copy-start(bf16[1024,1024]{1,0:T(8,128)(2,1)S(1)} %get-tuple-element.64) | copy-start | bytes 6291460
  238.9 11.6 %copy-start.30 = (bf16[1024,1024]{1,0:T(8,128)(2,1)}, bf16[1024,1024]{1,0:T(8,128)(2,1)S(1)}, u32[]{:S(2)}) copy-start(bf16[1024,1024]{1,0:T(8,128)(2,1)S(1)} %get-tuple-element.65) | copy-start | bytes 6291460
  238.9 11.6 %copy-start.17 = (bf16[1024,1024]{1,0:T(8,128)(2,1)S(1)}, bf16[1024,1024]{1,0:T(8,128)(2,1)}, u32[]{:S(2)}) copy-start(bf16[1024,1024]{1,0:T(8,128)(2,1)} %copy-done.16) | copy-start | bytes 6291460
  238.9 11.6 %copy-start.28 = (bf16[1024,1536]{1,0:T(8,128)(2,1)S(1)}, bf16[1024,1536]{1,0:T(8,128)(2,1)}, u32[]{:S(2)}) copy-start(bf16[1024,1536]{1,0:T(8,128)(2,1)} %all-gather.5.cloned.1.call-done) | copy-start | bytes 9437188
  265.3 42.4 %all-to-all-start = ((bf16[8,128,1536]{2,1,0:T(8,128)(2,1)}), bf16[8,128,1536]{2,1,0:T(8,128)(2,1)}, u32[]{:S(2)}, u32[]{:S(2)}) async-start(bf16[8,128,1536]{2,1,0:T(8,128)(2,1)} %bitcast.219), calls=%async_computation | async-start | bytes 6291456 | tf_op jit(solution)/shard_map/all_to_all | solution.py:698
  269.7 175.3 %reduce-scatter.5.cloned.1.call-start = ((), (), s32[]{:S(2)}) async-start(), calls=%async_computation.8 | async-start | bytes 7864320 | tf_op jit(solution)/shard_map/reduce_scatter | solution.py:708
  307.6 5.6 %slice-start.2 = ((s8[4718592]{0:T(1024)(128)(4,1)}), s8[4194304]{0:T(1024)(128)(4,1)S(1)}, s32[]{:S(2)}) async-start(s8[4718592]{0:T(1024)(128)(4,1)} %bitcast.205), calls=%async_computation.11 | async-start | bytes 8388608
  307.6 5.6 %slice-start.3 = ((s8[4718592]{0:T(1024)(128)(4,1)}), s8[524288]{0:T(1024)(128)(4,1)S(1)}, s32[]{:S(2)}) async-start(s8[4718592]{0:T(1024)(128)(4,1)} %bitcast.205), calls=%async_computation.12 | async-start | bytes 1048576
  317.0 4.7 %copy-start.26 = (f32[8,3,256]{2,1,0:T(4,128)S(1)}, f32[8,3,256]{2,1,0:T(4,128)}, u32[]{:S(2)}) copy-start(f32[8,3,256]{2,1,0:T(4,128)} %copy-done.25) | copy-start | bytes 73732
  317.0 42.4 %all-to-all-start.2 = ((bf16[8,128,1536]{2,1,0:T(8,128)(2,1)}), bf16[8,128,1536]{2,1,0:T(8,128)(2,1)}, u32[]{:S(2)}, u32[]{:S(2)}) async-start(bf16[8,128,1536]{2,1,0:T(8,128)(2,1)} %bitcast.218), calls=%async_computation.2 | async-start | bytes 6291456 | tf_op jit(solution)/shard_map/all_to_all | solution.py:710
  321.6 6.7 %slice-start.4 = ((s8[6291456]{0:T(1024)(128)(4,1)}), s8[4194304]{0:T(1024)(128)(4,1)S(1)}, s32[]{:S(2)}) async-start(s8[6291456]{0:T(1024)(128)(4,1)} %bitcast.212), calls=%async_computation.13 | async-start | bytes 8388608
  321.6 6.7 %slice-start.5 = ((s8[6291456]{0:T(1024)(128)(4,1)}), s8[2097152]{0:T(1024)(128)(4,1)S(1)}, s32[]{:S(2)}) async-start(s8[6291456]{0:T(1024)(128)(4,1)} %bitcast.212), calls=%async_computation.14 | async-start | bytes 4194304
  336.1 4.4 copy-start.10
  340.8 5.1 %copy-start.11 = (bf16[256,4,640]{0,2,1:T(8,128)(2,1)S(1)}, bf16[256,4,640]{0,2,1:T(8,128)(2,1)}, u32[]{:S(2)}) copy-start(bf16[256,4,640]{0,2,1:T(8,128)(2,1)} %copy-done.10) | copy-start | bytes 3932164
  346.0 5.5 %copy-start.4 = (f32[256,1536]{1,0:T(8,128)S(1)}, f32[256,1536]{1,0:T(8,128)}, u32[]{:S(2)}) copy-start(f32[256,1536]{1,0:T(8,128)} %copy-done.3) | copy-start | bytes 4718596
  346.0 5.5 %copy-start.18 = (f32[256,1536]{1,0:T(8,128)S(1)}, f32[256,1536]{1,0:T(8,128)}, u32[]{:S(2)}) copy-start(f32[256,1536]{1,0:T(8,128)} %get-tuple-element.93) | copy-start | bytes 4718596
  351.5 7.8 %copy-start.19 = (pred[2,256,1024]{2,1,0:T(32,128)(4,1)S(1)}, pred[2,256,1024]{2,1,0:T(32,128)(4,1)}, u32[]{:S(2)}) copy-start(pred[2,256,1024]{2,1,0:T(32,128)(4,1)} %get-tuple-element.78) | copy-start | bytes 1572868
  (13 other events, 34.8 us)
Sparse Core Ops, SparseCore 0:
  51.6 113.9 all-gather.2
  167.2 61.7 all-gather.4
  231.2 58.8 reduce-scatter.2
  292.3 110.7 reduce-scatter.4

commit v3 on v2

--- a/solution.py
+++ b/solution.py
@@ -505,6 +505,301 @@
     )(grad_a, grad_b, grad_s)
 
 
+def expert_kernel(key, mine, normed_hbm, upstream_hbm, gu_hbm, own_down,
+                  in_ref, prod_ref, gate_grad_ref, grad_gu, sum_down,
+                  x_t, ups, gu, down, act, silu, slope, both, gd, rec_right, rec_left, stage, gate,
+                  load_sem, src_sem, stage_sem, zss, zrs, rss, rrs):
+    col = lax.axis_index("col")
+    sources, _, length = key.shape
+    slots = in_ref.shape[0]
+    capacity = slots // sources
+    units = gu.shape[1] // 2
+    width = units // 4
+    chunk = 256
+    x = in_ref
+    right_dev, left_dev = {"col": (col + 1) % 4}, {"col": (col + 3) % 4}
+
+    load_gu = pltpu.make_async_copy(gu_hbm, gu, load_sem.at[0])
+    load_gu.start()
+    load_down = pltpu.make_async_copy(own_down, down.at[col], load_sem.at[1])
+    load_down.start()
+
+    def fetch(s, slot):
+        rows = pl.ds(pl.multiple_of(s * length, 16), length)
+        for i, hbm in enumerate((normed_hbm, upstream_hbm)):
+            to = prod_ref.at[pl.ds(pl.multiple_of((slot * 2 + i) * length, 16), length), :]
+            yield pltpu.make_async_copy(hbm.at[rows, :], to, src_sem.at[slot, i])
+
+    for copy in fetch(0, 0):
+        copy.start()
+    greet((), (1, 2, 3))
+
+    def pass_on(c, source, right, left):
+        for d, (cond, there) in enumerate(((right, right_dev), (left, left_dev))):
+            @pl.when(cond)
+            def _():
+                remote(source, down.at[c], zss.at[c, d], zrs.at[c], there).start()
+
+    pass_on(col, own_down, col < 3, col > 0)
+
+    def ag_step(s):
+        @pl.when(col >= s)
+        def _():
+            c = col - s
+            remote(down.at[c], down.at[c], zss.at[c, 0], zrs.at[c], right_dev).wait_recv()
+            @pl.when(col < 3)
+            def _():
+                remote(down.at[c], down.at[c], zss.at[c, 0], zrs.at[c], right_dev).start()
+        @pl.when(col + s < 4)
+        def _():
+            c = col + s
+            remote(down.at[c], down.at[c], zss.at[c, 1], zrs.at[c], left_dev).wait_recv()
+            @pl.when(col > 0)
+            def _():
+                remote(down.at[c], down.at[c], zss.at[c, 1], zrs.at[c], left_dev).start()
+
+    def to_right(d):
+        target = rec_right.at[d - 1]
+        return remote(target, target, rss.at[0, d - 1], rrs.at[0, d - 1], right_dev)
+
+    def to_left(d):
+        target = rec_left.at[d]
+        return remote(target, target, rss.at[1, d], rrs.at[1, d], left_dev)
+
+    def from_end(d):
+        if d > 0:
+            @pl.when(col == 0)
+            def _():
+                remote(gd.at[d], rec_right.at[d - 1], rss.at[0, d - 1], rrs.at[0, d - 1], right_dev).start()
+        if d < 3:
+            @pl.when(col == 3)
+            def _():
+                remote(gd.at[d], rec_left.at[d], rss.at[1, d], rrs.at[1, d], left_dev).start()
+
+    def add_rows(target, term):
+        def body(i, carry):
+            rows = pl.ds(pl.multiple_of(i * 64, 64), 64)
+            total = target[rows, :].astype(jnp.float32) + term[rows, :].astype(jnp.float32)
+            target[rows, :] = total.astype(target.dtype)
+            return carry
+        lax.fori_loop(0, width // 64, body, 0)
+
+    def hop_right(at, d):
+        @pl.when(col == at)
+        def _():
+            to_right(d).wait_recv()
+            add_rows(rec_right.at[d - 1], gd.at[d])
+            to_right(d).start()
+
+    def hop_left(at, d):
+        @pl.when(col == at)
+        def _():
+            to_left(d).wait_recv()
+            add_rows(rec_left.at[d], gd.at[d])
+            to_left(d).start()
+
+    def select(s, carry):
+        slot = s % 2
+        @pl.when(s + 1 < sources)
+        def _():
+            for copy in fetch(s + 1, 1 - slot):
+                copy.start()
+        for copy in fetch(s, slot):
+            copy.wait()
+        chosen = key[s] == lax.broadcasted_iota(jnp.int32, (capacity, length), 0)
+        value = jnp.sum(jnp.where(chosen, mine[s], 0.0), axis=1, keepdims=True)
+        rows = pl.ds(pl.multiple_of(s * capacity, 16), capacity)
+        gate[rows, :] = jnp.broadcast_to(value, (capacity, gate.shape[1]))
+        one_hot = jnp.where(chosen, 1.0, 0.0).astype(x.dtype)
+        for i, target in enumerate((x, ups)):
+            block = prod_ref[pl.ds(pl.multiple_of((slot * 2 + i) * length, 16), length), :]
+            target[rows, :] = dot(one_hot, block).astype(target.dtype)
+        return carry
+    lax.fori_loop(0, sources, select, 0)
+
+    load_gu.wait()
+
+    def forward(c):
+        first = pl.ds(c * width, width)
+        second = pl.ds(units + c * width, width)
+        def body(m, carry):
+            rows = pl.ds(pl.multiple_of(m * chunk, chunk), chunk)
+            gate_pre = dot(x[rows, :], gu[:, first])
+            up_pre = dot(x[rows, :], gu[:, second])
+            sigma = jax.nn.sigmoid(gate_pre)
+            silu_gate = gate_pre * sigma
+            silu[rows, first] = silu_gate
+            slope[rows, first] = up_pre * sigma * (1.0 + gate_pre * (1.0 - sigma))
+            low = (silu_gate * up_pre).astype(act.dtype)
+            act[rows, first] = low
+            both[rows, first] = (low.astype(jnp.float32) * gate[rows, 0:1]).astype(both.dtype)
+            return carry
+        lax.fori_loop(0, slots // chunk, body, 0)
+        gd[c] = t_dot(both[:, first], ups[...]).astype(gd.dtype)
+
+    forward(3)
+    from_end(3)
+    forward(0)
+    from_end(0)
+    ag_step(1)
+    forward(2)
+    forward(1)
+    for d in (2, 1):
+        if d > 0:
+            @pl.when(col == 0)
+            def _():
+                remote(gd.at[d], rec_right.at[d - 1], rss.at[0, d - 1], rrs.at[0, d - 1], right_dev).start()
+    for d in (1, 2):
+        @pl.when(col == 3)
+        def _():
+            remote(gd.at[d], rec_left.at[d], rss.at[1, d], rrs.at[1, d], left_dev).start()
+    load_down.wait()
+
+    def turn(m, carry):
+        rows = pl.ds(pl.multiple_of(m * chunk, chunk), chunk)
+        x_t[:, rows] = x[rows, :].T
+        return carry
+    lax.fori_loop(0, slots // chunk, turn, 0)
+    gate_grad_ref[...] = jnp.zeros_like(gate_grad_ref)
+
+    def out_stage(c, slot):
+        for i in range(2):
+            yield pltpu.make_async_copy(
+                stage.at[slot, :, pl.ds(i * width, width)],
+                grad_gu.at[:, pl.ds(pl.multiple_of(i * units + c * width, width), width)],
+                stage_sem.at[slot, i],
+            )
+
+    def backward(k):
+        c = unit_order(col, k)
+        first = pl.ds(pl.multiple_of(c * width, width), width)
+        second = pl.ds(pl.multiple_of(units + c * width, width), width)
+        def body(m, carry):
+            rows = pl.ds(pl.multiple_of(m * chunk, chunk), chunk)
+            plain = dot_t(ups[rows, :], down[c])
+            term = jnp.sum(act[rows, first].astype(jnp.float32) * plain, axis=1, keepdims=True)
+            gate_grad_ref[rows, :] += jnp.broadcast_to(term, (chunk, gate_grad_ref.shape[1]))
+            act_grad = plain * gate[rows, 0:1]
+            both[rows, first] = (act_grad * slope[rows, first]).astype(both.dtype)
+            both[rows, second] = (act_grad * silu[rows, first]).astype(both.dtype)
+            return carry
+        lax.fori_loop(0, slots // chunk, body, 0)
+        slot = k % 2
+        if k >= 2:
+            for copy in out_stage(unit_order(col, k - 2), slot):
+                copy.wait()
+        def grads(i, carry):
+            rows = pl.ds(pl.multiple_of(i * chunk, chunk), chunk)
+            stage[slot, rows, 0:width] = dot(x_t[rows, :], both[:, first]).astype(stage.dtype)
+            stage[slot, rows, width : 2 * width] = dot(x_t[rows, :], both[:, second]).astype(stage.dtype)
+            return carry
+        lax.fori_loop(0, x_t.shape[0] // chunk, grads, 0)
+        for copy in out_stage(c, slot):
+            copy.start()
+
+    backward(0)
+    ag_step(2)
+    hop_right(1, 3)
+    hop_left(2, 0)
+    backward(1)
+    backward(2)
+    ag_step(3)
+    hop_right(1, 2)
+    hop_right(2, 3)
+    hop_left(2, 1)
+    hop_left(1, 0)
+    backward(3)
+
+    def inputs(m, carry):
+        rows = pl.ds(pl.multiple_of(m * chunk, chunk), chunk)
+        in_ref[rows, :] = dot_t(both[rows, :], gu[...]).astype(in_ref.dtype)
+        return carry
+    lax.fori_loop(0, slots // chunk, inputs, 0)
+
+    def outputs(m, carry):
+        rows = pl.ds(pl.multiple_of(m * chunk, chunk), chunk)
+        total = dot(act[rows, 0:width], down[0])
+        for c in range(1, 4):
+            total = total + dot(act[rows, c * width : (c + 1) * width], down[c])
+        prod_ref[rows, :] = total.astype(prod_ref.dtype)
+        return carry
+    lax.fori_loop(0, slots // chunk, outputs, 0)
+
+    for k in (2, 3):
+        for copy in out_stage(unit_order(col, k), k % 2):
+            copy.wait()
+    for d in range(4):
+        @pl.when(col == d)
+        def _():
+            if d > 0:
+                to_right(d).wait_recv()
+            if d < 3:
+                to_left(d).wait_recv()
+            def body(i, carry):
+                rows = pl.ds(pl.multiple_of(i * 64, 64), 64)
+                total = gd[d, rows, :].astype(jnp.float32)
+                if d > 0:
+                    total = total + rec_right[d - 1, rows, :].astype(jnp.float32)
+                if d < 3:
+                    total = total + rec_left[d, rows, :].astype(jnp.float32)
+                sum_down[rows, :] = total
+                return carry
+            lax.fori_loop(0, width // 64, body, 0)
+            for e in range(d + 1, 4):
+                to_right(e).wait_send()
+            for e in range(d):
+                to_left(e).wait_send()
+            if d < 3:
+                for e in range(d + 1):
+                    remote(down.at[e], down.at[e], zss.at[e, 0], zrs.at[e], right_dev).wait_send()
+            if d > 0:
+                for e in range(d, 4):
+                    remote(down.at[e], down.at[e], zss.at[e, 1], zrs.at[e], left_dev).wait_send()
+
+
+def run_expert(key, mine, normed, upstream, full_gu, own_down):
+    sources, length = key.shape
+    model, units = full_gu.shape[0], full_gu.shape[1] // 2
+    width = own_down.shape[0]
+    slots = sources * length // 2
+    low, f32 = normed.dtype, jnp.float32
+    sems = pltpu.SemaphoreType.DMA
+    vm = pl.BlockSpec(memory_space=pltpu.VMEM)
+    return pl.pallas_call(
+        expert_kernel,
+        out_shape=(
+            jax.ShapeDtypeStruct((slots, model), low),
+            jax.ShapeDtypeStruct((slots, model), low),
+            jax.ShapeDtypeStruct((slots, 128), f32),
+            jax.ShapeDtypeStruct((model, 2 * units), low),
+            jax.ShapeDtypeStruct((width, model), f32),
+        ),
+        in_specs=[vm, vm, ANY, ANY, ANY, ANY],
+        out_specs=(vm, vm, vm, ANY, vm),
+        scratch_shapes=[
+            pltpu.VMEM((model, slots), low),
+            pltpu.VMEM((slots, model), low),
+            pltpu.VMEM((model, 2 * units), low),
+            pltpu.VMEM((4, width, model), low),
+            pltpu.VMEM((slots, units), low),
+            pltpu.VMEM((slots, units), f32),
+            pltpu.VMEM((slots, units), f32),
+            pltpu.VMEM((slots, 2 * units), low),
+            pltpu.VMEM((4, width, model), low),
+            pltpu.VMEM((3, width, model), low),
+            pltpu.VMEM((3, width, model), low),
+            pltpu.VMEM((2, model, 2 * width), low),
+            pltpu.VMEM((slots, 128), f32),
+            sems((2,)), sems((2, 2)), sems((2, 2)),
+            sems((4, 2)), sems((4,)), sems((2, 3)), sems((2, 3)),
+        ],
+        compiler_params=pltpu.CompilerParams(
+            collective_id=4, has_side_effects=True, vmem_limit_bytes=60 * 2**20
+        ),
+        cost_estimate=pl.CostEstimate(flops=0, bytes_accessed=1_000_000, transcendentals=0),
+    )(key.reshape(sources, 1, length), mine.reshape(sources, 1, length), normed, upstream, full_gu, own_down)
+
+
 def rms_factor(rows_in):
     return lax.rsqrt(jnp.mean(rows_in * rows_in, axis=1, keepdims=True) + EPSILON)
 
@@ -556,6 +851,50 @@
 
     small = lax.psum_scatter(grad_s, "row", scatter_dimension=0, tiled=False)
     return both(grad_a), both(grad_b), lax.psum_scatter(small, "col", scatter_dimension=0, tiled=False)
+
+
+def expert_elsewhere(place, routed, mine, plane_normed, plane_upstream, full_gu, own_down):
+    rows, length = place.shape
+    model = plane_normed.shape[1]
+    hidden_units = full_gu.shape[1] // 2
+    capacity = 2 * length * TOP // rows
+    full_down = lax.all_gather(own_down, "col", axis=0, tiled=True)
+    chosen_rows = (
+        (place[:, None, :] == jnp.arange(capacity, dtype=jnp.int32)[None, :, None]) & routed[:, None, :]
+    ).astype(jnp.bfloat16)
+
+    def of_slots(plane):
+        return jnp.einsum(
+            "rct,rtd->rcd",
+            chosen_rows,
+            plane.reshape(rows, length, model),
+            preferred_element_type=jnp.float32,
+        ).astype(jnp.bfloat16).reshape(rows * capacity, model)
+
+    grouped, grouped_up = of_slots(plane_normed), of_slots(plane_upstream)
+    slot_gate = jnp.sum(jnp.where(chosen_rows > 0, mine[:, None, :], 0.0), axis=2)
+    slot_gate = slot_gate.reshape(rows * capacity, 1)
+    grouped_grad = (grouped_up.astype(jnp.float32) * slot_gate).astype(jnp.bfloat16)
+    both_pre = dot(grouped, full_gu)
+    gate_pre, up_pre = both_pre[:, :hidden_units], both_pre[:, hidden_units:]
+    sigma = jax.nn.sigmoid(gate_pre)
+    silu_gate = gate_pre * sigma
+    activation = (silu_gate * up_pre).astype(jnp.bfloat16)
+    grad_down_local = t_dot(activation, grouped_grad).astype(jnp.bfloat16)
+    grad_down = lax.psum_scatter(grad_down_local, "col", scatter_dimension=0, tiled=True)
+    act_grad = dot_t(grouped_grad, full_down)
+    both_grad = jnp.concatenate(
+        [
+            (act_grad * up_pre * sigma * (1.0 + gate_pre * (1.0 - sigma))).astype(jnp.bfloat16),
+            (act_grad * silu_gate).astype(jnp.bfloat16),
+        ],
+        axis=1,
+    )
+    in_grad = dot_t(both_grad, full_gu).astype(jnp.bfloat16)
+    produced = dot(activation, full_down).astype(jnp.bfloat16)
+    slot_gate_grad = jnp.sum(produced.astype(jnp.float32) * grouped_up.astype(jnp.float32), axis=1)
+    grad_gu_local = t_dot(grouped, both_grad).astype(jnp.bfloat16)
+    return in_grad, produced, slot_gate_grad, grad_gu_local, grad_down.astype(jnp.float32)
 
 
 def masked_scores(queries, heads_of_key, segments, head_scale):
@@ -621,7 +960,6 @@
     else:
         full_a, full_out, small, plane_upstream = gather_all(own_a, w_out, own_s, cotangent)
     full_gu = lax.all_gather(own_gu, "col", axis=0, tiled=True)
-    full_down = lax.all_gather(own_down, "col", axis=0, tiled=True)
     full_router = small[:, :, :router_cols, :block].transpose(1, 3, 0, 2).reshape(model, experts)
     gain_one = small[:, :, router_cols, :piece].transpose(1, 0, 2).reshape(model).astype(jnp.float32)
     gain_two = small[:, :, router_cols + 1, :piece].transpose(1, 0, 2).reshape(model).astype(jnp.float32)
@@ -658,54 +996,25 @@
     gate_table = jnp.sum(jnp.where(named, gate_probs[:, :, None], 0.0), axis=1)
     gate_table = jnp.where(jnp.any(named, axis=1), gate_table, -1.0)
     plane_normed, plane_gate = spread(normed_two, gate_table.T)
-    plane_normed = plane_normed.reshape(rows, length, model)
-    plane_upstream = plane_upstream.reshape(rows, length, model)
     mine = lax.dynamic_index_in_dim(plane_gate, lax.axis_index("row"), axis=1, keepdims=False)
     routed = mine >= 0.0
     place = jnp.cumsum(routed.astype(jnp.int32), axis=1) - 1
-    slots = jnp.arange(capacity, dtype=jnp.int32)
-    chosen_rows = (
-        (place[:, None, :] == slots[None, :, None]) & routed[:, None, :]
-    ).astype(jnp.bfloat16)
-    grouped = jnp.einsum(
-        "rct,rtd->rcd", chosen_rows, plane_normed, preferred_element_type=jnp.float32
-    ).astype(jnp.bfloat16).reshape(rows * capacity, model)
-    slot_gate = jnp.sum(
-        jnp.where(chosen_rows > 0, mine[:, None, :], 0.0), axis=2
-    ).reshape(rows * capacity, 1)
-    grouped_up = jnp.einsum(
-        "rct,rtd->rcd", chosen_rows, plane_upstream, preferred_element_type=jnp.float32
-    ).reshape(rows * capacity, model)
-    grouped_grad = (grouped_up * slot_gate).astype(jnp.bfloat16)
-
-    both_pre = dot(grouped, full_gu)
-    gate_pre, up_pre = both_pre[:, :hidden_units], both_pre[:, hidden_units:]
-    sigma = jax.nn.sigmoid(gate_pre)
-    silu_gate = gate_pre * sigma
-    activation = (silu_gate * up_pre).astype(jnp.bfloat16)
-    grad_down_local = t_dot(activation, grouped_grad).astype(jnp.bfloat16)
-    grad_down = lax.psum_scatter(grad_down_local, "col", scatter_dimension=0, tiled=True)
-    later_grad, _ = lax.optimization_barrier((grouped_grad, grad_down_local))
-    act_grad = dot_t(later_grad, full_down)
-    both_grad = jnp.concatenate(
-        [
-            (act_grad * up_pre * sigma * (1.0 + gate_pre * (1.0 - sigma))).astype(jnp.bfloat16),
-            (act_grad * silu_gate).astype(jnp.bfloat16),
-        ],
-        axis=1,
-    )
-    in_grad = dot_t(both_grad, full_gu).astype(jnp.bfloat16)
+    if on_small_slice():
+        in_grad, produced, slot_gate_grad, grad_gu_local, grad_down = run_expert(
+            jnp.where(routed, place, -1), mine, plane_normed, plane_upstream, full_gu, own_down
+        )
+        slot_gate_grad = slot_gate_grad[:, 0]
+    else:
+        in_grad, produced, slot_gate_grad, grad_gu_local, grad_down = expert_elsewhere(
+            place, routed, mine, plane_normed, plane_upstream, full_gu, own_down
+        )
+    grad_gu = lax.psum_scatter(grad_gu_local, "col", scatter_dimension=0, tiled=True)
     back_grad = lax.all_to_all(
         in_grad.reshape(rows, capacity, model), "row", split_axis=0, concat_axis=0, tiled=True
     ).reshape(experts * capacity, model)
-    later_act, _ = lax.optimization_barrier((activation, in_grad))
-    produced = dot(later_act, full_down).astype(jnp.bfloat16)
-    slot_gate_grad = jnp.sum(produced.astype(jnp.float32) * grouped_up, axis=1)
     back_gate_grad = lax.all_to_all(
         slot_gate_grad.reshape(rows, 1, capacity), "row", split_axis=0, concat_axis=0, tiled=True
     ).reshape(experts * capacity)
-    grad_gu_local = t_dot(grouped, both_grad).astype(jnp.bfloat16)
-    grad_gu = lax.psum_scatter(grad_gu_local, "col", scatter_dimension=0, tiled=True)
     produced, back_grad = lax.optimization_barrier((produced, back_grad))
     back_rows = lax.all_to_all(
         produced.reshape(rows, capacity, model), "row", split_axis=0, concat_axis=0, tiled=True
@@ -792,10 +1101,7 @@
         ],
         axis=2,
     )
-    grad_down = grad_down.astype(jnp.float32)[None]
-    grad_a_full, d_tokens, output, grad_down = lax.optimization_barrier(
-        (grad_a_full, d_tokens, output, grad_down)
-    )
+    grad_a_full, d_tokens, output = lax.optimization_barrier((grad_a_full, d_tokens, output))
     sum_a, sum_out, sum_s = reduce_all(grad_a_full, grad_out_full, grad_s)
     return (
         output,
@@ -809,7 +1115,7 @@
         sum_s[:router_cols, :block].T,
         grad_gu[:, :hidden_units].astype(jnp.float32)[None],
         grad_gu[:, hidden_units:].astype(jnp.float32)[None],
-        grad_down,
+        grad_down[None],
     )
 
 

time: 460 us -> 453 us (0.985)
  Pallas kernels: 200 us -> 278 us
  matrix products: 119 us -> 57.9 us
  waiting for transfers between devices: 56.8 us -> 36.4 us
    pallas_call x0 -> x1, Pallas kernels: none -> 78.2 us  [run_expert(): pl.pallas_call(expert_kernel, out_shape=(jax.ShapeDtypeStruct((slots, mod...]
    all_gather x1 -> x0, waiting for transfers between devices: 28.7 us -> none  [per_device(): full_down = lax.all_gather(own_down, 'col', axis=0, tiled=True)]
    dot_general x5 -> x3, matrix products: 28.8 us -> 8.76 us  [dot_t(): lax.dot_general(a, b, (((1,), (1,)), ((), ())), preferred_element_type=jn...]
    dot_general x8 -> x6, matrix products: 37.5 us -> 20.3 us  [dot(): return jnp.dot(a, b, preferred_element_type=jnp.float32)]
    dot_general x5 -> x3, matrix products: 28 us -> 11 us  [t_dot(): lax.dot_general(a, b, (((0,), (0,)), ((), ())), preferred_element_type=jn...]
    all_to_all x1, waiting for transfers between devices: 21.1 us -> 32.4 us  [per_device(): lax.all_to_all(in_grad.reshape(rows, capacity, model), 'row', split_axis=...]
    dot_general x2 -> x0, matrix products: 6.82 us -> none  [the longest x1 4.18 us: per_device(): jnp.einsum('rct,rtd->rcd', chosen_rows, plane_upstream, preferred_element...]
    unnamed x81 -> x76, local copies, waits for them, and re-layouts: 10.8 us -> 5.38 us
  transfers between devices with their start and end apart: 6 -> 4, of which waited for: 3 -> 2; matrix products, arithmetic and copies ran while one was open for 32% -> 20% of each run, Pallas kernels for 35% -> 36%
where the time goes in v3:
time: 453 us; the launch traced here: 448 us
  Pallas kernels  278 us (61%)
  matrix products  57.9 us (13%)
  waiting for transfers between devices  36.4 us (8%)
  other arithmetic  25.1 us (6%)
  local copies, waits for them, and re-layouts  18.7 us (4%)
  between operations  14.8 us (3%)
  starting transfers between devices  9.4 us (2%)
  blocking collectives  7.66 us (2%)
    pallas_call x1, Pallas kernels, run_expert(): pl.pallas_call(expert_kernel, out_shape=(jax.ShapeDtypeStruct((slots, mod...  78.2 us
    pallas_call x1, Pallas kernels, reduce_attention(): pl.pallas_call(reduce_kernel, out_shape=(jax.ShapeDtypeStruct((block, wid...  70.9 us
    pallas_call x1, Pallas kernels, gather_plane(): pl.pallas_call(functools.partial(plane_kernel, count), out_shape=tuple((j...  56.3 us
    pallas_call x1, Pallas kernels, gather_line(): pl.pallas_call(line_kernel, out_shape=(jax.ShapeDtypeStruct((own_a.shape[...  39.3 us
    pallas_call x1, Pallas kernels, spread_tokens(): pl.pallas_call(spread_kernel, out_shape=(jax.ShapeDtypeStruct((8 * own_c....  33.5 us
    all_to_all x1, waiting for transfers between devices, per_device(): lax.all_to_all(in_grad.reshape(rows, capacity, model), 'row', split_axis=...  32.4 us
    dot_general x6, matrix products, dot(): return jnp.dot(a, b, preferred_element_type=jnp.float32)  20.3 us
    dot_general x3, matrix products, t_dot(): lax.dot_general(a, b, (((0,), (0,)), ((), ())), preferred_element_type=jn...  11 us
  transfers between devices with their start and end apart: 4, of which 2 were waited for; matrix products, arithmetic and copies ran while one was open for 20% of the time, Pallas kernels for 36%

profile of v3, /device:TPU:0, one launch (start us, length us, event | category | flops | bytes accessed | tf_op | source)
XLA Modules:
  0.0 448.2 jit_solution(9634144955924679229)
XLA Ops:
  8.6 2.7 pad_maximum_fusion
  12.0 39.3 %shard_map.229 = (bf16[192,2560]{1,0:T(8,128)(2,1)}, bf16[192,1536]{1,0:T(8,128)(2,1)}, bf16[4,8,16,256]{3,2,1,0:T(8,128)(2,1)}, bf16[2048,1536]{1,0:T(8,128)(2,1)}) custom-call(bf16[192,640]{1,0:T(8,128)(2,1)} %pad_maximum_fusion.2.own_a, bf16[192,384]{1,0:T(8,128)(2,1)} %own_b.1, bf16[16,256]{1,0:T(8,128)(2,1)} %pad.26.own_s, bf16[256,1536]{1,0:T(8,128)(2,1)} %own_c.1), custom_call_target="tpu_custom_call" | custom-call | bytes 1000000 | tf_op jit(solution)/shard_map/pallas_call | solution.py:208
  52.5 56.3 %shard_map.230 = (bf16[1536,2560]{1,0:T(8,128)(2,1)}, bf16[1536,1536]{1,0:T(8,128)(2,1)}) custom-call(bf16[192,2560]{1,0:T(8,128)(2,1)} %get-tuple-element.40.refs_0_, bf16[192,1536]{1,0:T(8,128)(2,1)} %get-tuple-element.41.refs_1_), custom_call_target="tpu_custom_call" | custom-call | bytes 1000000 | tf_op jit(solution)/shard_map/pallas_call | solution.py:264
  109.6 6.6 %convolution_convert_fusion.2 = bf16[256,2560]{1,0:T(8,128)(2,1)} fusion(bf16[1536,2560]{1,0:T(8,128)(2,1)} %get-tuple-element.42, bf16[256,1536]{1,0:T(8,128)(2,1)S(1)} %copy-done, f32[1536]{0:T(1024)S(1)} %reshape.243, f32[256]{0:T(256)S(1)} %get-tuple-element.83), kind=kOutput, calls=%fused_computation.11 | convolution fusion | flops 2015494144 | bytes 9968640 | tf_op jit(solution)/shard_map/dot_general | solution.py:808
  116.2 2.9 reshape.228
  123.6 4.6 %fusion.68 = (f32[8,3,256]{2,1,0:T(4,128)S(1)}, f32[8,3,256,256]{2,3,1,0:T(8,128)}) fusion(pred[256,256]{0,1:T(8,128)(4,1)S(1)} %fusion.44, bf16[256,8,64,1]{0,2,3,1:T(8,128)(2,1)S(1)} %bitcast.191, bf16[256,8,3,64]{0,3,2,1:T(8,128)(2,1)S(1)} %bitcast.184), kind=kOutput, calls=%fused_computation.134 | convolution fusion | flops 207618304 | bytes 7430144 | tf_op jit(solution)/shard_map/sub | solution.py:979
  128.2 3.6 fusion.23
  132.3 1.5 multiply_reduce_fusion.2
  135.8 33.5 %shard_map.231 = (bf16[2048,1536]{1,0:T(8,128)(2,1)}, f32[8,8,256]{2,1,0:T(8,128)}) custom-call(bf16[256,1536]{1,0:T(8,128)(2,1)} %copy-done.1, f32[8,256]{1,0:T(8,128)} %select_bitcast_fusion.own_g), custom_call_target="tpu_custom_call" | custom-call | bytes 1000000 | tf_op jit(solution)/shard_map/pallas_call | solution.py:305
  171.7 78.2 %shard_map.232 = (bf16[1024,1536]{1,0:T(8,128)(2,1)}, bf16[1024,1536]{1,0:T(8,128)(2,1)}, f32[1024,128]{1,0:T(8,128)}, bf16[1536,2048]{1,0:T(8,128)(2,1)}, f32[256,1536]{1,0:T(8,128)}) custom-call(s32[8,1,256]{2,1,0:T(1,128)} %compare_select_fusion.key, f32[8,1,256]{2,1,0:T(1,128)} %copy-done.15, bf16[2048,1536]{1,0:T(8,128)(2,1)} %get-tuple-element.45.normed_hbm, ...), custom_call_target="tpu_custom_call" | custom-call | bytes 1000000 | tf_op jit(solution)/shard_map/pallas_call | solution.py:768
  251.2 7.7 %all_to_all.15 = f32[8,1,128]{2,1,0:T(1,128)S(1)} all-to-all(f32[8,1,128]{2,1,0:T(1,128)S(1)} %bitcast.209), channel_id=1, replica_groups=mesh['row'=8,'col'=4] {'row'}, dimensions={0} | all-to-all | bytes 8192 | tf_op jit(solution)/shard_map/all_to_all | solution.py:1015
  258.9 4.4 all-to-all-start
  264.9 1.6 iota_compare_fusion
  267.3 1.6 fusion.71
  268.9 32.4 %all-to-all-done = bf16[8,128,1536]{2,1,0:T(8,128)(2,1)} async-done(((bf16[8,128,1536]{2,1,0:T(8,128)(2,1)}), bf16[8,128,1536]{2,1,0:T(8,128)(2,1)}, u32[]{:S(2)}, u32[]{:S(2)}) %all-to-all-start) | async-done | bytes 3145760 | tf_op jit(solution)/shard_map/all_to_all | solution.py:1012
  301.3 4.6 %multiply_reduce_fusion = (f32[1536]{0:T(1024)}, f32[256]{0:T(256)S(1)}, f32[256,1536]{1,0:T(8,128)S(1)}) fusion(f32[256,1536]{1,0:T(8,128)S(1)} %get-tuple-element.89, f32[256]{0:T(256)S(1)} %get-tuple-element.85, f32[1536]{0:T(1024)S(1)} %reshape.245, f32[256,1536]{1,0:T(8,128)} %fusion.71, bf16[1024,1536]{1,0:T(8,128)(2,1)} %bitcast.36, ...), kind=kOutput, calls=%fused_computation.40 | convolution fusion | flops 808319232 | bytes 8927232 | tf_op jit(solution)/shard_map/dot_general | solution.py:808
  305.8 1.6 multiply_subtract_fusion
  307.4 3.7 convolution_convert_fusion.3
  311.1 1.4 copy.91
  312.5 4.9 %all-to-all-start.2 = ((bf16[8,128,1536]{2,1,0:T(8,128)(2,1)}), bf16[8,128,1536]{2,1,0:T(8,128)(2,1)}, u32[]{:S(2)}, u32[]{:S(2)}) async-start(bf16[8,128,1536]{2,1,0:T(8,128)(2,1)} %bitcast.186), calls=%async_computation.2 | async-start | bytes 6291456 | tf_op jit(solution)/shard_map/all_to_all | solution.py:1019
  317.5 6.7 %fusion.1 = (f32[8,3,256]{2,1,0:T(4,128)S(1)}, f32[8,256,256,3]{2,1,3,0:T(8,128)}) fusion(f32[8,3,256,256]{2,3,1,0:T(8,128)} %get-tuple-element.87, f32[8,3,256]{2,1,0:T(4,128)S(1)} %get-tuple-element.86, bf16[256,8,64,1]{0,2,3,1:T(8,128)(2,1)} %bitcast.200, bf16[256,8,3,64]{0,3,2,1:T(8,128)(2,1)S(1)} %bitcast.194), kind=kOutput, calls=%fused_computation.5 | convolution fusion | flops 206039040 | bytes 13680640 | tf_op jit(solution)/shard_map/qkgd,skd->kgqs/dot_general | solution.py:1059
  324.2 4.3 fusion.3
  331.9 1.3 slice-done.9
  333.2 3.5 fusion.18
  337.0 5.3 %convolution_convert_fusion.1.grad_b = bf16[1536,1536]{1,0:T(8,128)(2,1)} fusion(bf16[256,1536]{0,1:T(8,128)(2,1)} %bitcast.179, f32[256,1536]{1,0:T(8,128)} %multiply_subtract_fusion), kind=kOutput, calls=%fused_computation.2 | convolution fusion | flops 1210712064 | bytes 7077888 | tf_op jit(solution)/shard_map/dot_general | solution.py:816
  342.3 5.5 %convolution_convert_fusion.grad_a = bf16[1536,2560]{1,0:T(8,128)(2,1)} fusion(bf16[256,2560]{0,1:T(8,128)(2,1)S(1)} %bitcast.183, bf16[256,1536]{1,0:T(8,128)(2,1)S(1)} %copy-done, f32[1536]{0:T(1024)S(1)} %reshape.243, f32[256]{0:T(256)S(1)} %copy-done.22), kind=kOutput, calls=%fused_computation.1 | convolution fusion | flops 2018770944 | bytes 9968640 | tf_op jit(solution)/shard_map/dot_general | solution.py:816
  347.8 3.1 fusion.15
  350.9 4.0 all-to-all-done.2
  354.9 3.3 convolution_multiply_fusion
  358.3 4.0 fusion.10
  362.4 70.9 %shard_map.233 = (f32[192,640]{1,0:T(8,128)S(1)}, f32[192,384]{1,0:T(8,128)S(1)}, f32[8,256]{1,0:T(8,128)S(1)}) custom-call(bf16[1536,2560]{1,0:T(8,128)(2,1)} %convolution_convert_fusion.grad_a, bf16[1536,1536]{1,0:T(8,128)(2,1)S(1)} %bitcast.173, f32[8,4,8,256]{3,2,1,0:T(8,128)S(1)} %select_maximum_fusion.grad_s), custom_call_target="tpu_custom_call" | custom-call | bytes 1000000 | tf_op jit(solution)/shard_map/pallas_call | solution.py:476
  435.8 3.5 fusion.35
  (155 shorter events, 24.9 us)
Async XLA Ops:
  7.2 164.6 %all-gather.2.cloned.1.call-start = ((), (), s32[]{:S(2)}) async-start(), calls=%async_computation.4 | async-start | bytes 7864320 | tf_op jit(solution)/shard_map/all_gather | solution.py:962
  8.6 2.7 copy-start.14
  8.6 2.7 copy-start.17
  8.6 2.7 copy-start.18
  51.3 57.5 %copy-start = (bf16[256,1536]{1,0:T(8,128)(2,1)S(1)}, bf16[256,1536]{1,0:T(8,128)(2,1)}, u32[]{:S(2)}) copy-start(bf16[256,1536]{1,0:T(8,128)(2,1)} %param.14) | copy-start | bytes 2359300
  51.4 384.4 %reduce-scatter.2.cloned.1.call-start = ((), (), s32[]{:S(2)}) async-start(), calls=%async_computation.5 | async-start | bytes 7864320 | tf_op jit(solution)/shard_map/reduce_scatter | solution.py:1011
  109.6 6.6 %copy-start.21 = (f32[256]{0:T(256)}, f32[256]{0:T(256)S(1)}, u32[]{:S(2)}) copy-start(f32[256]{0:T(256)S(1)} %get-tuple-element.83) | copy-start | bytes 3076
  120.3 3.2 copy-start.23
  122.1 6.2 %copy-start.6 = (bf16[256,4,384]{0,2,1:T(8,128)(2,1)}, bf16[256,4,384]{0,2,1:T(8,128)(2,1)S(1)}, u32[]{:S(2)}) copy-start(bf16[256,4,384]{0,2,1:T(8,128)(2,1)S(1)} %copy.83) | copy-start | bytes 2359300
  122.2 6.0 %copy-start.13 = (bf16[256,4,128]{0,2,1:T(8,128)(2,1)}, bf16[256,4,128]{0,2,1:T(8,128)(2,1)S(1)}, u32[]{:S(2)}) copy-start(bf16[256,4,128]{0,2,1:T(8,128)(2,1)S(1)} %copy.84) | copy-start | bytes 786436
  128.2 4.0 slice-start.2
  128.2 4.1 slice-start.3
  258.9 42.3 %all-to-all-start = ((bf16[8,128,1536]{2,1,0:T(8,128)(2,1)}), bf16[8,128,1536]{2,1,0:T(8,128)(2,1)}, u32[]{:S(2)}, u32[]{:S(2)}) async-start(bf16[8,128,1536]{2,1,0:T(8,128)(2,1)} %bitcast.187), calls=%async_computation | async-start | bytes 6291456 | tf_op jit(solution)/shard_map/all_to_all | solution.py:1012
  263.4 3.6 copy-start.2
  267.3 40.1 %slice-start.4 = ((s8[4718592]{0:T(1024)(128)(4,1)}), s8[524288]{0:T(1024)(128)(4,1)S(1)}, s32[]{:S(2)}) async-start(s8[4718592]{0:T(1024)(128)(4,1)} %bitcast.176), calls=%async_computation.10 | async-start | bytes 1048576
  301.2 4.6 %copy-start.8 = (bf16[256,1536]{1,0:T(8,128)(2,1)S(1)}, bf16[256,1536]{1,0:T(8,128)(2,1)}, u32[]{:S(2)}) copy-start(bf16[256,1536]{1,0:T(8,128)(2,1)} %own_c.1) | copy-start | bytes 2359300
  301.2 4.6 %copy-start.25 = (f32[256]{0:T(256)S(1)}, f32[256]{0:T(256)}, u32[]{:S(2)}) copy-start(f32[256]{0:T(256)} %get-tuple-element.84) | copy-start | bytes 3076
  301.2 6.2 %slice-start.5 = ((s8[4718592]{0:T(1024)(128)(4,1)}), s8[4194304]{0:T(1024)(128)(4,1)S(1)}, s32[]{:S(2)}) async-start(s8[4718592]{0:T(1024)(128)(4,1)} %bitcast.176), calls=%async_computation.11 | async-start | bytes 8388608
  312.5 42.4 %all-to-all-start.2 = ((bf16[8,128,1536]{2,1,0:T(8,128)(2,1)}), bf16[8,128,1536]{2,1,0:T(8,128)(2,1)}, u32[]{:S(2)}, u32[]{:S(2)}) async-start(bf16[8,128,1536]{2,1,0:T(8,128)(2,1)} %bitcast.186), calls=%async_computation.2 | async-start | bytes 6291456 | tf_op jit(solution)/shard_map/all_to_all | solution.py:1019
  317.4 6.7 %slice-start.6 = ((s8[6291456]{0:T(1024)(128)(4,1)}), s8[4194304]{0:T(1024)(128)(4,1)S(1)}, s32[]{:S(2)}) async-start(s8[6291456]{0:T(1024)(128)(4,1)} %bitcast.180), calls=%async_computation.12 | async-start | bytes 8388608
  317.5 6.7 %slice-start.7 = ((s8[6291456]{0:T(1024)(128)(4,1)}), s8[2097152]{0:T(1024)(128)(4,1)S(1)}, s32[]{:S(2)}) async-start(s8[6291456]{0:T(1024)(128)(4,1)} %bitcast.180), calls=%async_computation.13 | async-start | bytes 4194304
  331.9 4.8 %copy-start.4 = (bf16[256,4,640]{0,2,1:T(8,128)(2,1)}, bf16[256,4,640]{0,2,1:T(8,128)(2,1)S(1)}, u32[]{:S(2)}) copy-start(bf16[256,4,640]{0,2,1:T(8,128)(2,1)S(1)} %pad_maximum_fusion.1) | copy-start | bytes 3932164
  333.2 3.6 copy-start.19
  337.0 5.3 %copy-start.5 = (bf16[256,4,640]{0,2,1:T(8,128)(2,1)S(1)}, bf16[256,4,640]{0,2,1:T(8,128)(2,1)}, u32[]{:S(2)}) copy-start(bf16[256,4,640]{0,2,1:T(8,128)(2,1)} %copy-done.4) | copy-start | bytes 3932164
  342.3 5.5 %copy-start.10 = (f32[256,1536]{1,0:T(8,128)S(1)}, f32[256,1536]{1,0:T(8,128)}, u32[]{:S(2)}) copy-start(f32[256,1536]{1,0:T(8,128)} %get-tuple-element.93) | copy-start | bytes 4718596
  342.3 5.5 %copy-start.24 = (f32[256]{0:T(256)S(1)}, f32[256]{0:T(256)}, u32[]{:S(2)}) copy-start(f32[256]{0:T(256)} %get-tuple-element.82) | copy-start | bytes 3076
  347.8 7.1 %copy-start.26 = (f32[256,1]{0,1:T(1,128)S(1)}, f32[256,1]{0,1:T(1,128)}, u32[]{:S(2)}) copy-start(f32[256,1]{0,1:T(1,128)} %get-tuple-element.79) | copy-start | bytes 3076
  347.8 14.5 %slice-start = ((s8[4718592]{0:T(1024)(128)(4,1)}), s8[524288]{0:T(1024)(128)(4,1)S(1)}, s32[]{:S(2)}) async-start(s8[4718592]{0:T(1024)(128)(4,1)} %bitcast.172), calls=%async_computation.6 | async-start | bytes 1048576
  354.9 3.4 copy-start.11
  354.9 3.4 copy-start.20
  354.9 7.4 %slice-start.1 = ((s8[4718592]{0:T(1024)(128)(4,1)}), s8[4194304]{0:T(1024)(128)(4,1)S(1)}, s32[]{:S(2)}) async-start(s8[4718592]{0:T(1024)(128)(4,1)} %bitcast.172), calls=%async_computation.7 | async-start | bytes 8388608
  435.8 4.3 copy-start.9
  (9 other events, 13.8 us)
Sparse Core Ops, SparseCore 0:
  51.5 113.9 all-gather.1
  250.1 109.6 reduce-scatter.1

commit v4 on v3

--- a/solution.py
+++ b/solution.py
@@ -54,6 +54,13 @@
     for c in (2, 1, 0):
         out = jnp.where(col == c, table[c][k], out)
     return out
+
+
+def unit_at(col, k):
+    end = (col == 0) | (col == 3)
+    ends = jnp.where(col == 0, k, 3 - k)
+    middle = jnp.where(k == 0, col, jnp.where(k == 3, jnp.where(col == 1, 3, 0), jnp.where(col == 1, 2 * k - 2, 5 - 2 * k)))
+    return jnp.where(end, ends, middle)
 
 
 X, Y, SIB = 2, 4, 1
@@ -320,194 +327,17 @@
 
 
 def add_into(target, term):
-    target[...] = (target[...].astype(jnp.float32) + term[...].astype(jnp.float32)).astype(target.dtype)
-
-
-def reduce_kernel(grad_a, grad_b, grad_s, sum_a, sum_b, sum_s,
-                  own, rec_sib, rec_one, rec_two, rec_z, s_own, s_rec, s_mid, s_zrec,
-                  lss, lrs, ss1, rs1, ss2, rs2, zss, zrs, lo, s_ss, s_rs, sz_ss, sz_rs):
-    row, col = lax.axis_index("row"), lax.axis_index("col")
-    core = row % 2
-    chip = row // 2
-    cy, cx = chip // 2, chip % 2
-    block, width = own.shape[2], own.shape[3]
-    width_a = sum_a.shape[1]
-    width_b = width - width_a
-    cut = block // 2
-    greet(range(1, 8), (1, 2, 3))
-    sib = {"row": row_at(row, SIB)}
-    to_x, to_y = {"row": row_at(row, X)}, {"row": row_at(row, Y)}
-
-    def parts(c, q, of_core):
-        rows = pl.ds(pl.multiple_of((q * 2 + of_core) * block, 16), block)
-        return (
-            grad_a.at[rows, pl.ds(pl.multiple_of(c * width_a, 128), width_a)],
-            grad_b.at[rows, pl.ds(pl.multiple_of(c * width_b, 128), width_b)],
-        )
-
-    for i in range(1, 8):
-        there = row_at(row, i)
-        remote(grad_s.at[there], s_rec.at[i - 1], s_ss.at[i - 1], s_rs.at[i - 1], {"row": there}).start()
-    def start_first(k, carry):
-        c = (col + 1 + k) % 4
-        for q in range(4):
-            pa, pb = parts(c, q, 1 - core)
-            remote(pa, rec_sib.at[c, q, :, pl.ds(0, width_a)], ss1.at[c, q, 0], rs1.at[c, q, 0], sib).start()
-            remote(pb, rec_sib.at[c, q, :, pl.ds(width_a, width_b)], ss1.at[c, q, 1], rs1.at[c, q, 1], sib).start()
-            pa, pb = parts(c, q, core)
-            pltpu.make_async_copy(pa, own.at[c, q, :, pl.ds(0, width_a)], lss.at[c, q, 0]).start()
-            pltpu.make_async_copy(pb, own.at[c, q, :, pl.ds(width_a, width_b)], lss.at[c, q, 1]).start()
-        return carry
-    lax.fori_loop(0, 4, start_first, 0)
-    own_small = pltpu.make_async_copy(grad_s.at[row], s_own, lo.at[0])
-    own_small.start()
-
-    def chip_sum(c):
-        for q in range(4):
-            pa, pb = parts(c, q, core)
-            for i, (p, off, w) in enumerate(((pa, 0, width_a), (pb, width_a, width_b))):
-                pltpu.make_async_copy(p, own.at[c, q, :, pl.ds(off, w)], lss.at[c, q, i]).wait()
-                remote(p, rec_sib.at[c, q, :, pl.ds(off, w)], ss1.at[c, q, i], rs1.at[c, q, i], sib).wait_recv()
-            add_into(own.at[c, q], rec_sib.at[c, q])
-
-    top, low = pl.ds(0, cut), pl.ds(cut, block - cut)
-
-    def one(c):
-        for j in range(2):
-            yield remote(own.at[c, j * 2 + 1 - cx, top, :], rec_one.at[c, 0, j], ss2.at[c, 0, j], rs2.at[c, 0, j], to_x)
-            yield remote(own.at[c, (1 - cy) * 2 + j, low, :], rec_one.at[c, 1, j], ss2.at[c, 1, j], rs2.at[c, 1, j], to_y)
-
-    def one_sum(c):
-        for copy in one(c):
-            copy.wait_recv()
-        for j in range(2):
-            add_into(own.at[c, j * 2 + cx, top, :], rec_one.at[c, 0, j])
-            add_into(own.at[c, cy * 2 + j, low, :], rec_one.at[c, 1, j])
-
-    def two(c):
-        yield remote(own.at[c, (1 - cy) * 2 + cx, top, :], rec_two.at[c, 0], ss2.at[c, 0, 2], rs2.at[c, 0, 2], to_y)
-        yield remote(own.at[c, cy * 2 + 1 - cx, low, :], rec_two.at[c, 1], ss2.at[c, 1, 2], rs2.at[c, 1, 2], to_x)
-
-    def two_sum(c):
-        for copy in two(c):
-            copy.wait_recv()
-        add_into(own.at[c, chip, top, :], rec_two.at[c, 0])
-        add_into(own.at[c, chip, low, :], rec_two.at[c, 1])
-
-    def column(step):
-        there = (col + step) % 4
-        return remote(own.at[there, chip], rec_z.at[step - 1], zss.at[step - 1], zrs.at[step - 1], {"col": there})
-
-    def nth(k):
-        return (col + 1 + k) % 4
-
-    def stages(k, carry):
-        @pl.when(k < 4)
-        def _():
-            chip_sum(nth(k))
-            for copy in one(nth(k)):
-                copy.start()
-        @pl.when((k >= 1) & (k < 5))
-        def _():
-            one_sum(nth(k - 1))
-            for copy in two(nth(k - 1)):
-                copy.start()
-        @pl.when(k >= 2)
-        def _():
-            two_sum(nth(k - 2))
-        for step in (1, 2, 3):
-            @pl.when(k == step + 1)
-            def _():
-                column(step).start()
-        return carry
-    lax.fori_loop(0, 6, stages, 0)
-
-    own_small.wait()
-    total = s_own[...]
-    for i in range(1, 8):
-        there = row_at(row, i)
-        remote(grad_s.at[there], s_rec.at[i - 1], s_ss.at[i - 1], s_rs.at[i - 1], {"row": there}).wait()
-        total = total + s_rec[i - 1]
-    s_mid[...] = total
-
-    def small(step):
-        there = (col + step) % 4
-        return remote(s_mid.at[there], s_zrec.at[step - 1], sz_ss.at[step - 1], sz_rs.at[step - 1], {"col": there})
-
-    for step in (1, 2, 3):
-        small(step).start()
-    for step in (1, 2, 3):
-        small(step).wait()
-    sum_s[...] = s_mid[col] + s_zrec[0] + s_zrec[1] + s_zrec[2]
-    for step in (1, 2, 3):
-        column(step).wait_recv()
-    for start in range(0, block, 32):
-        rows = pl.ds(start, 32)
-        total = own[col, chip, rows, :].astype(jnp.float32)
-        for step in range(3):
-            total = total + rec_z[step, rows, :].astype(jnp.float32)
-        sum_a[rows, :] = total[:, :width_a]
-        sum_b[rows, :] = total[:, width_a:]
-    for step in (1, 2, 3):
-        column(step).wait_send()
-
-    def sent(c, carry):
-        for q in range(4):
-            pa, pb = parts(c, q, 1 - core)
-            remote(pa, rec_sib.at[c, q, :, pl.ds(0, width_a)], ss1.at[c, q, 0], rs1.at[c, q, 0], sib).wait_send()
-            remote(pb, rec_sib.at[c, q, :, pl.ds(width_a, width_b)], ss1.at[c, q, 1], rs1.at[c, q, 1], sib).wait_send()
-        for copy in one(c):
-            copy.wait_send()
-        for copy in two(c):
-            copy.wait_send()
-        return carry
-    lax.fori_loop(0, 4, sent, 0)
-
-
-def reduce_attention(grad_a, grad_b, grad_s):
-    sems = pltpu.SemaphoreType.DMA
-    block = grad_a.shape[0] // 8
-    width_a, width_b = grad_a.shape[1] // 4, grad_b.shape[1] // 4
-    width = width_a + width_b
-    cut = block // 2
-    low = grad_a.dtype
-    vm = pl.BlockSpec(memory_space=pltpu.VMEM)
-    small = grad_s.shape[1:]
-    return pl.pallas_call(
-        reduce_kernel,
-        out_shape=(
-            jax.ShapeDtypeStruct((block, width_a), jnp.float32),
-            jax.ShapeDtypeStruct((block, width_b), jnp.float32),
-            jax.ShapeDtypeStruct(small[1:], jnp.float32),
-        ),
-        in_specs=[ANY] * 3,
-        out_specs=(vm,) * 3,
-        scratch_shapes=[
-            pltpu.VMEM((4, 4, block, width), low),
-            pltpu.VMEM((4, 4, block, width), low),
-            pltpu.VMEM((4, 2, 2, cut, width), low),
-            pltpu.VMEM((4, 2, cut, width), low),
-            pltpu.VMEM((3, block, width), low),
-            pltpu.VMEM(small, jnp.float32),
-            pltpu.VMEM((7,) + small, jnp.float32),
-            pltpu.VMEM(small, jnp.float32),
-            pltpu.VMEM((3,) + small[1:], jnp.float32),
-            sems((4, 4, 2)), sems((1,)),
-            sems((4, 4, 2)), sems((4, 4, 2)),
-            sems((4, 2, 3)), sems((4, 2, 3)),
-            sems((3,)), sems((3,)), sems((1,)),
-            sems((7,)), sems((7,)), sems((3,)), sems((3,)),
-        ],
-        compiler_params=pltpu.CompilerParams(
-            collective_id=2, has_side_effects=True, vmem_limit_bytes=48 * 2**20
-        ),
-        cost_estimate=pl.CostEstimate(flops=0, bytes_accessed=1_000_000, transcendentals=0),
-    )(grad_a, grad_b, grad_s)
+    def body(i, carry):
+        rows = pl.ds(pl.multiple_of(i * 32, 32), 32)
+        total = target[rows, :].astype(jnp.float32) + term[rows, :].astype(jnp.float32)
+        target[rows, :] = total.astype(target.dtype)
+        return carry
+    lax.fori_loop(0, target.shape[0] // 32, body, 0)
 
 
 def expert_kernel(key, mine, normed_hbm, upstream_hbm, gu_hbm, own_down,
-                  in_ref, prod_ref, gate_grad_ref, grad_gu, sum_down,
-                  x_t, ups, gu, down, act, silu, slope, both, gd, rec_right, rec_left, stage, gate,
+                  in_ref, prod_ref, gate_grad_out, grad_gu, sum_down,
+                  gate_grad_ref, x_t, ups, gu, down, act, silu, slope, both, gd, rec_right, rec_left, stage, gate,
                   load_sem, src_sem, stage_sem, zss, zrs, rss, rrs):
     col = lax.axis_index("col")
     sources, _, length = key.shape
@@ -567,14 +397,12 @@
         return remote(target, target, rss.at[1, d], rrs.at[1, d], left_dev)
 
     def from_end(d):
-        if d > 0:
-            @pl.when(col == 0)
-            def _():
-                remote(gd.at[d], rec_right.at[d - 1], rss.at[0, d - 1], rrs.at[0, d - 1], right_dev).start()
-        if d < 3:
-            @pl.when(col == 3)
-            def _():
-                remote(gd.at[d], rec_left.at[d], rss.at[1, d], rrs.at[1, d], left_dev).start()
+        @pl.when((col == 0) & (d > 0))
+        def _():
+            remote(gd.at[d], rec_right.at[d - 1], rss.at[0, d - 1], rrs.at[0, d - 1], right_dev).start()
+        @pl.when((col == 3) & (d < 3))
+        def _():
+            remote(gd.at[d], rec_left.at[d], rss.at[1, d], rrs.at[1, d], left_dev).start()
 
     def add_rows(target, term):
         def body(i, carry):
@@ -584,19 +412,15 @@
             return carry
         lax.fori_loop(0, width // 64, body, 0)
 
-    def hop_right(at, d):
-        @pl.when(col == at)
-        def _():
-            to_right(d).wait_recv()
-            add_rows(rec_right.at[d - 1], gd.at[d])
-            to_right(d).start()
-
-    def hop_left(at, d):
-        @pl.when(col == at)
-        def _():
-            to_left(d).wait_recv()
-            add_rows(rec_left.at[d], gd.at[d])
-            to_left(d).start()
+    def hop_right(d):
+        to_right(d).wait_recv()
+        add_rows(rec_right.at[d - 1], gd.at[d])
+        to_right(d).start()
+
+    def hop_left(d):
+        to_left(d).wait_recv()
+        add_rows(rec_left.at[d], gd.at[d])
+        to_left(d).start()
 
     def select(s, carry):
         slot = s % 2
@@ -620,8 +444,8 @@
     load_gu.wait()
 
     def forward(c):
-        first = pl.ds(c * width, width)
-        second = pl.ds(units + c * width, width)
+        first = pl.ds(pl.multiple_of(c * width, width), width)
+        second = pl.ds(pl.multiple_of(units + c * width, width), width)
         def body(m, carry):
             rows = pl.ds(pl.multiple_of(m * chunk, chunk), chunk)
             gate_pre = dot(x[rows, :], gu[:, first])
@@ -637,22 +461,17 @@
         lax.fori_loop(0, slots // chunk, body, 0)
         gd[c] = t_dot(both[:, first], ups[...]).astype(gd.dtype)
 
-    forward(3)
-    from_end(3)
-    forward(0)
-    from_end(0)
-    ag_step(1)
-    forward(2)
-    forward(1)
-    for d in (2, 1):
-        if d > 0:
-            @pl.when(col == 0)
-            def _():
-                remote(gd.at[d], rec_right.at[d - 1], rss.at[0, d - 1], rrs.at[0, d - 1], right_dev).start()
-    for d in (1, 2):
-        @pl.when(col == 3)
+    def forward_step(i, carry):
+        c = jnp.where(i < 2, 3 - 3 * i, 4 - i)
+        forward(c)
+        pl.when((i < 2) | (col == 0))(lambda: from_end(c))
+        pl.when(i == 1)(lambda: ag_step(1))
+        @pl.when((i == 3) & (col == 3))
         def _():
-            remote(gd.at[d], rec_left.at[d], rss.at[1, d], rrs.at[1, d], left_dev).start()
+            from_end(1)
+            from_end(2)
+        return carry
+    lax.fori_loop(0, 4, forward_step, 0)
     load_down.wait()
 
     def turn(m, carry):
@@ -671,7 +490,7 @@
             )
 
     def backward(k):
-        c = unit_order(col, k)
+        c = unit_at(col, k)
         first = pl.ds(pl.multiple_of(c * width, width), width)
         second = pl.ds(pl.multiple_of(units + c * width, width), width)
         def body(m, carry):
@@ -685,8 +504,9 @@
             return carry
         lax.fori_loop(0, slots // chunk, body, 0)
         slot = k % 2
-        if k >= 2:
-            for copy in out_stage(unit_order(col, k - 2), slot):
+        @pl.when(k >= 2)
+        def _():
+            for copy in out_stage(unit_at(col, k - 2), slot):
                 copy.wait()
         def grads(i, carry):
             rows = pl.ds(pl.multiple_of(i * chunk, chunk), chunk)
@@ -697,18 +517,22 @@
         for copy in out_stage(c, slot):
             copy.start()
 
-    backward(0)
-    ag_step(2)
-    hop_right(1, 3)
-    hop_left(2, 0)
-    backward(1)
-    backward(2)
-    ag_step(3)
-    hop_right(1, 2)
-    hop_right(2, 3)
-    hop_left(2, 1)
-    hop_left(1, 0)
-    backward(3)
+    def backward_step(k, carry):
+        backward(k)
+        pl.when(k == 0)(lambda: ag_step(2))
+        pl.when((k == 0) & (col == 1))(lambda: hop_right(3))
+        pl.when((k == 0) & (col == 2))(lambda: hop_left(0))
+        pl.when(k == 2)(lambda: ag_step(3))
+        @pl.when((k == 2) & (col == 1))
+        def _():
+            hop_right(2)
+            hop_left(0)
+        @pl.when((k == 2) & (col == 2))
+        def _():
+            hop_right(3)
+            hop_left(1)
+        return carry
+    lax.fori_loop(0, 4, backward_step, 0)
 
     def inputs(m, carry):
         rows = pl.ds(pl.multiple_of(m * chunk, chunk), chunk)
@@ -725,36 +549,38 @@
         return carry
     lax.fori_loop(0, slots // chunk, outputs, 0)
 
+    turned = gate_grad_ref[...].T
+    for s in range(sources):
+        gate_grad_out[s] = turned[0:1, s * capacity : (s + 1) * capacity]
     for k in (2, 3):
-        for copy in out_stage(unit_order(col, k), k % 2):
+        for copy in out_stage(unit_at(col, k), k % 2):
             copy.wait()
-    for d in range(4):
-        @pl.when(col == d)
+    pl.when(col > 0)(lambda: to_right(col).wait_recv())
+    pl.when(col < 3)(lambda: to_left(col).wait_recv())
+
+    def to_sum(i, carry):
+        rows = pl.ds(pl.multiple_of(i * 64, 64), 64)
+        sum_down[rows, :] = gd[col, rows, :].astype(jnp.float32)
+        @pl.when(col > 0)
         def _():
-            if d > 0:
-                to_right(d).wait_recv()
-            if d < 3:
-                to_left(d).wait_recv()
-            def body(i, carry):
-                rows = pl.ds(pl.multiple_of(i * 64, 64), 64)
-                total = gd[d, rows, :].astype(jnp.float32)
-                if d > 0:
-                    total = total + rec_right[d - 1, rows, :].astype(jnp.float32)
-                if d < 3:
-                    total = total + rec_left[d, rows, :].astype(jnp.float32)
-                sum_down[rows, :] = total
-                return carry
-            lax.fori_loop(0, width // 64, body, 0)
-            for e in range(d + 1, 4):
-                to_right(e).wait_send()
-            for e in range(d):
-                to_left(e).wait_send()
-            if d < 3:
-                for e in range(d + 1):
-                    remote(down.at[e], down.at[e], zss.at[e, 0], zrs.at[e], right_dev).wait_send()
-            if d > 0:
-                for e in range(d, 4):
-                    remote(down.at[e], down.at[e], zss.at[e, 1], zrs.at[e], left_dev).wait_send()
+            sum_down[rows, :] += rec_right[jnp.maximum(col - 1, 0), rows, :].astype(jnp.float32)
+        @pl.when(col < 3)
+        def _():
+            sum_down[rows, :] += rec_left[jnp.minimum(col, 2), rows, :].astype(jnp.float32)
+        return carry
+    lax.fori_loop(0, width // 64, to_sum, 0)
+
+    def sent(e, carry):
+        pl.when(e > col)(lambda: to_right(e).wait_send())
+        pl.when(e < col)(lambda: to_left(e).wait_send())
+        @pl.when((col < 3) & (e <= col))
+        def _():
+            remote(down.at[e], down.at[e], zss.at[e, 0], zrs.at[e], right_dev).wait_send()
+        @pl.when((col > 0) & (e >= col))
+        def _():
+            remote(down.at[e], down.at[e], zss.at[e, 1], zrs.at[e], left_dev).wait_send()
+        return carry
+    lax.fori_loop(0, 4, sent, 0)
 
 
 def run_expert(key, mine, normed, upstream, full_gu, own_down):
@@ -770,13 +596,14 @@
         out_shape=(
             jax.ShapeDtypeStruct((slots, model), low),
             jax.ShapeDtypeStruct((slots, model), low),
-            jax.ShapeDtypeStruct((slots, 128), f32),
+            jax.ShapeDtypeStruct((sources, 1, slots // sources), f32),
             jax.ShapeDtypeStruct((model, 2 * units), low),
             jax.ShapeDtypeStruct((width, model), f32),
         ),
         in_specs=[vm, vm, ANY, ANY, ANY, ANY],
         out_specs=(vm, vm, vm, ANY, vm),
         scratch_shapes=[
+            pltpu.VMEM((slots, 128), f32),
             pltpu.VMEM((model, slots), low),
             pltpu.VMEM((slots, model), low),
             pltpu.VMEM((model, 2 * units), low),
@@ -800,6 +627,402 @@
     )(key.reshape(sources, 1, length), mine.reshape(sources, 1, length), normed, upstream, full_gu, own_down)
 
 
+def backward_kernel(slot_of, gates, ids, router_p, gain_one, gain_two, lse, seg_row, seg_col,
+                    gate_grad, in_grad, produced, hidden_hbm, tokens_hbm, cot_hbm, normed_hbm, attended_hbm,
+                    two_hbm, qkv_hbm, full_a_hbm, full_out_hbm,
+                    out_ref, d_tokens, sum_a, sum_b, sum_s,
+                    rec_in, rec_gate, rec_prod, hidden, tokens, cot, two, qkv, full_a, full_out,
+                    n_t, a_t, branch, bias, out_rows, grad_c, qg, lgs, small,
+                    own, sib_out, rec_sib, rec_one, rec_two, rec_z, s_rec, s_mid, s_zrec,
+                    load, in_ss, in_rs, g_ss, g_rs, pr_ss, pr_rs, loc,
+                    ss1, rs1, ss2, rs2, zss, zrs, s_ss, s_rs, sz_ss, sz_rs):
+    row, col = lax.axis_index("row"), lax.axis_index("col")
+    core = row % 2
+    chip = row // 2
+    cy, cx = chip // 2, chip % 2
+    length, model = hidden.shape
+    capacity = rec_in.shape[0] // 8
+    block = own.shape[2]
+    width_a, width_b = sum_a.shape[1], sum_b.shape[1]
+    cut = block // 2
+    half = length // 2
+    f32, low = jnp.float32, branch.dtype
+    sib = {"row": row_at(row, SIB)}
+    to_x, to_y = {"row": row_at(row, X)}, {"row": row_at(row, Y)}
+
+    def each_flip(function):
+        def body(i, carry):
+            function(7 - i)
+            return carry
+        lax.fori_loop(0, 7, body, 0)
+
+    def block_of(r):
+        return pl.ds(pl.multiple_of(r * capacity, 16), capacity)
+
+    own_in = pltpu.make_async_copy(in_grad.at[block_of(row), :], rec_in.at[block_of(row), :], loc.at[0])
+    own_gate = pltpu.make_async_copy(gate_grad.at[row], rec_gate.at[row], loc.at[1])
+    own_prod = pltpu.make_async_copy(produced.at[block_of(row), :], rec_prod.at[block_of(row), :], loc.at[2])
+    loads = [
+        pltpu.make_async_copy(source, target, load.at[i])
+        for i, (source, target) in enumerate((
+            (normed_hbm, branch), (attended_hbm, out_ref), (hidden_hbm, hidden), (cot_hbm, cot), (two_hbm, two),
+            (qkv_hbm, qkv), (tokens_hbm, tokens), (full_out_hbm, full_out), (full_a_hbm, full_a),
+        ))
+    ]
+    greet(range(1, 8), (1, 2, 3))
+
+    def back(flip):
+        there = row_at(row, flip)
+        device = {"row": there}
+        return (
+            remote(in_grad.at[block_of(there), :], rec_in.at[block_of(row), :],
+                   in_ss.at[flip - 1], in_rs.at[flip - 1], device),
+            remote(gate_grad.at[there], rec_gate.at[row], g_ss.at[flip - 1], g_rs.at[flip - 1], device),
+        )
+
+    def back_prod(flip):
+        there = row_at(row, flip)
+        return remote(produced.at[block_of(there), :], rec_prod.at[block_of(row), :],
+                      pr_ss.at[flip - 1], pr_rs.at[flip - 1], {"row": there})
+
+    each_flip(lambda flip: [copy.start() for copy in back(flip)])
+    for copy in (own_in, own_gate, own_prod):
+        copy.start()
+    for copy in loads:
+        copy.start()
+    loads[0].wait()
+    n_t[...] = branch[...].T
+    loads[1].wait()
+    a_t[...] = out_ref[...].T
+    key_pos = lax.broadcasted_iota(jnp.int32, (length, length), 0)
+    query_pos = lax.broadcasted_iota(jnp.int32, (length, length), 1)
+    allowed = (key_pos <= query_pos) & (seg_col[...] == seg_row[...])
+    bias[...] = jnp.where(allowed, 0.0, NEGATIVE)
+    small[...] = jnp.zeros_like(small)
+    for copy in loads[2:]:
+        copy.wait()
+    for copy in (own_in, own_gate):
+        copy.wait()
+    each_flip(lambda flip: [copy.wait_recv() for copy in back(flip)])
+    each_flip(lambda flip: back_prod(flip).start())
+
+    all_gate = jnp.concatenate([rec_gate[e] for e in range(8)], axis=1)
+    wide = rec_in.shape[0]
+    lanes = lgs.shape[1]
+
+    def at_slot(rows, k):
+        return slot_of[rows, k : k + 1] == lax.broadcasted_iota(jnp.int32, (half, wide), 1)
+
+    def to_hidden(m, carry):
+        rows = pl.ds(pl.multiple_of(m * half, half), half)
+        first, second = at_slot(rows, 0), at_slot(rows, 1)
+        picked = jnp.where(first | second, 1.0, 0.0).astype(low)
+        two_grad = dot(picked, rec_in[...])
+        grad_0 = jnp.sum(jnp.where(first, all_gate, 0.0), axis=1, keepdims=True)
+        grad_1 = jnp.sum(jnp.where(second, all_gate, 0.0), axis=1, keepdims=True)
+        gate_0, gate_1 = gates[rows, 0:1], gates[rows, 1:2]
+        mean = gate_0 * grad_0 + gate_1 * grad_1
+        lane = lax.broadcasted_iota(jnp.int32, (half, lanes), 1)
+        logit_grad = jnp.where(lane == ids[rows, 0:1], gate_0 * (grad_0 - mean), 0.0)
+        logit_grad = logit_grad + jnp.where(lane == ids[rows, 1:2], gate_1 * (grad_1 - mean), 0.0)
+        logit_grad = logit_grad.astype(low)
+        lgs[rows, :] = logit_grad
+        two_grad = two_grad + dot_t(logit_grad, router_p[...])
+        h = hidden[rows, :]
+        factor = lax.rsqrt(jnp.mean(h * h, axis=1, keepdims=True) + EPSILON)
+        small[9:10, :] += jnp.sum(two_grad * h * factor, axis=0, keepdims=True)
+        scaled = two_grad * gain_two[...]
+        inner = jnp.mean(scaled * h, axis=1, keepdims=True)
+        grad = cot[rows, :].astype(f32) + factor * scaled - h * (factor * factor * factor * inner)
+        d_tokens[rows, :] = grad
+        branch[rows, :] = grad.astype(low)
+        return carry
+    lax.fori_loop(0, 2, to_hidden, 0)
+    small[0:8, :] = t_dot(lgs[...], two[...])[0:8, :]
+
+    def nth(k):
+        return (col + 1 + k) % 4
+
+    lanes_of = {"a": pl.ds(0, width_a), "b": pl.ds(width_a, width_b)}
+    part_at = {"a": 0, "b": 1}
+
+    def to_sibling(part, c, q):
+        view = lanes_of[part]
+        i = part_at[part]
+        return remote(sib_out.at[c, q, :, view], rec_sib.at[c, q, :, view], ss1.at[c, q, i], rs1.at[c, q, i], sib)
+
+    def weight_grads(part, c, left, right):
+        view = lanes_of[part]
+        def body(q, carry):
+            theirs = pl.ds(pl.multiple_of((q * 2 + 1 - core) * block, 16), block)
+            sib_out[c, q, :, view] = dot(left[theirs, :], right()).astype(low)
+            to_sibling(part, c, q).start()
+            mine = pl.ds(pl.multiple_of((q * 2 + core) * block, 16), block)
+            own[c, q, :, view] = dot(left[mine, :], right()).astype(low)
+            return carry
+        lax.fori_loop(0, 4, body, 0)
+
+    def cols_b(c):
+        return pl.ds(pl.multiple_of(c * width_b, 128), width_b)
+
+    def attend_back(c):
+        span_c = width_b // QUERY_PER_KEY
+        for i in range(QUERY_PER_KEY):
+            for u in range(2):
+                rows = pl.ds(pl.multiple_of(c * width_b + (u * QUERY_PER_KEY + i) * HEAD_SIZE, HEAD_SIZE), HEAD_SIZE)
+                out_rows[(2 * i + u) * HEAD_SIZE : (2 * i + u + 1) * HEAD_SIZE, :] = full_out[rows, :]
+        grad_c[...] = dot_t(branch[...], out_rows[...]).astype(low)
+        at_c = pl.multiple_of(c * width_a, 128)
+        key = qkv[:, pl.ds(at_c + width_b, span_c)]
+        value = qkv[:, pl.ds(at_c + width_b + span_c, span_c)]
+        first = lax.broadcasted_iota(jnp.int32, (length, span_c), 1) < HEAD_SIZE
+        none = jnp.zeros_like(key)
+        keys = (jnp.where(first, key, none), jnp.where(first, none, key))
+        values = (jnp.where(first, value, none), jnp.where(first, none, value))
+        scale = HEAD_SIZE ** (-0.5)
+        key_grads = [jnp.zeros((length, span_c), f32) for _ in range(2)]
+        value_grads = [jnp.zeros((length, span_c), f32) for _ in range(2)]
+        for i in range(QUERY_PER_KEY):
+            q_i = qkv[:, pl.ds(at_c + i * span_c, span_c)]
+            g_i = grad_c[:, i * span_c : (i + 1) * span_c]
+            q_grad = jnp.zeros((length, span_c), f32)
+            for u in range(2):
+                log_total = lse[c * 2 + u, :, i * length : (i + 1) * length]
+                probs = jnp.exp(dot_t(keys[u], q_i) * scale + bias[...] - log_total)
+                prob_grad = dot_t(values[u], g_i)
+                delta = jnp.sum(probs * prob_grad, axis=0, keepdims=True)
+                score_grad = (probs * (prob_grad - delta)).astype(low)
+                value_grads[u] += dot(probs.astype(low), g_i)
+                key_grads[u] += dot(score_grad, q_i)
+                q_grad += t_dot(score_grad, keys[u])
+            qg[c, :, i * span_c : (i + 1) * span_c] = (q_grad * scale).astype(low)
+        key_grad = jnp.where(first, key_grads[0], key_grads[1]) * scale
+        qg[c, :, width_b : width_b + span_c] = key_grad.astype(low)
+        qg[c, :, width_b + span_c : width_a] = jnp.where(first, value_grads[0], value_grads[1]).astype(low)
+
+    top, bottom = pl.ds(0, cut), pl.ds(cut, block - cut)
+
+    def one(part, c):
+        view, i = lanes_of[part], part_at[part]
+        for j in range(2):
+            yield remote(own.at[c, j * 2 + 1 - cx, top, view], rec_one.at[c, 0, j, :, view],
+                         ss2.at[c, i, 0, j], rs2.at[c, i, 0, j], to_x)
+            yield remote(own.at[c, (1 - cy) * 2 + j, bottom, view], rec_one.at[c, 1, j, :, view],
+                         ss2.at[c, i, 1, j], rs2.at[c, i, 1, j], to_y)
+
+    def two_step(part, c):
+        view, i = lanes_of[part], part_at[part]
+        yield remote(own.at[c, (1 - cy) * 2 + cx, top, view], rec_two.at[c, 0, :, view],
+                     ss2.at[c, i, 0, 2], rs2.at[c, i, 0, 2], to_y)
+        yield remote(own.at[c, cy * 2 + 1 - cx, bottom, view], rec_two.at[c, 1, :, view],
+                     ss2.at[c, i, 1, 2], rs2.at[c, i, 1, 2], to_x)
+
+    def column(part, step):
+        there = (col + step) % 4
+        view, i = lanes_of[part], part_at[part]
+        return remote(own.at[there, chip, :, view], rec_z.at[step - 1, :, view],
+                      zss.at[i, step - 1], zrs.at[i, step - 1], {"col": there})
+
+    def stage_one(part, k):
+        c, view = nth(k), lanes_of[part]
+        def body(q, carry):
+            to_sibling(part, c, q).wait_recv()
+            add_into(own.at[c, q, :, view], rec_sib.at[c, q, :, view])
+            return carry
+        lax.fori_loop(0, 4, body, 0)
+        for copy in one(part, c):
+            copy.start()
+
+    def stage_two(part, k):
+        c, view = nth(k), lanes_of[part]
+        for copy in one(part, c):
+            copy.wait_recv()
+        for j in range(2):
+            add_into(own.at[c, j * 2 + cx, top, view], rec_one.at[c, 0, j, :, view])
+            add_into(own.at[c, cy * 2 + j, bottom, view], rec_one.at[c, 1, j, :, view])
+        for copy in two_step(part, c):
+            copy.start()
+
+    def stage_three(part, k):
+        c, view = nth(k), lanes_of[part]
+        for copy in two_step(part, c):
+            copy.wait_recv()
+        add_into(own.at[c, chip, top, view], rec_two.at[c, 0, :, view])
+        add_into(own.at[c, chip, bottom, view], rec_two.at[c, 1, :, view])
+        pl.when(k < 3)(lambda: column(part, k + 1).start())
+
+    def out_grads(k, carry):
+        c = nth(k)
+        weight_grads("b", c, a_t, lambda: branch[:, cols_b(c)])
+        pl.when(k >= 1)(lambda: stage_one("b", k - 1))
+        pl.when(k >= 2)(lambda: stage_two("b", k - 2))
+        pl.when(k >= 3)(lambda: stage_three("b", k - 3))
+        return carry
+    lax.fori_loop(0, 4, out_grads, 0)
+
+    def input_grads(k, carry):
+        c = nth(k)
+        attend_back(c)
+        weight_grads("a", c, n_t, lambda: qg[c])
+        pl.when(k == 0)(lambda: stage_one("b", k + 3))
+        pl.when(k >= 1)(lambda: stage_one("a", k - 1))
+        pl.when(k <= 1)(lambda: stage_two("b", k + 2))
+        pl.when(k >= 2)(lambda: stage_two("a", k - 2))
+        pl.when(k <= 2)(lambda: stage_three("b", k + 1))
+        pl.when(k >= 3)(lambda: stage_three("a", k - 3))
+        return carry
+    lax.fori_loop(0, 4, input_grads, 0)
+    stage_one("a", 3)
+    stage_two("a", 2)
+    stage_three("a", 1)
+
+    def to_tokens(m, carry):
+        rows = pl.ds(pl.multiple_of(m * half, half), half)
+        grad = dot_t(qg[0, rows, :], full_a[:, 0:width_a])
+        for c in range(1, 4):
+            grad = grad + dot_t(qg[c, rows, :], full_a[:, c * width_a : (c + 1) * width_a])
+        x = tokens[rows, :].astype(f32)
+        factor = lax.rsqrt(jnp.mean(x * x, axis=1, keepdims=True) + EPSILON)
+        small[8:9, :] += jnp.sum(grad * x * factor, axis=0, keepdims=True)
+        scaled = grad * gain_one[...]
+        inner = jnp.mean(scaled * x, axis=1, keepdims=True)
+        d_tokens[rows, :] += factor * scaled - x * (factor * factor * factor * inner)
+        return carry
+    lax.fori_loop(0, 2, to_tokens, 0)
+
+    span = s_mid.shape[1]
+
+    def small_plane(flip):
+        there = row_at(row, flip)
+        view = small.at[:, pl.ds(pl.multiple_of((there // 2) * span, 128), span)]
+        return remote(view, s_rec.at[flip - 1], s_ss.at[flip - 1], s_rs.at[flip - 1], {"row": there})
+
+    def small_column(step):
+        return remote(s_mid, s_zrec.at[step - 1], sz_ss.at[step - 1], sz_rs.at[step - 1], {"col": (col + step) % 4})
+
+    each_flip(lambda flip: small_plane(flip).start())
+    stage_two("a", 3)
+    stage_three("a", 2)
+    s_mid[...] = small[:, pl.ds(pl.multiple_of(chip * span, 128), span)]
+
+    def add_small(flip):
+        small_plane(flip).wait_recv()
+        s_mid[...] += s_rec[flip - 1]
+
+    each_flip(add_small)
+    for step in (1, 2, 3):
+        small_column(step).start()
+    stage_three("a", 3)
+
+    own_prod.wait()
+    each_flip(lambda flip: back_prod(flip).wait_recv())
+
+    def to_output(m, carry):
+        rows = pl.ds(pl.multiple_of(m * half, half), half)
+        total = hidden[rows, :]
+        for k in range(2):
+            picked = jnp.where(at_slot(rows, k), 1.0, 0.0).astype(low)
+            total = total + dot(picked, rec_prod[...]) * gates[rows, k : k + 1]
+        out_ref[rows, :] = total.astype(low)
+        return carry
+    lax.fori_loop(0, 2, to_output, 0)
+
+    total = s_mid[...]
+    for step in (1, 2, 3):
+        small_column(step).wait_recv()
+        total = total + s_zrec[step - 1]
+    sum_s[...] = total
+    for part in ("b", "a"):
+        for step in (1, 2, 3):
+            column(part, step).wait_recv()
+
+    def to_sums(i, carry):
+        rows = pl.ds(pl.multiple_of(i * 32, 32), 32)
+        total = own[col, chip, rows, :].astype(f32)
+        for step in range(3):
+            total = total + rec_z[step, rows, :].astype(f32)
+        sum_a[rows, :] = total[:, :width_a]
+        sum_b[rows, :] = total[:, width_a:]
+        return carry
+    lax.fori_loop(0, block // 32, to_sums, 0)
+
+
+    def all_sent(flip):
+        for copy in back(flip):
+            copy.wait_send()
+        back_prod(flip).wait_send()
+        small_plane(flip).wait_send()
+
+    each_flip(all_sent)
+    for step in (1, 2, 3):
+        small_column(step).wait_send()
+        column("a", step).wait_send()
+        column("b", step).wait_send()
+
+    def sent(c, carry):
+        for part in ("a", "b"):
+            def body(q, carry):
+                to_sibling(part, c, q).wait_send()
+                return carry
+            lax.fori_loop(0, 4, body, 0)
+            for copy in one(part, c):
+                copy.wait_send()
+            for copy in two_step(part, c):
+                copy.wait_send()
+        return carry
+    lax.fori_loop(0, 4, sent, 0)
+
+
+def run_backward(slot_of, gates, ids, router, gain_one, gain_two, lse, segments, gate_grad, in_grad, produced,
+                 hidden, tokens, cotangent, normed, attended, normed_two, qkv, full_a, full_out):
+    sems = pltpu.SemaphoreType.DMA
+    length, model = tokens.shape
+    block = full_a.shape[0] // 8
+    width_a, width_b = full_a.shape[1] // 4, full_out.shape[1] // 4
+    width = width_a + width_b
+    cut = block // 2
+    low, f32 = tokens.dtype, jnp.float32
+    vm = pl.BlockSpec(memory_space=pltpu.VMEM)
+    slots = in_grad.shape[0]
+    capacity = slots // 8
+    span = model // 4
+    router_p = jnp.pad(router, ((0, 0), (0, 128 - router.shape[1])))
+    v = pltpu.VMEM
+    rows_low = v((length, model), low)
+    return pl.pallas_call(
+        backward_kernel,
+        out_shape=(
+            jax.ShapeDtypeStruct((length, model), low),
+            jax.ShapeDtypeStruct((length, model), f32),
+            jax.ShapeDtypeStruct((block, width_a), f32),
+            jax.ShapeDtypeStruct((block, width_b), f32),
+            jax.ShapeDtypeStruct((16, span), f32),
+        ),
+        in_specs=[vm] * 9 + [ANY] * 12,
+        out_specs=(vm,) * 5,
+        scratch_shapes=[
+            v((slots, model), low), v((8, 1, capacity), f32), v((slots, model), low),
+            v((length, model), f32), rows_low, rows_low, rows_low,
+            v(qkv.shape, low), v(full_a.shape, low), v(full_out.shape, low),
+            v((model, length), low), v((model, length), low), rows_low,
+            v((length, length), f32), v((width_b, model), low), v((length, width_b), low), v((4, length, width_a), low),
+            v((length, 128), low), v((16, model), f32),
+            v((4, 4, block, width), low), v((4, 4, block, width), low), v((4, 4, block, width), low),
+            v((4, 2, 2, cut, width), low), v((4, 2, cut, width), low), v((3, block, width), low),
+            v((7, 16, span), f32), v((16, span), f32), v((3, 16, span), f32),
+            sems((9,)), sems((7,)), sems((7,)), sems((7,)), sems((7,)), sems((7,)), sems((7,)), sems((3,)),
+            sems((4, 4, 2)), sems((4, 4, 2)), sems((4, 2, 2, 3)), sems((4, 2, 2, 3)),
+            sems((2, 3)), sems((2, 3)), sems((7,)), sems((7,)), sems((3,)), sems((3,)),
+        ],
+        compiler_params=pltpu.CompilerParams(
+            collective_id=2, has_side_effects=True, vmem_limit_bytes=60 * 2**20
+        ),
+        cost_estimate=pl.CostEstimate(flops=0, bytes_accessed=1_000_000, transcendentals=0),
+    )(slot_of, gates, ids, router_p, gain_one[None], gain_two[None], lse, segments.reshape(1, length),
+      segments.reshape(length, 1), gate_grad, in_grad, produced, hidden, tokens, cotangent, normed, attended,
+      normed_two, qkv, full_a, full_out)
+
+
 def rms_factor(rows_in):
     return lax.rsqrt(jnp.mean(rows_in * rows_in, axis=1, keepdims=True) + EPSILON)
 
@@ -818,6 +1041,18 @@
 
 def on_small_slice():
     return lax.axis_size("row") == 8 and lax.axis_size("col") == 4
+
+
+def pair_heads(a):
+    if not on_small_slice():
+        return a
+    a = a.reshape(a.shape[0], -1, 2, QUERY_PER_KEY, HEAD_SIZE)
+    return a.transpose(0, 1, 3, 2, 4).reshape(a.shape[0], -1)
+
+
+def part_heads(a):
+    a = a.reshape(a.shape[0], -1, QUERY_PER_KEY, 2, HEAD_SIZE)
+    return a.transpose(0, 1, 3, 2, 4).reshape(a.shape[0], -1)
 
 
 def gather_all(own_a, own_b, own_s, own_c):
@@ -842,9 +1077,6 @@
 
 
 def reduce_all(grad_a, grad_b, grad_s):
-    if on_small_slice():
-        return reduce_attention(grad_a, grad_b, grad_s)
-
     def both(g):
         plane = lax.psum_scatter(g, "row", scatter_dimension=0, tiled=True).astype(jnp.float32)
         return lax.psum_scatter(plane, "col", scatter_dimension=1, tiled=True)
@@ -950,7 +1182,7 @@
         [row_of(router.T), row_of(attn_gain[None]), row_of(expert_gain[None])], axis=0
     )
     own_s = jnp.pad(own_s, ((0, 16 - own_s.shape[0]), (0, 0)))
-    own_a = jnp.concatenate([w_query, w_key, w_value], axis=1)
+    own_a = jnp.concatenate([pair_heads(w_query), w_key, w_value], axis=1)
     if on_small_slice():
         line_a, line_out, small, plane_upstream = gather_line(own_a, w_out, own_s, cotangent)
         own_gu, own_down, line_a, line_out = lax.optimization_barrier(
@@ -967,8 +1199,11 @@
     rows_f = tokens.astype(jnp.float32)
     factor_one = rms_factor(rows_f)
     normed = (rows_f * factor_one * gain_one).astype(jnp.bfloat16)
-    qkv = dot(normed, full_a).astype(jnp.bfloat16).reshape(length, cols, width_a)
+    flat_qkv = dot(normed, full_a).astype(jnp.bfloat16)
+    qkv = flat_qkv.reshape(length, cols, width_a)
     query_rows = qkv[:, :, :width_q].reshape(length, -1)
+    if on_small_slice():
+        query_rows = part_heads(query_rows)
     rows_of_key = qkv[:, :, width_q : width_q + width_k].reshape(length, -1)
     rows_of_value = qkv[:, :, width_q + width_k :].reshape(length, -1)
     heads_of_key = rows_of_key.reshape(length, KEY_VALUE_HEADS, HEAD_SIZE)
@@ -999,11 +1234,41 @@
     mine = lax.dynamic_index_in_dim(plane_gate, lax.axis_index("row"), axis=1, keepdims=False)
     routed = mine >= 0.0
     place = jnp.cumsum(routed.astype(jnp.int32), axis=1) - 1
+    any_named = jnp.any(named, axis=1)
+    before = jnp.cumsum(any_named.astype(jnp.int32), axis=0) - 1
+    slot_of = jnp.sum(
+        jnp.where(named, before[:, None, :] + jnp.arange(experts, dtype=jnp.int32) * capacity, 0),
+        axis=2,
+    )
     if on_small_slice():
         in_grad, produced, slot_gate_grad, grad_gu_local, grad_down = run_expert(
             jnp.where(routed, place, -1), mine, plane_normed, plane_upstream, full_gu, own_down
         )
-        slot_gate_grad = slot_gate_grad[:, 0]
+        grad_gu = lax.psum_scatter(grad_gu_local, "col", scatter_dimension=0, tiled=True)
+        lse = (row_max + jnp.log(totals)).reshape(KEY_VALUE_HEADS, 1, QUERY_PER_KEY * length)
+        output, d_tokens, sum_a, sum_out, sum_s = run_backward(
+            slot_of, gate_probs, expert_ids, full_router, gain_one, gain_two, lse, segments,
+            slot_gate_grad, in_grad, produced, hidden, tokens, cotangent, normed, attended, normed_two,
+            flat_qkv, full_a, full_out,
+        )
+        core = lax.axis_index("row") % 2
+        col = lax.axis_index("col")
+        own_router = lax.dynamic_slice(sum_s, (col * router_cols, core * block), (router_cols, block))
+        own_gains = lax.dynamic_slice(sum_s, (experts, core * block + col * piece), (2, piece))
+        return (
+            output,
+            d_tokens,
+            own_gains[0],
+            part_heads(sum_a[:, :width_q]),
+            sum_a[:, width_q : width_q + width_k],
+            sum_a[:, width_q + width_k :],
+            sum_out,
+            own_gains[1],
+            own_router.T,
+            grad_gu[:, :hidden_units].astype(jnp.float32)[None],
+            grad_gu[:, hidden_units:].astype(jnp.float32)[None],
+            grad_down[None],
+        )
     else:
         in_grad, produced, slot_gate_grad, grad_gu_local, grad_down = expert_elsewhere(
             place, routed, mine, plane_normed, plane_upstream, full_gu, own_down
@@ -1020,12 +1285,6 @@
         produced.reshape(rows, capacity, model), "row", split_axis=0, concat_axis=0, tiled=True
     ).reshape(experts * capacity, model)
 
-    any_named = jnp.any(named, axis=1)
-    before = jnp.cumsum(any_named.astype(jnp.int32), axis=0) - 1
-    slot_of = jnp.sum(
-        jnp.where(named, before[:, None, :] + jnp.arange(experts, dtype=jnp.int32) * capacity, 0),
-        axis=2,
-    )
     all_slots = jnp.arange(experts * capacity, dtype=jnp.int32)
     is_slot = slot_of.T[:, :, None] == all_slots[None, None, :]
     from_slot = is_slot.astype(jnp.bfloat16)

time: 453 us -> 416 us (0.918)
  Pallas kernels: 278 us -> 349 us
  matrix products: 57.9 us -> 10.1 us
  waiting for transfers between devices: 36.4 us -> 0.04 us
  other arithmetic: 25.1 us -> 14.5 us
  starting transfers between devices: 9.4 us -> 0.08 us
  local copies, waits for them, and re-layouts: 18.7 us -> 27.6 us
  blocking collectives: 7.66 us -> 0 us
    pallas_call x1, Pallas kernels: 70.9 us -> 142 us  [run_backward(): pl.pallas_call(backward_kernel, out_shape=(jax.ShapeDtypeStruct((length,...]
    all_to_all x2 -> x0, waiting for transfers between devices: 36.4 us -> none  [the longest x1 32.4 us: per_device(): lax.all_to_all(in_grad.reshape(rows, capacity, model), 'row', split_axis=...]
    dot_general x10 -> x1, matrix products: 29.3 us -> 1.08 us  [masked_scores(): jnp.einsum('qkgd,skd->kgqs', heads_of_query, heads_of_key, preferred_elem...]
    dot_general x6 -> x3, matrix products: 20.3 us -> 7.23 us  [dot(): return jnp.dot(a, b, preferred_element_type=jnp.float32)]
    all_to_all x2 -> x0, starting transfers between devices: 9.32 us -> none  [the longest x1 4.88 us: per_device(): lax.all_to_all(produced.reshape(rows, capacity, model), 'row', split_axis...]
    all_to_all x1 -> x0, blocking collectives: 7.66 us -> none  [per_device(): lax.all_to_all(slot_gate_grad.reshape(rows, 1, capacity), 'row', split_ax...]
    sub x2 -> x0, other arithmetic: 4.65 us -> none  [the longest x1 3.05 us: per_device(): hidden_grad + factor_one * scaled_one]
    sub x1 -> x0, matrix products: 4.62 us -> none  [per_device(): expo_rows = jnp.exp(scores - row_max)]
  transfers between devices with their start and end apart: 4 -> 2, of which waited for: 2 -> 0; matrix products, arithmetic and copies ran while one was open for 20% -> 9% of each run, Pallas kernels for 36% -> 56%
where the time goes in v4:
time: 416 us
  Pallas kernels  349 us (84%)
  local copies, waits for them, and re-layouts  27.6 us (7%)
  other arithmetic  14.5 us (3%)
  between operations  14.5 us (3%)
  matrix products  10.1 us (2%)
    pallas_call x1, Pallas kernels, run_backward(): pl.pallas_call(backward_kernel, out_shape=(jax.ShapeDtypeStruct((length,...  142 us
    pallas_call x1, Pallas kernels, run_expert(): pl.pallas_call(expert_kernel, out_shape=(jax.ShapeDtypeStruct((slots, mod...  78 us
    pallas_call x1, Pallas kernels, gather_plane(): pl.pallas_call(functools.partial(plane_kernel, count), out_shape=tuple((j...  56.3 us
    pallas_call x1, Pallas kernels, gather_line(): pl.pallas_call(line_kernel, out_shape=(jax.ShapeDtypeStruct((own_a.shape[...  39.3 us
    pallas_call x1, Pallas kernels, spread_tokens(): pl.pallas_call(spread_kernel, out_shape=(jax.ShapeDtypeStruct((8 * own_c....  33.5 us
    unnamed x44, local copies, waits for them, and re-layouts  9.69 us
  transfers between devices with their start and end apart: 2, of which 0 were waited for; matrix products, arithmetic and copies ran while one was open for 9% of the time, Pallas kernels for 56%

profile of v4, /device:TPU:0, one launch (start us, length us, event | category | flops | bytes accessed | tf_op | source)
XLA Modules:
  0.0 415.5 jit_solution(8010838196617548780)
XLA Ops:
  7.2 1.0 copy.94
  9.8 2.7 pad_maximum_fusion
  13.2 39.3 %shard_map.229 = (bf16[192,2560]{1,0:T(8,128)(2,1)}, bf16[192,1536]{1,0:T(8,128)(2,1)}, bf16[4,8,16,256]{3,2,1,0:T(8,128)(2,1)}, bf16[2048,1536]{1,0:T(8,128)(2,1)}) custom-call(bf16[192,640]{1,0:T(8,128)(2,1)} %pad_maximum_fusion.1.own_a, bf16[192,384]{1,0:T(8,128)(2,1)} %own_b.1, bf16[16,256]{1,0:T(8,128)(2,1)} %pad.22.own_s, bf16[256,1536]{1,0:T(8,128)(2,1)} %cot_hbm.1), custom_call_target="tpu_custom_call" | custom-call | bytes 1000000 | tf_op jit(solution)/shard_map/pallas_call | solution.py:215
  52.6 0.9 slice_convert_fusion
  53.6 56.3 %shard_map.230 = (bf16[1536,2560]{1,0:T(8,128)(2,1)}, bf16[1536,1536]{1,0:T(8,128)(2,1)}) custom-call(bf16[192,2560]{1,0:T(8,128)(2,1)} %get-tuple-element.37.refs_0_, bf16[192,1536]{1,0:T(8,128)(2,1)} %get-tuple-element.38.refs_1_), custom_call_target="tpu_custom_call" | custom-call | bytes 1000000 | tf_op jit(solution)/shard_map/pallas_call | solution.py:271
  110.5 0.9 copy-done.4
  111.4 5.5 %convolution_convert_fusion.qkv_hbm = bf16[256,2560]{1,0:T(8,128)(2,1)S(1)} fusion(bf16[256,1536]{1,0:T(8,128)(2,1)S(1)} %fusion.5.normed_hbm, bf16[1536,2560]{1,0:T(8,128)(2,1)} %get-tuple-element.39.full_a_hbm), kind=kOutput, calls=%fused_computation.5 | convolution fusion | flops 2013921280 | bytes 9961472 | tf_op jit(solution)/shard_map/dot_general | solution.py:1031
  117.4 1.2 slice.71
  118.5 1.0 fusion.21
  119.5 1.1 copy.99
  120.7 1.5 copy.123
  122.6 0.9 slice_bitcast_fusion.2
  123.8 1.1 fusion.1
  124.9 1.4 fusion
  126.2 1.8 fusion.6
  128.4 1.5 multiply_reduce_fusion
  131.7 33.5 %shard_map.231 = (bf16[2048,1536]{1,0:T(8,128)(2,1)}, f32[8,8,256]{2,1,0:T(8,128)}) custom-call(bf16[256,1536]{1,0:T(8,128)(2,1)} %copy-done.2, f32[8,256]{1,0:T(8,128)} %select_bitcast_fusion.own_g), custom_call_target="tpu_custom_call" | custom-call | bytes 1000000 | tf_op jit(solution)/shard_map/pallas_call | solution.py:312
  165.2 0.9 compare_convert_fusion
  167.6 78.0 %shard_map.232 = (bf16[1024,1536]{1,0:T(8,128)(2,1)}, bf16[1024,1536]{1,0:T(8,128)(2,1)}, f32[8,1,128]{2,1,0:T(1,128)}, bf16[1536,2048]{1,0:T(8,128)(2,1)}, f32[256,1536]{1,0:T(8,128)}) custom-call(s32[8,1,256]{2,1,0:T(1,128)} %compare_select_fusion.key, f32[8,1,256]{2,1,0:T(1,128)} %copy-done.11, bf16[2048,1536]{1,0:T(8,128)(2,1)} %get-tuple-element.42.normed_hbm, ...), custom_call_target="tpu_custom_call" | custom-call | bytes 1000000 | tf_op jit(solution)/shard_map/pallas_call | solution.py:594
  245.7 1.2 copy.116.attended_hbm
  248.5 0.8 copy.113.ids
  249.9 0.8 pad.23.router_p
  251.7 0.8 copy.112.slot_of
  253.3 141.6 %shard_map.233 = (bf16[256,1536]{1,0:T(8,128)(2,1)}, f32[256,1536]{1,0:T(8,128)}, f32[192,640]{1,0:T(8,128)}, f32[192,384]{1,0:T(8,128)}, f32[16,384]{1,0:T(8,128)}) custom-call(s32[256,2]{1,0:T(8,128)} %copy.112.slot_of, f32[256,2]{1,0:T(8,128)} %copy-done.7, s32[256,2]{1,0:T(8,128)} %copy.113.ids, bf16[1536,128]{1,0:T(8,128)(2,1)} %pad.23.router_p, ...), custom_call_target="tpu_custom_call" | custom-call | bytes 1000000 | tf_op jit(solution)/shard_map/pallas_call | solution.py:992
  394.9 1.0 slice.62
  396.1 0.9 copy.119
  397.7 1.4 dynamic-slice_bitcast_fusion
  399.6 1.6 fusion.22
  401.3 3.5 fusion.7
  404.8 0.9 copy.128
  405.7 1.1 copy.129
  407.6 1.1 copy.131
  (99 shorter events, 13.8 us)
Async XLA Ops:
  7.2 5.3 %copy-start.14 = (bf16[192,128]{1,0:T(8,128)(2,1)S(1)}, bf16[192,128]{1,0:T(8,128)(2,1)}, u32[]{:S(2)}) copy-start(bf16[192,128]{1,0:T(8,128)(2,1)} %param.17) | copy-start | bytes 147460
  7.2 5.3 %copy-start.13 = (bf16[192,128]{1,0:T(8,128)(2,1)S(1)}, bf16[192,128]{1,0:T(8,128)(2,1)}, u32[]{:S(2)}) copy-start(bf16[192,128]{1,0:T(8,128)(2,1)} %param.18) | copy-start | bytes 147460
  7.2 160.4 %all-gather.2.cloned.1.call-start = ((), (), s32[]{:S(2)}) async-start(), calls=%async_computation.1 | async-start | bytes 7864320 | tf_op jit(solution)/shard_map/all_gather | solution.py:1194
  12.5 97.5 %copy-start.1 = (bf16[256,1536]{1,0:T(8,128)(2,1)S(1)}, bf16[256,1536]{1,0:T(8,128)(2,1)}, u32[]{:S(2)}) copy-start(bf16[256,1536]{1,0:T(8,128)(2,1)} %tokens_hbm.1) | copy-start | bytes 2359300
  52.5 348.7 %reduce-scatter.2.cloned.1.call-start = ((), (), s32[]{:S(2)}) async-start(), calls=%async_computation.2 | async-start | bytes 7864320 | tf_op jit(solution)/shard_map/reduce_scatter | solution.py:1247
  110.5 0.9 copy-start.4
  116.8 5.4 %copy-start.3 = (bf16[256,2560]{1,0:T(8,128)(2,1)}, bf16[256,2560]{1,0:T(8,128)(2,1)S(1)}, u32[]{:S(2)}) copy-start(bf16[256,2560]{1,0:T(8,128)(2,1)S(1)} %convolution_convert_fusion.qkv_hbm) | copy-start | bytes 3932164
  117.4 6.3 %copy-start.15 = (s32[1,256]{1,0:T(1,128)S(1)}, s32[1,256]{1,0:T(1,128)}, u32[]{:S(2)}) copy-start(s32[1,256]{1,0:T(1,128)} %seg_row.1) | copy-start | bytes 3076
  119.5 2.8 copy-start.8
  124.8 3.1 slice-start
  126.2 2.2 slice-start.1
  129.9 115.7 %copy-start = (f32[256,1536]{1,0:T(8,128)}, f32[256,1536]{1,0:T(8,128)S(1)}, u32[]{:S(2)}) copy-start(f32[256,1536]{1,0:T(8,128)S(1)} %get-tuple-element.109.hidden_hbm) | copy-start | bytes 4718596
  129.9 0.7 copy-start.12
  130.2 1.5 copy-start.2
  130.9 114.7 %copy-start.7 = (f32[256,2]{1,0:T(8,128)}, f32[256,2]{1,0:T(8,128)S(1)}, u32[]{:S(2)}) copy-start(f32[256,2]{1,0:T(8,128)S(1)} %broadcast_divide_fusion.gates) | copy-start | bytes 6148
  166.0 1.6 copy-start.11
  396.1 8.7 %copy-start.9 = (bf16[256,1536]{1,0:T(8,128)(2,1)S(1)}, bf16[256,1536]{1,0:T(8,128)(2,1)}, u32[]{:S(2)}) copy-start(bf16[256,1536]{1,0:T(8,128)(2,1)} %get-tuple-element.122) | copy-start | bytes 2359300
  401.2 4.4 %copy-start.6 = (f32[256,1536]{1,0:T(8,128)S(1)}, f32[256,1536]{1,0:T(8,128)}, u32[]{:S(2)}) copy-start(f32[256,1536]{1,0:T(8,128)} %get-tuple-element.123) | copy-start | bytes 4718596
  404.8 2.0 copy-start.10
  404.8 2.8 copy-start.5
Sparse Core Ops, SparseCore 0:
  52.7 113.9 all-gather.1
  245.8 119.1 reduce-scatter.1

commit v5 on v4

--- a/solution.py
+++ b/solution.py
@@ -134,7 +134,7 @@
     return pltpu.make_async_copy(source, middle, sem), pltpu.make_async_copy(middle, target, sem)
 
 
-def line_kernel(own_a, own_b, own_s, own_c, line_a, line_b, full_s, full_c, mid_a, mid_b, mid_c,
+def line_kernel(own_a, own_b, own_s, own_c, w_gate, w_up, line_a, line_b, full_s, full_c, own_gu, mid_a, mid_b, mid_c, mid_gu,
                 zss, zrs, css, crs, s_zs, s_zr, s_ps, s_pr, loc):
     row, col = lax.axis_index("row"), lax.axis_index("col")
     width_a, width_b = own_a.shape[1], own_b.shape[1]
@@ -157,6 +157,12 @@
         copy.start()
     small_copy = pltpu.make_async_copy(own_s, full_s.at[col, row], loc.at[3])
     small_copy.start()
+    units = w_gate.shape[1]
+    to_gu = [
+        pltpu.make_async_copy(w, mid_gu.at[:, pl.ds(i * units, units)], loc.at[4 + i])
+        for i, w in enumerate((w_gate, w_up))
+    ]
+    from_gu = pltpu.make_async_copy(mid_gu, own_gu, loc.at[6])
     greet(range(1, 8), (1, 2, 3))
 
     def along(c, source_a, source_b, right, left):
@@ -178,10 +184,15 @@
     for i, step in enumerate((1, 2, 3)):
         remote(own_s, full_s.at[col, row], s_zs.at[i], s_zr.at[i], {"col": (col + step) % 4}).start()
     plane_send(vc, row, csv, crv, own_c)
+    for copy in to_gu:
+        copy.start()
     for first, second in copies:
         first.wait()
         second.start()
     small_copy.wait()
+    for copy in to_gu:
+        copy.wait()
+    from_gu.start()
     arrived(1)
     for i, step in enumerate((3, 2, 1)):
         remote(own_s, full_s.at[(col + step) % 4, row], s_zs.at[i], s_zr.at[i], {"col": (col + 1) % 4}).wait()
@@ -193,6 +204,7 @@
     plane_last(vc, hc, row, csv, crv)
     for _, second in copies:
         second.wait()
+    from_gu.wait()
     plane_finish(vc, hc, row, csv, crv)
     for i in range(1, 8):
         there = row_at(row, i)
@@ -209,7 +221,7 @@
                 remote(of_b(c), of_b(c), zss.at[1, c, d], zrs.at[1, c], there).wait_send()
 
 
-def gather_line(own_a, own_b, own_s, own_c):
+def gather_line(own_a, own_b, own_s, own_c, w_gate, w_up):
     sems = pltpu.SemaphoreType.DMA
     rows_c = own_c.shape[0]
     return pl.pallas_call(
@@ -219,20 +231,22 @@
             jax.ShapeDtypeStruct((own_b.shape[0], own_b.shape[1] * 4), own_b.dtype),
             jax.ShapeDtypeStruct((4, 8) + own_s.shape, own_s.dtype),
             jax.ShapeDtypeStruct((8 * rows_c, own_c.shape[1]), own_c.dtype),
+            jax.ShapeDtypeStruct((w_gate.shape[0], 2 * w_gate.shape[1]), w_gate.dtype),
         ),
-        in_specs=[ANY] * 4,
-        out_specs=(ANY,) * 4,
+        in_specs=[ANY] * 6,
+        out_specs=(ANY,) * 5,
         scratch_shapes=[
             pltpu.VMEM(own_a.shape, own_a.dtype),
             pltpu.VMEM(own_b.shape, own_b.dtype),
             pltpu.VMEM(own_c.shape, own_c.dtype),
+            pltpu.VMEM((w_gate.shape[0], 2 * w_gate.shape[1]), w_gate.dtype),
             sems((2, 4, 2)), sems((2, 4)),
             sems((9,)), sems((9,)),
-            sems((3,)), sems((3,)), sems((7,)), sems((7,)), sems((4,)),
+            sems((3,)), sems((3,)), sems((7,)), sems((7,)), sems((7,)),
         ],
         compiler_params=pltpu.CompilerParams(collective_id=0, has_side_effects=True),
         cost_estimate=pl.CostEstimate(flops=0, bytes_accessed=1_000_000, transcendentals=0),
-    )(own_a, own_b, own_s, own_c)
+    )(own_a, own_b, own_s, own_c, w_gate, w_up)
 
 
 def plane_kernel(count, *refs):
@@ -335,11 +349,36 @@
     lax.fori_loop(0, target.shape[0] // 32, body, 0)
 
 
+def finish_kernel(count, *refs):
+    for source, target in zip(refs[:count], refs[count + 1 : 2 * count + 1]):
+        target[...] = source[...]
+    gu, gate, up = refs[count], refs[2 * count + 1], refs[2 * count + 2]
+    gate[...] = gu[:, : gate.shape[1]].astype(gate.dtype)
+    up[...] = gu[:, gate.shape[1] :].astype(up.dtype)
+
+
+def finish(arrays, grad_gu):
+    steps = 4
+
+    def spec(a, columns=None):
+        return pl.BlockSpec((a.shape[0] // steps, columns or a.shape[1]), lambda i: (i, 0))
+
+    units = grad_gu.shape[1] // 2
+    half = jax.ShapeDtypeStruct((grad_gu.shape[0], units), jnp.float32)
+    return pl.pallas_call(
+        functools.partial(finish_kernel, len(arrays)),
+        grid=(steps,),
+        out_shape=tuple(jax.ShapeDtypeStruct(a.shape, a.dtype) for a in arrays) + (half, half),
+        in_specs=[spec(a) for a in arrays] + [spec(grad_gu)],
+        out_specs=tuple(spec(a) for a in arrays) + (spec(half), spec(half)),
+    )(*arrays, grad_gu)
+
+
 def expert_kernel(key, mine, normed_hbm, upstream_hbm, gu_hbm, own_down,
-                  in_ref, prod_ref, gate_grad_out, grad_gu, sum_down,
+                  in_ref, prod_ref, gate_grad_out, grad_gu, sum_down, back_far,
                   gate_grad_ref, x_t, ups, gu, down, act, silu, slope, both, gd, rec_right, rec_left, stage, gate,
-                  load_sem, src_sem, stage_sem, zss, zrs, rss, rrs):
-    col = lax.axis_index("col")
+                  load_sem, src_sem, stage_sem, zss, zrs, rss, rrs, fss, frs):
+    row, col = lax.axis_index("row"), lax.axis_index("col")
     sources, _, length = key.shape
     slots = in_ref.shape[0]
     capacity = slots // sources
@@ -362,7 +401,7 @@
 
     for copy in fetch(0, 0):
         copy.start()
-    greet((), (1, 2, 3))
+    greet((X + Y, X + Y + SIB), (1, 2, 3))
 
     def pass_on(c, source, right, left):
         for d, (cond, there) in enumerate(((right, right_dev), (left, left_dev))):
@@ -489,6 +528,17 @@
                 stage_sem.at[slot, i],
             )
 
+    def far(j):
+        there = row_at(row, X + Y + j)
+        rows = pl.ds(pl.multiple_of(there * capacity, 16), capacity)
+        return remote(in_ref.at[rows, :], back_far.at[j], fss.at[j], frs.at[j], {"row": there})
+
+    def inputs(i, carry):
+        chip = row_at(row, 2 * (3 - i)) // 2
+        rows = pl.ds(pl.multiple_of(chip * 2 * capacity, 16), 2 * capacity)
+        in_ref[rows, :] = dot_t(both[rows, :], gu[...]).astype(in_ref.dtype)
+        return carry
+
     def backward(k):
         c = unit_at(col, k)
         first = pl.ds(pl.multiple_of(c * width, width), width)
@@ -503,6 +553,11 @@
             both[rows, second] = (act_grad * silu[rows, first]).astype(both.dtype)
             return carry
         lax.fori_loop(0, slots // chunk, body, 0)
+        @pl.when(k == 3)
+        def _():
+            inputs(0, 0)
+            far(0).start()
+            far(1).start()
         slot = k % 2
         @pl.when(k >= 2)
         def _():
@@ -534,11 +589,7 @@
         return carry
     lax.fori_loop(0, 4, backward_step, 0)
 
-    def inputs(m, carry):
-        rows = pl.ds(pl.multiple_of(m * chunk, chunk), chunk)
-        in_ref[rows, :] = dot_t(both[rows, :], gu[...]).astype(in_ref.dtype)
-        return carry
-    lax.fori_loop(0, slots // chunk, inputs, 0)
+    lax.fori_loop(1, sources // 2, inputs, 0)
 
     def outputs(m, carry):
         rows = pl.ds(pl.multiple_of(m * chunk, chunk), chunk)
@@ -581,6 +632,8 @@
             remote(down.at[e], down.at[e], zss.at[e, 1], zrs.at[e], left_dev).wait_send()
         return carry
     lax.fori_loop(0, 4, sent, 0)
+    for j in range(2):
+        far(j).wait()
 
 
 def run_expert(key, mine, normed, upstream, full_gu, own_down):
@@ -599,9 +652,10 @@
             jax.ShapeDtypeStruct((sources, 1, slots // sources), f32),
             jax.ShapeDtypeStruct((model, 2 * units), low),
             jax.ShapeDtypeStruct((width, model), f32),
+            jax.ShapeDtypeStruct((2, slots // sources, model), low),
         ),
         in_specs=[vm, vm, ANY, ANY, ANY, ANY],
-        out_specs=(vm, vm, vm, ANY, vm),
+        out_specs=(vm, vm, vm, ANY, vm, ANY),
         scratch_shapes=[
             pltpu.VMEM((slots, 128), f32),
             pltpu.VMEM((model, slots), low),
@@ -618,7 +672,7 @@
             pltpu.VMEM((2, model, 2 * width), low),
             pltpu.VMEM((slots, 128), f32),
             sems((2,)), sems((2, 2)), sems((2, 2)),
-            sems((4, 2)), sems((4,)), sems((2, 3)), sems((2, 3)),
+            sems((4, 2)), sems((4,)), sems((2, 3)), sems((2, 3)), sems((2,)), sems((2,)),
         ],
         compiler_params=pltpu.CompilerParams(
             collective_id=4, has_side_effects=True, vmem_limit_bytes=60 * 2**20
@@ -627,14 +681,14 @@
     )(key.reshape(sources, 1, length), mine.reshape(sources, 1, length), normed, upstream, full_gu, own_down)
 
 
-def backward_kernel(slot_of, gates, ids, router_p, gain_one, gain_two, lse, seg_row, seg_col,
-                    gate_grad, in_grad, produced, hidden_hbm, tokens_hbm, cot_hbm, normed_hbm, attended_hbm,
+def backward_kernel(table, router_p, gain_one, gain_two, lse,
+                    gate_grad, in_grad, back_far, produced, hidden_hbm, tokens_hbm, cot_hbm, normed_hbm, attended_hbm,
                     two_hbm, qkv_hbm, full_a_hbm, full_out_hbm,
-                    out_ref, d_tokens, sum_a, sum_b, sum_s,
-                    rec_in, rec_gate, rec_prod, hidden, tokens, cot, two, qkv, full_a, full_out,
+                    out_ref, d_tokens, sum_q, sum_k, sum_v, sum_b, sum_s,
+                    cols, rec_in, rec_gate, rec_prod, hidden, tokens, cot, two, qkv, full_a, full_out,
                     n_t, a_t, branch, bias, out_rows, grad_c, qg, lgs, small,
                     own, sib_out, rec_sib, rec_one, rec_two, rec_z, s_rec, s_mid, s_zrec,
-                    load, in_ss, in_rs, g_ss, g_rs, pr_ss, pr_rs, loc,
+                    load, in_ss, in_rs, g_ss, g_rs, pr_ss, pr_rs, loc, far_sem,
                     ss1, rs1, ss2, rs2, zss, zrs, s_ss, s_rs, sz_ss, sz_rs):
     row, col = lax.axis_index("row"), lax.axis_index("col")
     core = row % 2
@@ -643,7 +697,8 @@
     length, model = hidden.shape
     capacity = rec_in.shape[0] // 8
     block = own.shape[2]
-    width_a, width_b = sum_a.shape[1], sum_b.shape[1]
+    width_b = sum_b.shape[1]
+    width_a = own.shape[3] - width_b
     cut = block // 2
     half = length // 2
     f32, low = jnp.float32, branch.dtype
@@ -671,23 +726,36 @@
     ]
     greet(range(1, 8), (1, 2, 3))
 
+    far_in = [
+        pltpu.make_async_copy(back_far.at[j], rec_in.at[block_of(row_at(row, X + Y + j)), :], far_sem.at[j])
+        for j in range(2)
+    ]
+
     def back(flip):
         there = row_at(row, flip)
-        device = {"row": there}
-        return (
-            remote(in_grad.at[block_of(there), :], rec_in.at[block_of(row), :],
-                   in_ss.at[flip - 1], in_rs.at[flip - 1], device),
-            remote(gate_grad.at[there], rec_gate.at[row], g_ss.at[flip - 1], g_rs.at[flip - 1], device),
-        )
+        return remote(in_grad.at[block_of(there), :], rec_in.at[block_of(row), :],
+                      in_ss.at[flip - 1], in_rs.at[flip - 1], {"row": there})
+
+    def back_gate(flip):
+        there = row_at(row, flip)
+        return remote(gate_grad.at[there], rec_gate.at[row], g_ss.at[flip - 1], g_rs.at[flip - 1], {"row": there})
+
+    def each_near(function):
+        def body(i, carry):
+            function(5 - i)
+            return carry
+        lax.fori_loop(0, 5, body, 0)
 
     def back_prod(flip):
         there = row_at(row, flip)
         return remote(produced.at[block_of(there), :], rec_prod.at[block_of(row), :],
                       pr_ss.at[flip - 1], pr_rs.at[flip - 1], {"row": there})
 
-    each_flip(lambda flip: [copy.start() for copy in back(flip)])
-    for copy in (own_in, own_gate, own_prod):
+    each_near(lambda flip: back(flip).start())
+    each_flip(lambda flip: back_gate(flip).start())
+    for copy in (own_in, own_gate, own_prod, *far_in):
         copy.start()
+    cols[...] = table[...].T
     for copy in loads:
         copy.start()
     loads[0].wait()
@@ -696,22 +764,22 @@
     a_t[...] = out_ref[...].T
     key_pos = lax.broadcasted_iota(jnp.int32, (length, length), 0)
     query_pos = lax.broadcasted_iota(jnp.int32, (length, length), 1)
-    allowed = (key_pos <= query_pos) & (seg_col[...] == seg_row[...])
+    allowed = (key_pos <= query_pos) & (cols[:, 6:7] == table[6:7, :])
     bias[...] = jnp.where(allowed, 0.0, NEGATIVE)
     small[...] = jnp.zeros_like(small)
     for copy in loads[2:]:
         copy.wait()
-    for copy in (own_in, own_gate):
+    for copy in (own_in, own_gate, *far_in):
         copy.wait()
-    each_flip(lambda flip: [copy.wait_recv() for copy in back(flip)])
-    each_flip(lambda flip: back_prod(flip).start())
+    each_flip(lambda flip: back_gate(flip).wait_recv())
+    each_near(lambda flip: back(flip).wait_recv())
 
     all_gate = jnp.concatenate([rec_gate[e] for e in range(8)], axis=1)
     wide = rec_in.shape[0]
     lanes = lgs.shape[1]
 
     def at_slot(rows, k):
-        return slot_of[rows, k : k + 1] == lax.broadcasted_iota(jnp.int32, (half, wide), 1)
+        return cols[rows, k : k + 1] == lax.broadcasted_iota(jnp.int32, (half, wide), 1).astype(f32)
 
     def to_hidden(m, carry):
         rows = pl.ds(pl.multiple_of(m * half, half), half)
@@ -720,11 +788,11 @@
         two_grad = dot(picked, rec_in[...])
         grad_0 = jnp.sum(jnp.where(first, all_gate, 0.0), axis=1, keepdims=True)
         grad_1 = jnp.sum(jnp.where(second, all_gate, 0.0), axis=1, keepdims=True)
-        gate_0, gate_1 = gates[rows, 0:1], gates[rows, 1:2]
+        gate_0, gate_1 = cols[rows, 4:5], cols[rows, 5:6]
         mean = gate_0 * grad_0 + gate_1 * grad_1
-        lane = lax.broadcasted_iota(jnp.int32, (half, lanes), 1)
-        logit_grad = jnp.where(lane == ids[rows, 0:1], gate_0 * (grad_0 - mean), 0.0)
-        logit_grad = logit_grad + jnp.where(lane == ids[rows, 1:2], gate_1 * (grad_1 - mean), 0.0)
+        lane = lax.broadcasted_iota(jnp.int32, (half, lanes), 1).astype(f32)
+        logit_grad = jnp.where(lane == cols[rows, 2:3], gate_0 * (grad_0 - mean), 0.0)
+        logit_grad = logit_grad + jnp.where(lane == cols[rows, 3:4], gate_1 * (grad_1 - mean), 0.0)
         logit_grad = logit_grad.astype(low)
         lgs[rows, :] = logit_grad
         two_grad = two_grad + dot_t(logit_grad, router_p[...])
@@ -873,6 +941,7 @@
         return carry
     lax.fori_loop(0, 4, input_grads, 0)
     stage_one("a", 3)
+    each_flip(lambda flip: back_prod(flip).start())
     stage_two("a", 2)
     stage_three("a", 1)
 
@@ -922,7 +991,7 @@
         total = hidden[rows, :]
         for k in range(2):
             picked = jnp.where(at_slot(rows, k), 1.0, 0.0).astype(low)
-            total = total + dot(picked, rec_prod[...]) * gates[rows, k : k + 1]
+            total = total + dot(picked, rec_prod[...]) * cols[rows, 4 + k : 5 + k]
         out_ref[rows, :] = total.astype(low)
         return carry
     lax.fori_loop(0, 2, to_output, 0)
@@ -941,15 +1010,24 @@
         total = own[col, chip, rows, :].astype(f32)
         for step in range(3):
             total = total + rec_z[step, rows, :].astype(f32)
-        sum_a[rows, :] = total[:, :width_a]
+        span_c = width_b // QUERY_PER_KEY
+        zero, one_, two_ = (total[:, i * span_c : (i + 1) * span_c] for i in range(QUERY_PER_KEY))
+        turned = pltpu.roll(one_, HEAD_SIZE, 1)
+        first = lax.broadcasted_iota(jnp.int32, zero.shape, 1) < HEAD_SIZE
+        sum_q[rows, 0:span_c] = jnp.where(first, zero, turned)
+        sum_q[rows, span_c : 2 * span_c] = jnp.where(first, two_, zero)
+        sum_q[rows, 2 * span_c : width_b] = jnp.where(first, turned, two_)
+        sum_k[rows, :] = total[:, width_b : width_b + span_c]
+        sum_v[rows, :] = total[:, width_b + span_c : width_a]
         sum_b[rows, :] = total[:, width_a:]
         return carry
     lax.fori_loop(0, block // 32, to_sums, 0)
 
 
+    each_near(lambda flip: back(flip).wait_send())
+
     def all_sent(flip):
-        for copy in back(flip):
-            copy.wait_send()
+        back_gate(flip).wait_send()
         back_prod(flip).wait_send()
         small_plane(flip).wait_send()
 
@@ -973,8 +1051,11 @@
     lax.fori_loop(0, 4, sent, 0)
 
 
-def run_backward(slot_of, gates, ids, router, gain_one, gain_two, lse, segments, gate_grad, in_grad, produced,
+def run_backward(slot_of, gates, ids, router, gain_one, gain_two, lse, segments, gate_grad, in_grad, back_far, produced,
                  hidden, tokens, cotangent, normed, attended, normed_two, qkv, full_a, full_out):
+    table = jnp.concatenate(
+        [slot_of.T.astype(jnp.float32), ids.T.astype(jnp.float32), gates.T, segments[None].astype(jnp.float32),
+         jnp.zeros((1, segments.shape[0]), jnp.float32)], axis=0)
     sems = pltpu.SemaphoreType.DMA
     length, model = tokens.shape
     block = full_a.shape[0] // 8
@@ -994,14 +1075,16 @@
         out_shape=(
             jax.ShapeDtypeStruct((length, model), low),
             jax.ShapeDtypeStruct((length, model), f32),
-            jax.ShapeDtypeStruct((block, width_a), f32),
+            jax.ShapeDtypeStruct((block, width_b), f32),
+            jax.ShapeDtypeStruct((block, (width_a - width_b) // 2), f32),
+            jax.ShapeDtypeStruct((block, (width_a - width_b) // 2), f32),
             jax.ShapeDtypeStruct((block, width_b), f32),
             jax.ShapeDtypeStruct((16, span), f32),
         ),
-        in_specs=[vm] * 9 + [ANY] * 12,
-        out_specs=(vm,) * 5,
+        in_specs=[vm] * 5 + [ANY] * 13,
+        out_specs=(vm,) * 7,
         scratch_shapes=[
-            v((slots, model), low), v((8, 1, capacity), f32), v((slots, model), low),
+            v((length, 8), f32), v((slots, model), low), v((8, 1, capacity), f32), v((slots, model), low),
             v((length, model), f32), rows_low, rows_low, rows_low,
             v(qkv.shape, low), v(full_a.shape, low), v(full_out.shape, low),
             v((model, length), low), v((model, length), low), rows_low,
@@ -1010,7 +1093,7 @@
             v((4, 4, block, width), low), v((4, 4, block, width), low), v((4, 4, block, width), low),
             v((4, 2, 2, cut, width), low), v((4, 2, cut, width), low), v((3, block, width), low),
             v((7, 16, span), f32), v((16, span), f32), v((3, 16, span), f32),
-            sems((9,)), sems((7,)), sems((7,)), sems((7,)), sems((7,)), sems((7,)), sems((7,)), sems((3,)),
+            sems((9,)), sems((7,)), sems((7,)), sems((7,)), sems((7,)), sems((7,)), sems((7,)), sems((3,)), sems((2,)),
             sems((4, 4, 2)), sems((4, 4, 2)), sems((4, 2, 2, 3)), sems((4, 2, 2, 3)),
             sems((2, 3)), sems((2, 3)), sems((7,)), sems((7,)), sems((3,)), sems((3,)),
         ],
@@ -1018,9 +1101,8 @@
             collective_id=2, has_side_effects=True, vmem_limit_bytes=60 * 2**20
         ),
         cost_estimate=pl.CostEstimate(flops=0, bytes_accessed=1_000_000, transcendentals=0),
-    )(slot_of, gates, ids, router_p, gain_one[None], gain_two[None], lse, segments.reshape(1, length),
-      segments.reshape(length, 1), gate_grad, in_grad, produced, hidden, tokens, cotangent, normed, attended,
-      normed_two, qkv, full_a, full_out)
+    )(table, router_p, gain_one, gain_two, lse, gate_grad, in_grad, back_far, produced, hidden, tokens,
+      cotangent, normed, attended, normed_two, qkv, full_a, full_out)
 
 
 def rms_factor(rows_in):
@@ -1170,7 +1252,6 @@
     router_cols = router.shape[1]
 
     hidden_units = w_gate.shape[2]
-    own_gu = jnp.concatenate([w_gate[0], w_up[0]], axis=1)
     own_down = w_down[0]
 
     lane = 256
@@ -1184,17 +1265,17 @@
     own_s = jnp.pad(own_s, ((0, 16 - own_s.shape[0]), (0, 0)))
     own_a = jnp.concatenate([pair_heads(w_query), w_key, w_value], axis=1)
     if on_small_slice():
-        line_a, line_out, small, plane_upstream = gather_line(own_a, w_out, own_s, cotangent)
-        own_gu, own_down, line_a, line_out = lax.optimization_barrier(
-            (own_gu, own_down, line_a, line_out)
+        line_a, line_out, small, plane_upstream, own_gu = gather_line(
+            own_a, w_out, own_s, cotangent, w_gate[0], w_up[0]
         )
         full_a, full_out = gather_plane(3, (line_a, line_out))
     else:
+        own_gu = jnp.concatenate([w_gate[0], w_up[0]], axis=1)
         full_a, full_out, small, plane_upstream = gather_all(own_a, w_out, own_s, cotangent)
     full_gu = lax.all_gather(own_gu, "col", axis=0, tiled=True)
     full_router = small[:, :, :router_cols, :block].transpose(1, 3, 0, 2).reshape(model, experts)
-    gain_one = small[:, :, router_cols, :piece].transpose(1, 0, 2).reshape(model).astype(jnp.float32)
-    gain_two = small[:, :, router_cols + 1, :piece].transpose(1, 0, 2).reshape(model).astype(jnp.float32)
+    gain_one = small[:, :, router_cols, :piece].transpose(1, 0, 2).reshape(1, model).astype(jnp.float32)
+    gain_two = small[:, :, router_cols + 1, :piece].transpose(1, 0, 2).reshape(1, model).astype(jnp.float32)
 
     rows_f = tokens.astype(jnp.float32)
     factor_one = rms_factor(rows_f)
@@ -1241,32 +1322,35 @@
         axis=2,
     )
     if on_small_slice():
-        in_grad, produced, slot_gate_grad, grad_gu_local, grad_down = run_expert(
+        in_grad, produced, slot_gate_grad, grad_gu_local, grad_down, back_far = run_expert(
             jnp.where(routed, place, -1), mine, plane_normed, plane_upstream, full_gu, own_down
         )
         grad_gu = lax.psum_scatter(grad_gu_local, "col", scatter_dimension=0, tiled=True)
         lse = (row_max + jnp.log(totals)).reshape(KEY_VALUE_HEADS, 1, QUERY_PER_KEY * length)
-        output, d_tokens, sum_a, sum_out, sum_s = run_backward(
+        output, d_tokens, sum_q, sum_k, sum_v, sum_out, sum_s = run_backward(
             slot_of, gate_probs, expert_ids, full_router, gain_one, gain_two, lse, segments,
-            slot_gate_grad, in_grad, produced, hidden, tokens, cotangent, normed, attended, normed_two,
+            slot_gate_grad, in_grad, back_far, produced, hidden, tokens, cotangent, normed, attended, normed_two,
             flat_qkv, full_a, full_out,
         )
         core = lax.axis_index("row") % 2
         col = lax.axis_index("col")
         own_router = lax.dynamic_slice(sum_s, (col * router_cols, core * block), (router_cols, block))
         own_gains = lax.dynamic_slice(sum_s, (experts, core * block + col * piece), (2, piece))
+        output, d_tokens, sum_q, sum_k, sum_v, sum_out, grad_down, grad_gate, grad_up = finish(
+            (output, d_tokens, sum_q, sum_k, sum_v, sum_out, grad_down), grad_gu
+        )
         return (
             output,
             d_tokens,
             own_gains[0],
-            part_heads(sum_a[:, :width_q]),
-            sum_a[:, width_q : width_q + width_k],
-            sum_a[:, width_q + width_k :],
+            sum_q,
+            sum_k,
+            sum_v,
             sum_out,
             own_gains[1],
             own_router.T,
-            grad_gu[:, :hidden_units].astype(jnp.float32)[None],
-            grad_gu[:, hidden_units:].astype(jnp.float32)[None],
+            grad_gate[None],
+            grad_up[None],
             grad_down[None],
         )
     else:

time: 416 us -> 408 us (0.981)
  local copies, waits for them, and re-layouts: 27.6 us -> 18 us
  Pallas kernels: 349 us -> 355 us
  other arithmetic: 14.5 us -> 9.03 us
    pallas_call x0 -> x1, Pallas kernels: none -> 6.29 us  [finish(): pl.pallas_call(functools.partial(finish_kernel, len(arrays)), grid=(steps...]
    unnamed x44 -> x24, local copies, waits for them, and re-layouts: 9.69 us -> 4.1 us
  transfers between devices with their start and end apart: 2 -> 2, of which waited for: 0 -> 0; matrix products, arithmetic and copies ran while one was open for 9% -> 8% of each run, Pallas kernels for 56% -> 56%
where the time goes in v5:
time: 408 us; the launch traced here: 407 us
  Pallas kernels  355 us (87%)
  local copies, waits for them, and re-layouts  18 us (4%)
  between operations  14.5 us (4%)
  matrix products  10.1 us (2%)
  other arithmetic  9.03 us (2%)
    pallas_call x1, Pallas kernels, run_backward(): pl.pallas_call(backward_kernel, out_shape=(jax.ShapeDtypeStruct((length,...  140 us
    pallas_call x1, Pallas kernels, run_expert(): pl.pallas_call(expert_kernel, out_shape=(jax.ShapeDtypeStruct((slots, mod...  80 us
    pallas_call x1, Pallas kernels, gather_plane(): pl.pallas_call(functools.partial(plane_kernel, count), out_shape=tuple((j...  56.3 us
    pallas_call x1, Pallas kernels, gather_line(): pl.pallas_call(line_kernel, out_shape=(jax.ShapeDtypeStruct((own_a.shape[...  39.4 us
    pallas_call x1, Pallas kernels, spread_tokens(): pl.pallas_call(spread_kernel, out_shape=(jax.ShapeDtypeStruct((8 * own_c....  33.5 us
  transfers between devices with their start and end apart: 2, of which 0 were waited for; matrix products, arithmetic and copies ran while one was open for 8% of the time, Pallas kernels for 56%

profile of v5, /device:TPU:0, one launch (start us, length us, event | category | flops | bytes accessed | tf_op | source)
XLA Modules:
  0.0 406.9 jit_solution(8177230206567379273)
XLA Ops:
  7.2 1.0 copy.62
  8.4 0.7 fusion.15
  9.8 1.5 pad_maximum_fusion.own_a
  11.3 39.4 %shard_map.229 = (bf16[192,2560]{1,0:T(8,128)(2,1)}, bf16[192,1536]{1,0:T(8,128)(2,1)}, bf16[4,8,16,256]{3,2,1,0:T(8,128)(2,1)}, bf16[2048,1536]{1,0:T(8,128)(2,1)}, bf16[384,2048]{1,0:T(8,128)(2,1)}) custom-call(bf16[192,640]{1,0:T(8,128)(2,1)} %pad_maximum_fusion.own_a, bf16[192,384]{1,0:T(8,128)(2,1)} %own_b.1, bf16[16,256]{1,0:T(8,128)(2,1)} %pad.22.own_s, ...), custom_call_target="tpu_custom_call" | custom-call | bytes 1000000 | tf_op jit(solution)/shard_map/pallas_call | solution.py:227
  50.8 0.9 slice_convert_fusion
  51.8 56.3 %shard_map.230 = (bf16[1536,2560]{1,0:T(8,128)(2,1)}, bf16[1536,1536]{1,0:T(8,128)(2,1)}) custom-call(bf16[192,2560]{1,0:T(8,128)(2,1)} %get-tuple-element.44.refs_0_, bf16[192,1536]{1,0:T(8,128)(2,1)} %get-tuple-element.45.refs_1_), custom_call_target="tpu_custom_call" | custom-call | bytes 1000000 | tf_op jit(solution)/shard_map/pallas_call | solution.py:285
  108.7 0.9 copy-done.4
  109.6 5.5 %convolution_convert_fusion.qkv_hbm = bf16[256,2560]{1,0:T(8,128)(2,1)S(1)} fusion(bf16[256,1536]{1,0:T(8,128)(2,1)S(1)} %fusion.5.normed_hbm, bf16[1536,2560]{1,0:T(8,128)(2,1)} %get-tuple-element.46.full_a_hbm), kind=kOutput, calls=%fused_computation.5 | convolution fusion | flops 2013921280 | bytes 9961472 | tf_op jit(solution)/shard_map/dot_general | solution.py:1113
  115.6 1.2 slice.51
  116.7 1.0 fusion.20
  117.7 1.1 copy.67
  118.9 1.5 copy.83
  120.8 0.9 slice_bitcast_fusion
  121.9 1.1 fusion.1
  123.0 1.4 fusion
  124.4 1.8 fusion.6
  126.6 1.5 multiply_reduce_fusion
  128.9 0.6 select_bitcast_fusion.own_g
  129.5 33.5 %shard_map.231 = (bf16[2048,1536]{1,0:T(8,128)(2,1)}, f32[8,8,256]{2,1,0:T(8,128)}) custom-call(bf16[256,1536]{1,0:T(8,128)(2,1)} %copy-done.2, f32[8,256]{1,0:T(8,128)} %select_bitcast_fusion.own_g), custom_call_target="tpu_custom_call" | custom-call | bytes 1000000 | tf_op jit(solution)/shard_map/pallas_call | solution.py:326
  163.0 0.9 compare_convert_fusion
  164.9 0.6 compare_select_fusion.key
  165.5 80.0 %shard_map.232 = (bf16[1024,1536]{1,0:T(8,128)(2,1)}, bf16[1024,1536]{1,0:T(8,128)(2,1)}, f32[8,1,128]{2,1,0:T(1,128)}, bf16[1536,2048]{1,0:T(8,128)(2,1)}, f32[...) custom-call(s32[8,1,256]{2,1,0:T(1,128)} %compare_select_fusion.key, f32[8,1,256]{2,1,0:T(1,128)} %copy-done.6, ...), custom_call_target="tpu_custom_call" | custom-call | bytes 1000000 | tf_op jit(solution)/shard_map/pallas_call | solution.py:647
  245.5 1.2 copy.79.attended_hbm
  246.7 0.7 reshape.232.gain_one
  247.4 0.7 reshape.233.gain_two
  249.2 0.6 add.104.lse
  249.8 0.8 pad.23.router_p
  250.8 0.6 concatenate.11.table
  251.4 139.6 %shard_map.233 = (bf16[256,1536]{1,0:T(8,128)(2,1)}, f32[256,1536]{1,0:T(8,128)}, f32[192,384]{1,0:T(8,128)}, f32[192,128]{1,0:T(8,128)}, f32[192,128]{1,0:T(8,1...) custom-call(f32[8,256]{1,0:T(8,128)} %concatenate.11.table, bf16[1536,128]{1,0:T(8,128)(2,1)} %pad.23.router_p, ...), custom_call_target="tpu_custom_call" | custom-call | bytes 1000000 | tf_op jit(solution)/shard_map/pallas_call | solution.py:1073
  391.1 0.8 constant_dynamic-slice_fusion
  391.8 1.4 dynamic-slice_bitcast_fusion
  393.7 6.3 %shard_map.234 = (bf16[256,1536]{1,0:T(8,128)(2,1)}, f32[256,1536]{1,0:T(8,128)}, f32[192,384]{1,0:T(8,128)}, f32[192,128]{1,0:T(8,128)}, f32[192,128]{1,0:T(8,1...) custom-call(bf16[256,1536]{1,0:T(8,128)(2,1)} %get-tuple-element.56.refs_0_, ...), custom_call_target="tpu_custom_call" | custom-call | tf_op jit(solution)/shard_map/pallas_call | solution.py:368
  (75 shorter events, 6.4 us)
Async XLA Ops:
  7.2 158.3 %all-gather.2.cloned.1.call-start = ((), (), s32[]{:S(2)}) async-start(), calls=%async_computation.1 | async-start | bytes 7864320 | tf_op jit(solution)/shard_map/all_gather | solution.py:1275
  11.3 96.8 %copy-start.1 = (bf16[256,1536]{1,0:T(8,128)(2,1)S(1)}, bf16[256,1536]{1,0:T(8,128)(2,1)}, u32[]{:S(2)}) copy-start(bf16[256,1536]{1,0:T(8,128)(2,1)} %tokens_hbm.1) | copy-start | bytes 2359300
  50.7 343.0 %reduce-scatter.2.cloned.1.call-start = ((), (), s32[]{:S(2)}) async-start(), calls=%async_computation.2 | async-start | bytes 7864320 | tf_op jit(solution)/shard_map/reduce_scatter | solution.py:1328
  108.7 0.9 copy-start.4
  115.0 5.4 %copy-start.3 = (bf16[256,2560]{1,0:T(8,128)(2,1)}, bf16[256,2560]{1,0:T(8,128)(2,1)S(1)}, u32[]{:S(2)}) copy-start(bf16[256,2560]{1,0:T(8,128)(2,1)S(1)} %convolution_convert_fusion.qkv_hbm) | copy-start | bytes 3932164
  115.6 6.3 %copy-start.8 = (s32[1,256]{1,0:T(1,128)S(1)}, s32[1,256]{1,0:T(1,128)}, u32[]{:S(2)}) copy-start(s32[1,256]{1,0:T(1,128)} %param.25) | copy-start | bytes 3076
  117.7 2.8 copy-start.5
  123.0 3.1 slice-start
  124.4 2.2 slice-start.1
  128.1 117.4 %copy-start = (f32[256,1536]{1,0:T(8,128)}, f32[256,1536]{1,0:T(8,128)S(1)}, u32[]{:S(2)}) copy-start(f32[256,1536]{1,0:T(8,128)S(1)} %get-tuple-element.85.hidden_hbm) | copy-start | bytes 4718596
  128.1 0.7 copy-start.7
  128.3 1.2 copy-start.2
  163.9 1.6 copy-start.6
Sparse Core Ops, SparseCore 0:
  50.9 114.0 all-gather.1
  245.6 132.9 reduce-scatter.1

commit v6 on v5

--- a/solution.py
+++ b/solution.py
@@ -349,29 +349,49 @@
     lax.fori_loop(0, target.shape[0] // 32, body, 0)
 
 
-def finish_kernel(count, *refs):
-    for source, target in zip(refs[:count], refs[count + 1 : 2 * count + 1]):
+def finish_kernel(count, experts, block, piece, *refs):
+    for source, target in zip(refs[:count], refs[count + 2 : 2 * count + 2]):
         target[...] = source[...]
-    gu, gate, up = refs[count], refs[2 * count + 1], refs[2 * count + 2]
+    gu, sums = refs[count : count + 2]
+    gate, up, router, gain_a, gain_e, turned = refs[2 * count + 2 :]
     gate[...] = gu[:, : gate.shape[1]].astype(gate.dtype)
     up[...] = gu[:, gate.shape[1] :].astype(up.dtype)
 
-
-def finish(arrays, grad_gu):
+    @pl.when(pl.program_id(0) == 0)
+    def _():
+        core, col = lax.axis_index("row") % 2, lax.axis_index("col")
+        turned[...] = sums[...].T
+        mine = turned[pl.ds(pl.multiple_of(core * block, 8), block), :].T
+        rows = lax.broadcasted_iota(jnp.int32, mine.shape, 0)
+        for j in range(router.shape[0]):
+            at = col * router.shape[0] + j
+            router[j : j + 1, :] = jnp.sum(jnp.where(rows == at, mine, 0.0), axis=0, keepdims=True)
+        own = turned[pl.ds(pl.multiple_of(core * block + col * piece, 8), piece), :].T
+        gain_a[...] = own[experts : experts + 1, :]
+        gain_e[...] = own[experts + 1 : experts + 2, :]
+
+
+def finish(arrays, grad_gu, sums, block, piece, router_cols):
     steps = 4
-
-    def spec(a, columns=None):
-        return pl.BlockSpec((a.shape[0] // steps, columns or a.shape[1]), lambda i: (i, 0))
-
-    units = grad_gu.shape[1] // 2
-    half = jax.ShapeDtypeStruct((grad_gu.shape[0], units), jnp.float32)
+    experts = router_cols * 4
+
+    def spec(a):
+        return pl.BlockSpec((a.shape[0] // steps, a.shape[1]), lambda i: (i, 0))
+
+    def once(a):
+        return pl.BlockSpec(a.shape, lambda i: (0, 0))
+
+    f32 = jnp.float32
+    half = jax.ShapeDtypeStruct((grad_gu.shape[0], grad_gu.shape[1] // 2), f32)
+    small = [jax.ShapeDtypeStruct(shape, f32) for shape in ((router_cols, block), (1, piece), (1, piece))]
     return pl.pallas_call(
-        functools.partial(finish_kernel, len(arrays)),
+        functools.partial(finish_kernel, len(arrays), experts, block, piece),
         grid=(steps,),
-        out_shape=tuple(jax.ShapeDtypeStruct(a.shape, a.dtype) for a in arrays) + (half, half),
-        in_specs=[spec(a) for a in arrays] + [spec(grad_gu)],
-        out_specs=tuple(spec(a) for a in arrays) + (spec(half), spec(half)),
-    )(*arrays, grad_gu)
+        out_shape=(*(jax.ShapeDtypeStruct(a.shape, a.dtype) for a in arrays), half, half, *small),
+        in_specs=[*(spec(a) for a in arrays), spec(grad_gu), once(sums)],
+        out_specs=(*(spec(a) for a in arrays), spec(half), spec(half), *(once(a) for a in small)),
+        scratch_shapes=[pltpu.VMEM((sums.shape[1], sums.shape[0]), f32)],
+    )(*arrays, grad_gu, sums)
 
 
 def expert_kernel(key, mine, normed_hbm, upstream_hbm, gu_hbm, own_down,
@@ -681,7 +701,7 @@
     )(key.reshape(sources, 1, length), mine.reshape(sources, 1, length), normed, upstream, full_gu, own_down)
 
 
-def backward_kernel(table, router_p, gain_one, gain_two, lse,
+def backward_kernel(table, router_p, gains, lse,
                     gate_grad, in_grad, back_far, produced, hidden_hbm, tokens_hbm, cot_hbm, normed_hbm, attended_hbm,
                     two_hbm, qkv_hbm, full_a_hbm, full_out_hbm,
                     out_ref, d_tokens, sum_q, sum_k, sum_v, sum_b, sum_s,
@@ -720,7 +740,7 @@
     loads = [
         pltpu.make_async_copy(source, target, load.at[i])
         for i, (source, target) in enumerate((
-            (normed_hbm, branch), (attended_hbm, out_ref), (hidden_hbm, hidden), (cot_hbm, cot), (two_hbm, two),
+            (normed_hbm, branch), (attended_hbm, a_t), (hidden_hbm, hidden), (cot_hbm, cot), (two_hbm, two),
             (qkv_hbm, qkv), (tokens_hbm, tokens), (full_out_hbm, full_out), (full_a_hbm, full_a),
         ))
     ]
@@ -760,14 +780,12 @@
         copy.start()
     loads[0].wait()
     n_t[...] = branch[...].T
-    loads[1].wait()
-    a_t[...] = out_ref[...].T
     key_pos = lax.broadcasted_iota(jnp.int32, (length, length), 0)
     query_pos = lax.broadcasted_iota(jnp.int32, (length, length), 1)
     allowed = (key_pos <= query_pos) & (cols[:, 6:7] == table[6:7, :])
     bias[...] = jnp.where(allowed, 0.0, NEGATIVE)
     small[...] = jnp.zeros_like(small)
-    for copy in loads[2:]:
+    for copy in loads[1:]:
         copy.wait()
     for copy in (own_in, own_gate, *far_in):
         copy.wait()
@@ -799,7 +817,7 @@
         h = hidden[rows, :]
         factor = lax.rsqrt(jnp.mean(h * h, axis=1, keepdims=True) + EPSILON)
         small[9:10, :] += jnp.sum(two_grad * h * factor, axis=0, keepdims=True)
-        scaled = two_grad * gain_two[...]
+        scaled = two_grad * gains[1:2, :]
         inner = jnp.mean(scaled * h, axis=1, keepdims=True)
         grad = cot[rows, :].astype(f32) + factor * scaled - h * (factor * factor * factor * inner)
         d_tokens[rows, :] = grad
@@ -953,7 +971,7 @@
         x = tokens[rows, :].astype(f32)
         factor = lax.rsqrt(jnp.mean(x * x, axis=1, keepdims=True) + EPSILON)
         small[8:9, :] += jnp.sum(grad * x * factor, axis=0, keepdims=True)
-        scaled = grad * gain_one[...]
+        scaled = grad * gains[0:1, :]
         inner = jnp.mean(scaled * x, axis=1, keepdims=True)
         d_tokens[rows, :] += factor * scaled - x * (factor * factor * factor * inner)
         return carry
@@ -1051,7 +1069,7 @@
     lax.fori_loop(0, 4, sent, 0)
 
 
-def run_backward(slot_of, gates, ids, router, gain_one, gain_two, lse, segments, gate_grad, in_grad, back_far, produced,
+def run_backward(slot_of, gates, ids, router, gains, lse, segments, gate_grad, in_grad, back_far, produced,
                  hidden, tokens, cotangent, normed, attended, normed_two, qkv, full_a, full_out):
     table = jnp.concatenate(
         [slot_of.T.astype(jnp.float32), ids.T.astype(jnp.float32), gates.T, segments[None].astype(jnp.float32),
@@ -1081,7 +1099,7 @@
             jax.ShapeDtypeStruct((block, width_b), f32),
             jax.ShapeDtypeStruct((16, span), f32),
         ),
-        in_specs=[vm] * 5 + [ANY] * 13,
+        in_specs=[vm] * 4 + [ANY] * 13,
         out_specs=(vm,) * 7,
         scratch_shapes=[
             v((length, 8), f32), v((slots, model), low), v((8, 1, capacity), f32), v((slots, model), low),
@@ -1101,7 +1119,7 @@
             collective_id=2, has_side_effects=True, vmem_limit_bytes=60 * 2**20
         ),
         cost_estimate=pl.CostEstimate(flops=0, bytes_accessed=1_000_000, transcendentals=0),
-    )(table, router_p, gain_one, gain_two, lse, gate_grad, in_grad, back_far, produced, hidden, tokens,
+    )(table, router_p, gains, lse, gate_grad, in_grad, back_far, produced, hidden, tokens,
       cotangent, normed, attended, normed_two, qkv, full_a, full_out)
 
 
@@ -1127,9 +1145,9 @@
 
 def pair_heads(a):
     if not on_small_slice():
-        return a
-    a = a.reshape(a.shape[0], -1, 2, QUERY_PER_KEY, HEAD_SIZE)
-    return a.transpose(0, 1, 3, 2, 4).reshape(a.shape[0], -1)
+        return [a]
+    heads = [a[:, i * HEAD_SIZE : (i + 1) * HEAD_SIZE] for i in range(a.shape[1] // HEAD_SIZE)]
+    return [heads[u * QUERY_PER_KEY + i] for i in range(QUERY_PER_KEY) for u in range(2)]
 
 
 def part_heads(a):
@@ -1256,14 +1274,15 @@
 
     lane = 256
 
-    def row_of(v):
-        return jnp.pad(v, ((0, 0), (0, lane - v.shape[1])))
-
-    own_s = jnp.concatenate(
-        [row_of(router.T), row_of(attn_gain[None]), row_of(expert_gain[None])], axis=0
-    )
-    own_s = jnp.pad(own_s, ((0, 16 - own_s.shape[0]), (0, 0)))
-    own_a = jnp.concatenate([pair_heads(w_query), w_key, w_value], axis=1)
+    def at_row(v, row):
+        return jnp.pad(v, ((row, 16 - row - v.shape[0]), (0, lane - v.shape[1])))
+
+    own_s = (
+        at_row(router.T, 0)
+        + at_row(attn_gain[None], router_cols)
+        + at_row(expert_gain[None], router_cols + 1)
+    )
+    own_a = jnp.concatenate([*pair_heads(w_query), w_key, w_value], axis=1)
     if on_small_slice():
         line_a, line_out, small, plane_upstream, own_gu = gather_line(
             own_a, w_out, own_s, cotangent, w_gate[0], w_up[0]
@@ -1274,8 +1293,10 @@
         full_a, full_out, small, plane_upstream = gather_all(own_a, w_out, own_s, cotangent)
     full_gu = lax.all_gather(own_gu, "col", axis=0, tiled=True)
     full_router = small[:, :, :router_cols, :block].transpose(1, 3, 0, 2).reshape(model, experts)
-    gain_one = small[:, :, router_cols, :piece].transpose(1, 0, 2).reshape(1, model).astype(jnp.float32)
-    gain_two = small[:, :, router_cols + 1, :piece].transpose(1, 0, 2).reshape(1, model).astype(jnp.float32)
+    gains = (
+        small[:, :, router_cols : router_cols + 2, :piece].transpose(2, 1, 0, 3).reshape(2, model).astype(jnp.float32)
+    )
+    gain_one, gain_two = gains[0:1], gains[1:2]
 
     rows_f = tokens.astype(jnp.float32)
     factor_one = rms_factor(rows_f)
@@ -1328,26 +1349,22 @@
         grad_gu = lax.psum_scatter(grad_gu_local, "col", scatter_dimension=0, tiled=True)
         lse = (row_max + jnp.log(totals)).reshape(KEY_VALUE_HEADS, 1, QUERY_PER_KEY * length)
         output, d_tokens, sum_q, sum_k, sum_v, sum_out, sum_s = run_backward(
-            slot_of, gate_probs, expert_ids, full_router, gain_one, gain_two, lse, segments,
-            slot_gate_grad, in_grad, back_far, produced, hidden, tokens, cotangent, normed, attended, normed_two,
+            slot_of, gate_probs, expert_ids, full_router, gains, lse, segments,
+            slot_gate_grad, in_grad, back_far, produced, hidden, tokens, cotangent, normed, attended.T, normed_two,
             flat_qkv, full_a, full_out,
         )
-        core = lax.axis_index("row") % 2
-        col = lax.axis_index("col")
-        own_router = lax.dynamic_slice(sum_s, (col * router_cols, core * block), (router_cols, block))
-        own_gains = lax.dynamic_slice(sum_s, (experts, core * block + col * piece), (2, piece))
-        output, d_tokens, sum_q, sum_k, sum_v, sum_out, grad_down, grad_gate, grad_up = finish(
-            (output, d_tokens, sum_q, sum_k, sum_v, sum_out, grad_down), grad_gu
+        output, d_tokens, sum_q, sum_k, sum_v, sum_out, grad_down, grad_gate, grad_up, own_router, gain_a, gain_e = finish(
+            (output, d_tokens, sum_q, sum_k, sum_v, sum_out, grad_down), grad_gu, sum_s, block, piece, router_cols
         )
         return (
             output,
             d_tokens,
-            own_gains[0],
+            gain_a.reshape(piece),
             sum_q,
             sum_k,
             sum_v,
             sum_out,
-            own_gains[1],
+            gain_e.reshape(piece),
             own_router.T,
             grad_gate[None],
             grad_up[None],

time: 408 us -> 405 us (level)
  transfers between devices with their start and end apart: 2 -> 2, of which waited for: 0 -> 0; matrix products, arithmetic and copies ran while one was open for 8% -> 7% of each run, Pallas kernels for 56% -> 57%
where the time goes in v6:
time: 405 us
  Pallas kernels  357 us (88%)
  local copies, waits for them, and re-layouts  14.5 us (4%)
  between operations  14.5 us (4%)
  matrix products  10.1 us (2%)
  other arithmetic  7.95 us (2%)
    pallas_call x1, Pallas kernels, run_backward(): pl.pallas_call(backward_kernel, out_shape=(jax.ShapeDtypeStruct((length,...  142 us
    pallas_call x1, Pallas kernels, run_expert(): pl.pallas_call(expert_kernel, out_shape=(jax.ShapeDtypeStruct((slots, mod...  80 us
    pallas_call x1, Pallas kernels, gather_plane(): pl.pallas_call(functools.partial(plane_kernel, count), out_shape=tuple((j...  56.3 us
    pallas_call x1, Pallas kernels, gather_line(): pl.pallas_call(line_kernel, out_shape=(jax.ShapeDtypeStruct((own_a.shape[...  39.4 us
    pallas_call x1, Pallas kernels, spread_tokens(): pl.pallas_call(spread_kernel, out_shape=(jax.ShapeDtypeStruct((8 * own_c....  33.5 us
  transfers between devices with their start and end apart: 2, of which 0 were waited for; matrix products, arithmetic and copies ran while one was open for 7% of the time, Pallas kernels for 57%

profile of v6, /device:TPU:0, one launch (start us, length us, event | category | flops | bytes accessed | tf_op | source)
XLA Modules:
  0.0 404.6 jit_solution(5449570074988232856)
XLA Ops:
  7.2 1.0 fusion.15
  8.3 1.3 pad_add_fusion.own_s
  9.6 1.7 concatenate.6.own_a
  11.3 39.4 %shard_map.229 = (bf16[192,2560]{1,0:T(8,128)(2,1)}, bf16[192,1536]{1,0:T(8,128)(2,1)}, bf16[4,8,16,256]{3,2,1,0:T(8,128)(2,1)}, bf16[2048,1536]{1,0:T(8,128)(2,1)}, bf16[384,2048]{1,0:T(8,128)(2,1)}) custom-call(bf16[192,640]{1,0:T(8,128)(2,1)} %concatenate.6.own_a, bf16[192,384]{1,0:T(8,128)(2,1)} %own_b.1, bf16[16,256]{1,0:T(8,128)(2,1)} %pad_add_fusion.own_s, ...), custom_call_target="tpu_custom_call" | custom-call | bytes 1000000 | tf_op jit(solution)/shard_map/pallas_call | solution.py:227
  50.7 0.9 convert_bitcast_fusion
  51.7 56.3 %shard_map.230 = (bf16[1536,2560]{1,0:T(8,128)(2,1)}, bf16[1536,1536]{1,0:T(8,128)(2,1)}) custom-call(bf16[192,2560]{1,0:T(8,128)(2,1)} %get-tuple-element.47.refs_0_, bf16[192,1536]{1,0:T(8,128)(2,1)} %get-tuple-element.48.refs_1_), custom_call_target="tpu_custom_call" | custom-call | bytes 1000000 | tf_op jit(solution)/shard_map/pallas_call | solution.py:285
  108.6 0.9 copy-done.5
  109.4 5.5 %convolution_convert_fusion.qkv_hbm = bf16[256,2560]{1,0:T(8,128)(2,1)S(1)} fusion(bf16[256,1536]{1,0:T(8,128)(2,1)S(1)} %fusion.5.normed_hbm, bf16[1536,2560]{1,0:T(8,128)(2,1)} %get-tuple-element.49.full_a_hbm), kind=kOutput, calls=%fused_computation.5 | convolution fusion | flops 2013921280 | bytes 9961472 | tf_op jit(solution)/shard_map/dot_general | solution.py:1131
  114.9 0.5 reshape.186
  115.5 1.2 slice.74
  116.6 1.0 fusion.14
  117.6 1.1 copy.56
  118.7 1.5 copy.70
  120.7 0.9 slice_bitcast_fusion
  121.8 1.1 fusion.1
  122.9 1.4 fusion
  124.3 1.8 fusion.6
  126.1 0.4 slice-done.1
  126.5 1.5 multiply_reduce_fusion
  128.8 0.6 select_bitcast_fusion.own_g
  129.4 33.5 %shard_map.231 = (bf16[2048,1536]{1,0:T(8,128)(2,1)}, f32[8,8,256]{2,1,0:T(8,128)}) custom-call(bf16[256,1536]{1,0:T(8,128)(2,1)} %copy-done.2, f32[8,256]{1,0:T(8,128)} %select_bitcast_fusion.own_g), custom_call_target="tpu_custom_call" | custom-call | bytes 1000000 | tf_op jit(solution)/shard_map/pallas_call | solution.py:326
  162.9 0.9 compare_convert_fusion
  163.8 0.6 reduce-window.16
  164.8 0.6 compare_select_fusion.key
  165.4 80.0 %shard_map.232 = (bf16[1024,1536]{1,0:T(8,128)(2,1)}, bf16[1024,1536]{1,0:T(8,128)(2,1)}, f32[8,1,128]{2,1,0:T(1,128)}, bf16[1536,2048]{1,0:T(8,128)(2,1)}, f32[...) custom-call(s32[8,1,256]{2,1,0:T(1,128)} %compare_select_fusion.key, f32[8,1,256]{2,1,0:T(1,128)} %copy-done.7, ...), custom_call_target="tpu_custom_call" | custom-call | bytes 1000000 | tf_op jit(solution)/shard_map/pallas_call | solution.py:667
  245.7 0.6 add.89.lse
  246.4 0.6 reduce-window.14
  247.2 0.7 convert_element_type.82.gains
  247.9 0.8 pad.19.router_p
  248.9 0.6 concatenate.7.table
  249.5 141.5 %shard_map.233 = (bf16[256,1536]{1,0:T(8,128)(2,1)}, f32[256,1536]{1,0:T(8,128)}, f32[192,384]{1,0:T(8,128)}, f32[192,128]{1,0:T(8,128)}, f32[192,128]{1,0:T(8,1...) custom-call(f32[8,256]{1,0:T(8,128)} %concatenate.7.table, bf16[1536,128]{1,0:T(8,128)(2,1)} %pad.19.router_p, ...), custom_call_target="tpu_custom_call" | custom-call | bytes 1000000 | tf_op jit(solution)/shard_map/pallas_call | solution.py:1091
  391.0 6.7 %shard_map.234 = (bf16[256,1536]{1,0:T(8,128)(2,1)}, f32[256,1536]{1,0:T(8,128)}, f32[192,384]{1,0:T(8,128)}, f32[192,128]{1,0:T(8,128)}, f32[192,128]{1,0:T(8,1...) custom-call(bf16[256,1536]{1,0:T(8,128)(2,1)} %get-tuple-element.59., ...), custom_call_target="tpu_custom_call" | custom-call | tf_op jit(solution)/shard_map/pallas_call | solution.py:387
  (71 shorter events, 3.1 us)
Async XLA Ops:
  7.2 158.2 %all-gather.2.cloned.1.call-start = ((), (), s32[]{:S(2)}) async-start(), calls=%async_computation.1 | async-start | bytes 7864320 | tf_op jit(solution)/shard_map/all_gather | solution.py:1294
  11.3 96.8 %copy-start.1 = (bf16[256,1536]{1,0:T(8,128)(2,1)S(1)}, bf16[256,1536]{1,0:T(8,128)(2,1)}, u32[]{:S(2)}) copy-start(bf16[256,1536]{1,0:T(8,128)(2,1)} %tokens_hbm.1) | copy-start | bytes 2359300
  50.7 340.4 %reduce-scatter.2.cloned.1.call-start = ((), (), s32[]{:S(2)}) async-start(), calls=%async_computation.2 | async-start | bytes 7864320 | tf_op jit(solution)/shard_map/reduce_scatter | solution.py:1349
  108.6 0.9 copy-start.5
  114.9 5.4 %copy-start.4 = (bf16[256,2560]{1,0:T(8,128)(2,1)}, bf16[256,2560]{1,0:T(8,128)(2,1)S(1)}, u32[]{:S(2)}) copy-start(bf16[256,2560]{1,0:T(8,128)(2,1)S(1)} %convolution_convert_fusion.qkv_hbm) | copy-start | bytes 3932164
  115.5 6.3 %copy-start.9 = (s32[1,256]{1,0:T(1,128)S(1)}, s32[1,256]{1,0:T(1,128)}, u32[]{:S(2)}) copy-start(s32[1,256]{1,0:T(1,128)} %param.25) | copy-start | bytes 3076
  117.6 2.8 copy-start.6
  122.9 3.2 slice-start
  124.3 2.2 slice-start.1
  126.1 1.9 copy-start.3
  128.0 117.4 %copy-start = (f32[256,1536]{1,0:T(8,128)}, f32[256,1536]{1,0:T(8,128)S(1)}, u32[]{:S(2)}) copy-start(f32[256,1536]{1,0:T(8,128)S(1)} %get-tuple-element.95.hidden_hbm) | copy-start | bytes 4718596
  128.0 0.7 copy-start.8
  128.2 1.2 copy-start.2
  163.8 1.6 copy-start.7
Sparse Core Ops, SparseCore 0:
  50.8 113.9 all-gather.1
  245.5 134.3 reduce-scatter.1

commit v7 on v6

--- a/solution.py
+++ b/solution.py
@@ -165,22 +165,20 @@
     from_gu = pltpu.make_async_copy(mid_gu, own_gu, loc.at[6])
     greet(range(1, 8), (1, 2, 3))
 
-    def along(c, source_a, source_b, right, left):
+    def along(i, c, source, target, right, left):
         for d, (cond, step) in enumerate(((right, 1), (left, 3))):
             @pl.when(cond)
             def _():
-                there = {"col": (col + step) % 4}
-                remote(source_a, of_a(c), zss.at[0, c, d], zrs.at[0, c], there).start()
-                remote(source_b, of_b(c), zss.at[1, c, d], zrs.at[1, c], there).start()
+                remote(source, target, zss.at[i, c, d], zrs.at[i, c], {"col": (col + step) % 4}).start()
 
     def arrived(k):
         c = unit_order(col, k)
-        there = {"col": (col + 1) % 4}
-        remote(of_a(c), of_a(c), zss.at[0, c, 0], zrs.at[0, c], there).wait_recv()
-        remote(of_b(c), of_b(c), zss.at[1, c, 0], zrs.at[1, c], there).wait_recv()
-        along(c, of_a(c), of_b(c), (c < col) & (col < 3), (c > col) & (col > 0))
-
-    along(col, own_a, own_b, col < 3, col > 0)
+        for i, view in enumerate((of_a(c), of_b(c))):
+            remote(view, view, zss.at[i, c, 0], zrs.at[i, c], {"col": (col + 1) % 4}).wait_recv()
+            along(i, c, view, view, (c < col) & (col < 3), (c > col) & (col > 0))
+
+    along(0, col, own_a, of_a(col), col < 3, col > 0)
+    along(1, col, own_b, of_b(col), col < 3, col > 0)
     for i, step in enumerate((1, 2, 3)):
         remote(own_s, full_s.at[col, row], s_zs.at[i], s_zr.at[i], {"col": (col + step) % 4}).start()
     plane_send(vc, row, csv, crv, own_c)
@@ -372,7 +370,7 @@
 
 
 def finish(arrays, grad_gu, sums, block, piece, router_cols):
-    steps = 4
+    steps = 2
     experts = router_cols * 4
 
     def spec(a):
@@ -395,9 +393,9 @@
 
 
 def expert_kernel(key, mine, normed_hbm, upstream_hbm, gu_hbm, own_down,
-                  in_ref, prod_ref, gate_grad_out, grad_gu, sum_down, back_far,
-                  gate_grad_ref, x_t, ups, gu, down, act, silu, slope, both, gd, rec_right, rec_left, stage, gate,
-                  load_sem, src_sem, stage_sem, zss, zrs, rss, rrs, fss, frs):
+                  in_out, prod_out, gate_grad_out, grad_gu, sum_down, back_far,
+                  in_ref, prod_ref, gate_grad_ref, x_t, ups, gu, down, act, silu, slope, both, gd, rec_right, rec_left, stage, gate,
+                  load_sem, src_sem, stage_sem, zss, zrs, rss, rrs, fss, frs, in_sem, prod_sem):
     row, col = lax.axis_index("row"), lax.axis_index("col")
     sources, _, length = key.shape
     slots = in_ref.shape[0]
@@ -553,10 +551,15 @@
         rows = pl.ds(pl.multiple_of(there * capacity, 16), capacity)
         return remote(in_ref.at[rows, :], back_far.at[j], fss.at[j], frs.at[j], {"row": there})
 
-    def inputs(i, carry):
+    def of_chip(i):
         chip = row_at(row, 2 * (3 - i)) // 2
         rows = pl.ds(pl.multiple_of(chip * 2 * capacity, 16), 2 * capacity)
+        return rows, pltpu.make_async_copy(in_ref.at[rows, :], in_out.at[rows, :], in_sem.at[i])
+
+    def inputs(i, carry):
+        rows, copy = of_chip(i)
         in_ref[rows, :] = dot_t(both[rows, :], gu[...]).astype(in_ref.dtype)
+        copy.start()
         return carry
 
     def backward(k):
@@ -617,6 +620,7 @@
         for c in range(1, 4):
             total = total + dot(act[rows, c * width : (c + 1) * width], down[c])
         prod_ref[rows, :] = total.astype(prod_ref.dtype)
+        pltpu.make_async_copy(prod_ref.at[rows, :], prod_out.at[rows, :], prod_sem.at[m]).start()
         return carry
     lax.fori_loop(0, slots // chunk, outputs, 0)
 
@@ -654,6 +658,13 @@
     lax.fori_loop(0, 4, sent, 0)
     for j in range(2):
         far(j).wait()
+
+    def written(i, carry):
+        of_chip(i)[1].wait()
+        rows = pl.ds(pl.multiple_of(i * chunk, chunk), chunk)
+        pltpu.make_async_copy(prod_ref.at[rows, :], prod_out.at[rows, :], prod_sem.at[i]).wait()
+        return carry
+    lax.fori_loop(0, 4, written, 0)
 
 
 def run_expert(key, mine, normed, upstream, full_gu, own_down):
@@ -675,8 +686,10 @@
             jax.ShapeDtypeStruct((2, slots // sources, model), low),
         ),
         in_specs=[vm, vm, ANY, ANY, ANY, ANY],
-        out_specs=(vm, vm, vm, ANY, vm, ANY),
+        out_specs=(ANY, ANY, vm, ANY, vm, ANY),
         scratch_shapes=[
+            pltpu.VMEM((slots, model), low),
+            pltpu.VMEM((slots, model), low),
             pltpu.VMEM((slots, 128), f32),
             pltpu.VMEM((model, slots), low),
             pltpu.VMEM((slots, model), low),
@@ -692,7 +705,7 @@
             pltpu.VMEM((2, model, 2 * width), low),
             pltpu.VMEM((slots, 128), f32),
             sems((2,)), sems((2, 2)), sems((2, 2)),
-            sems((4, 2)), sems((4,)), sems((2, 3)), sems((2, 3)), sems((2,)), sems((2,)),
+            sems((4, 2)), sems((4,)), sems((2, 3)), sems((2, 3)), sems((2,)), sems((2,)), sems((4,)), sems((4,)),
         ],
         compiler_params=pltpu.CompilerParams(
             collective_id=4, has_side_effects=True, vmem_limit_bytes=60 * 2**20
@@ -704,11 +717,11 @@
 def backward_kernel(table, router_p, gains, lse,
                     gate_grad, in_grad, back_far, produced, hidden_hbm, tokens_hbm, cot_hbm, normed_hbm, attended_hbm,
                     two_hbm, qkv_hbm, full_a_hbm, full_out_hbm,
-                    out_ref, d_tokens, sum_q, sum_k, sum_v, sum_b, sum_s,
-                    cols, rec_in, rec_gate, rec_prod, hidden, tokens, cot, two, qkv, full_a, full_out,
+                    out_hbm, d_hbm, sum_q, sum_k, sum_v, sum_b, sum_s,
+                    out_ref, d_tokens, cols, rec_in, rec_gate, rec_prod, hidden, tokens, cot, two, qkv, full_a, full_out,
                     n_t, a_t, branch, bias, out_rows, grad_c, qg, lgs, small,
                     own, sib_out, rec_sib, rec_one, rec_two, rec_z, s_rec, s_mid, s_zrec,
-                    load, in_ss, in_rs, g_ss, g_rs, pr_ss, pr_rs, loc, far_sem,
+                    load, in_ss, in_rs, g_ss, g_rs, pr_ss, pr_rs, loc, far_sem, write,
                     ss1, rs1, ss2, rs2, zss, zrs, s_ss, s_rs, sz_ss, sz_rs):
     row, col = lax.axis_index("row"), lax.axis_index("col")
     core = row % 2
@@ -976,6 +989,8 @@
         d_tokens[rows, :] += factor * scaled - x * (factor * factor * factor * inner)
         return carry
     lax.fori_loop(0, 2, to_tokens, 0)
+    write_tokens = pltpu.make_async_copy(d_tokens, d_hbm, write.at[0])
+    write_tokens.start()
 
     span = s_mid.shape[1]
 
@@ -1013,6 +1028,8 @@
         out_ref[rows, :] = total.astype(low)
         return carry
     lax.fori_loop(0, 2, to_output, 0)
+    write_output = pltpu.make_async_copy(out_ref, out_hbm, write.at[1])
+    write_output.start()
 
     total = s_mid[...]
     for step in (1, 2, 3):
@@ -1041,6 +1058,8 @@
         return carry
     lax.fori_loop(0, block // 32, to_sums, 0)
 
+    write_tokens.wait()
+    write_output.wait()
 
     each_near(lambda flip: back(flip).wait_send())
 
@@ -1100,9 +1119,9 @@
             jax.ShapeDtypeStruct((16, span), f32),
         ),
         in_specs=[vm] * 4 + [ANY] * 13,
-        out_specs=(vm,) * 7,
+        out_specs=(ANY, ANY) + (vm,) * 5,
         scratch_shapes=[
-            v((length, 8), f32), v((slots, model), low), v((8, 1, capacity), f32), v((slots, model), low),
+            rows_low, v((length, model), f32), v((length, 8), f32), v((slots, model), low), v((8, 1, capacity), f32), v((slots, model), low),
             v((length, model), f32), rows_low, rows_low, rows_low,
             v(qkv.shape, low), v(full_a.shape, low), v(full_out.shape, low),
             v((model, length), low), v((model, length), low), rows_low,
@@ -1111,7 +1130,7 @@
             v((4, 4, block, width), low), v((4, 4, block, width), low), v((4, 4, block, width), low),
             v((4, 2, 2, cut, width), low), v((4, 2, cut, width), low), v((3, block, width), low),
             v((7, 16, span), f32), v((16, span), f32), v((3, 16, span), f32),
-            sems((9,)), sems((7,)), sems((7,)), sems((7,)), sems((7,)), sems((7,)), sems((7,)), sems((3,)), sems((2,)),
+            sems((9,)), sems((7,)), sems((7,)), sems((7,)), sems((7,)), sems((7,)), sems((7,)), sems((3,)), sems((2,)), sems((2,)),
             sems((4, 4, 2)), sems((4, 4, 2)), sems((4, 2, 2, 3)), sems((4, 2, 2, 3)),
             sems((2, 3)), sems((2, 3)), sems((7,)), sems((7,)), sems((3,)), sems((3,)),
         ],

time: 405 us -> 402 us (level)
  transfers between devices with their start and end apart: 2 -> 2, of which waited for: 0 -> 0; matrix products, arithmetic and copies ran while one was open for 7% -> 7% of each run, Pallas kernels for 57% -> 58%
where the time goes in v7:
time: 402 us; the launch traced here: 401 us
  Pallas kernels  354 us (88%)
  local copies, waits for them, and re-layouts  14.5 us (4%)
  between operations  14.5 us (4%)
  matrix products  10.1 us (3%)
  other arithmetic  7.95 us (2%)
    pallas_call x1, Pallas kernels, run_backward(): pl.pallas_call(backward_kernel, out_shape=(jax.ShapeDtypeStruct((length,...  141 us
    pallas_call x1, Pallas kernels, run_expert(): pl.pallas_call(expert_kernel, out_shape=(jax.ShapeDtypeStruct((slots, mod...  78.1 us
    pallas_call x1, Pallas kernels, gather_plane(): pl.pallas_call(functools.partial(plane_kernel, count), out_shape=tuple((j...  56.3 us
    pallas_call x1, Pallas kernels, gather_line(): pl.pallas_call(line_kernel, out_shape=(jax.ShapeDtypeStruct((own_a.shape[...  39.4 us
    pallas_call x1, Pallas kernels, spread_tokens(): pl.pallas_call(spread_kernel, out_shape=(jax.ShapeDtypeStruct((8 * own_c....  33.5 us
  transfers between devices with their start and end apart: 2, of which 0 were waited for; matrix products, arithmetic and copies ran while one was open for 7% of the time, Pallas kernels for 58%

profile of v7, /device:TPU:0, one launch (start us, length us, event | category | flops | bytes accessed | tf_op | source)
XLA Modules:
  0.0 401.0 jit_solution(4300783850426597572)
XLA Ops:
  7.2 1.0 fusion.15
  8.3 1.3 pad_add_fusion.own_s
  9.6 1.7 concatenate.6.own_a
  11.3 39.4 %shard_map.229 = (bf16[192,2560]{1,0:T(8,128)(2,1)}, bf16[192,1536]{1,0:T(8,128)(2,1)}, bf16[4,8,16,256]{3,2,1,0:T(8,128)(2,1)}, bf16[2048,1536]{1,0:T(8,128)(2,1)}, bf16[384,2048]{1,0:T(8,128)(2,1)}) custom-call(bf16[192,640]{1,0:T(8,128)(2,1)} %concatenate.6.own_a, bf16[192,384]{1,0:T(8,128)(2,1)} %own_b.1, bf16[16,256]{1,0:T(8,128)(2,1)} %pad_add_fusion.own_s, ...), custom_call_target="tpu_custom_call" | custom-call | bytes 1000000 | tf_op jit(solution)/shard_map/pallas_call | solution.py:225
  50.7 0.9 convert_bitcast_fusion
  51.7 56.3 %shard_map.230 = (bf16[1536,2560]{1,0:T(8,128)(2,1)}, bf16[1536,1536]{1,0:T(8,128)(2,1)}) custom-call(bf16[192,2560]{1,0:T(8,128)(2,1)} %get-tuple-element.47.refs_0_, bf16[192,1536]{1,0:T(8,128)(2,1)} %get-tuple-element.48.refs_1_), custom_call_target="tpu_custom_call" | custom-call | bytes 1000000 | tf_op jit(solution)/shard_map/pallas_call | solution.py:283
  108.6 0.9 copy-done.5
  109.4 5.5 %convolution_convert_fusion.qkv_hbm = bf16[256,2560]{1,0:T(8,128)(2,1)S(1)} fusion(bf16[256,1536]{1,0:T(8,128)(2,1)S(1)} %fusion.5.normed_hbm, bf16[1536,2560]{1,0:T(8,128)(2,1)} %get-tuple-element.49.full_a_hbm), kind=kOutput, calls=%fused_computation.5 | convolution fusion | flops 2013921280 | bytes 9961472 | tf_op jit(solution)/shard_map/dot_general | solution.py:1150
  114.9 0.5 reshape.186
  115.5 1.2 slice.74
  116.6 1.0 fusion.14
  117.6 1.1 copy.56
  118.7 1.5 copy.70
  120.6 0.9 slice_bitcast_fusion
  121.8 1.1 fusion.1
  122.9 1.4 fusion
  124.3 1.8 fusion.6
  126.1 0.4 slice-done.1
  126.5 1.5 multiply_reduce_fusion
  128.8 0.6 select_bitcast_fusion.own_g
  129.4 33.5 %shard_map.231 = (bf16[2048,1536]{1,0:T(8,128)(2,1)}, f32[8,8,256]{2,1,0:T(8,128)}) custom-call(bf16[256,1536]{1,0:T(8,128)(2,1)} %copy-done.2, f32[8,256]{1,0:T(8,128)} %select_bitcast_fusion.own_g), custom_call_target="tpu_custom_call" | custom-call | bytes 1000000 | tf_op jit(solution)/shard_map/pallas_call | solution.py:324
  162.9 0.9 compare_convert_fusion
  163.8 0.6 reduce-window.16
  164.7 0.6 compare_select_fusion.key
  165.4 78.1 %shard_map.232 = (bf16[1024,1536]{1,0:T(8,128)(2,1)}, bf16[1024,1536]{1,0:T(8,128)(2,1)}, f32[8,1,128]{2,1,0:T(1,128)}, bf16[1536,2048]{1,0:T(8,128)(2,1)}, f32[...) custom-call(s32[8,1,256]{2,1,0:T(1,128)} %compare_select_fusion.key, f32[8,1,256]{2,1,0:T(1,128)} %copy-done.7, ...), custom_call_target="tpu_custom_call" | custom-call | bytes 1000000 | tf_op jit(solution)/shard_map/pallas_call | solution.py:678
  243.8 0.6 add.89.lse
  244.4 0.6 reduce-window.14
  245.2 0.7 convert_element_type.82.gains
  245.9 0.8 pad.19.router_p
  246.9 0.6 concatenate.7.table
  247.5 140.8 %shard_map.233 = (bf16[256,1536]{1,0:T(8,128)(2,1)}, f32[256,1536]{1,0:T(8,128)}, f32[192,384]{1,0:T(8,128)}, f32[192,128]{1,0:T(8,128)}, f32[192,128]{1,0:T(8,1...) custom-call(f32[8,256]{1,0:T(8,128)} %concatenate.7.table, bf16[1536,128]{1,0:T(8,128)(2,1)} %pad.19.router_p, ...), custom_call_target="tpu_custom_call" | custom-call | bytes 1000000 | tf_op jit(solution)/shard_map/pallas_call | solution.py:1110
  388.4 5.8 %shard_map.234 = (bf16[256,1536]{1,0:T(8,128)(2,1)}, f32[256,1536]{1,0:T(8,128)}, f32[192,384]{1,0:T(8,128)}, f32[192,128]{1,0:T(8,128)}, f32[192,128]{1,0:T(8,1...) custom-call(bf16[256,1536]{1,0:T(8,128)(2,1)} %get-tuple-element.59., ...), custom_call_target="tpu_custom_call" | custom-call | tf_op jit(solution)/shard_map/pallas_call | solution.py:385
  (71 shorter events, 3.1 us)
Async XLA Ops:
  7.2 158.2 %all-gather.2.cloned.1.call-start = ((), (), s32[]{:S(2)}) async-start(), calls=%async_computation.1 | async-start | bytes 7864320 | tf_op jit(solution)/shard_map/all_gather | solution.py:1313
  11.3 96.8 %copy-start.1 = (bf16[256,1536]{1,0:T(8,128)(2,1)S(1)}, bf16[256,1536]{1,0:T(8,128)(2,1)}, u32[]{:S(2)}) copy-start(bf16[256,1536]{1,0:T(8,128)(2,1)} %tokens_hbm.1) | copy-start | bytes 2359300
  50.7 337.7 %reduce-scatter.2.cloned.1.call-start = ((), (), s32[]{:S(2)}) async-start(), calls=%async_computation.2 | async-start | bytes 7864320 | tf_op jit(solution)/shard_map/reduce_scatter | solution.py:1368
  108.5 0.9 copy-start.5
  114.9 5.4 %copy-start.4 = (bf16[256,2560]{1,0:T(8,128)(2,1)}, bf16[256,2560]{1,0:T(8,128)(2,1)S(1)}, u32[]{:S(2)}) copy-start(bf16[256,2560]{1,0:T(8,128)(2,1)S(1)} %convolution_convert_fusion.qkv_hbm) | copy-start | bytes 3932164
  115.4 6.3 %copy-start.9 = (s32[1,256]{1,0:T(1,128)S(1)}, s32[1,256]{1,0:T(1,128)}, u32[]{:S(2)}) copy-start(s32[1,256]{1,0:T(1,128)} %param.25) | copy-start | bytes 3076
  117.6 2.8 copy-start.6
  122.9 3.2 slice-start
  124.3 2.2 slice-start.1
  126.0 1.9 copy-start.3
  128.0 115.5 %copy-start = (f32[256,1536]{1,0:T(8,128)}, f32[256,1536]{1,0:T(8,128)S(1)}, u32[]{:S(2)}) copy-start(f32[256,1536]{1,0:T(8,128)S(1)} %get-tuple-element.95.hidden_hbm) | copy-start | bytes 4718596
  128.0 0.7 copy-start.8
  128.2 1.2 copy-start.2
  163.8 1.6 copy-start.7
Sparse Core Ops, SparseCore 0:
  50.8 113.9 all-gather.1
  243.6 134.3 reduce-scatter.1

commit v8 on v7

--- a/solution.py
+++ b/solution.py
@@ -402,7 +402,7 @@
     capacity = slots // sources
     units = gu.shape[1] // 2
     width = units // 4
-    chunk = 256
+    chunk = 512
     x = in_ref
     right_dev, left_dev = {"col": (col + 1) % 4}, {"col": (col + 3) % 4}
 
@@ -661,10 +661,14 @@
 
     def written(i, carry):
         of_chip(i)[1].wait()
-        rows = pl.ds(pl.multiple_of(i * chunk, chunk), chunk)
-        pltpu.make_async_copy(prod_ref.at[rows, :], prod_out.at[rows, :], prod_sem.at[i]).wait()
         return carry
     lax.fori_loop(0, 4, written, 0)
+
+    def produced(m, carry):
+        rows = pl.ds(pl.multiple_of(m * chunk, chunk), chunk)
+        pltpu.make_async_copy(prod_ref.at[rows, :], prod_out.at[rows, :], prod_sem.at[m]).wait()
+        return carry
+    lax.fori_loop(0, slots // chunk, produced, 0)
 
 
 def run_expert(key, mine, normed, upstream, full_gu, own_down):
@@ -733,7 +737,7 @@
     width_b = sum_b.shape[1]
     width_a = own.shape[3] - width_b
     cut = block // 2
-    half = length // 2
+    half = length
     f32, low = jnp.float32, branch.dtype
     sib = {"row": row_at(row, SIB)}
     to_x, to_y = {"row": row_at(row, X)}, {"row": row_at(row, Y)}
@@ -836,7 +840,7 @@
         d_tokens[rows, :] = grad
         branch[rows, :] = grad.astype(low)
         return carry
-    lax.fori_loop(0, 2, to_hidden, 0)
+    lax.fori_loop(0, 1, to_hidden, 0)
     small[0:8, :] = t_dot(lgs[...], two[...])[0:8, :]
 
     def nth(k):
@@ -988,7 +992,7 @@
         inner = jnp.mean(scaled * x, axis=1, keepdims=True)
         d_tokens[rows, :] += factor * scaled - x * (factor * factor * factor * inner)
         return carry
-    lax.fori_loop(0, 2, to_tokens, 0)
+    lax.fori_loop(0, 1, to_tokens, 0)
     write_tokens = pltpu.make_async_copy(d_tokens, d_hbm, write.at[0])
     write_tokens.start()
 
@@ -1027,7 +1031,7 @@
             total = total + dot(picked, rec_prod[...]) * cols[rows, 4 + k : 5 + k]
         out_ref[rows, :] = total.astype(low)
         return carry
-    lax.fori_loop(0, 2, to_output, 0)
+    lax.fori_loop(0, 1, to_output, 0)
     write_output = pltpu.make_async_copy(out_ref, out_hbm, write.at[1])
     write_output.start()
 

time: 402 us -> 402 us (level)
  no operation moved by 1% of the time
where the time goes in v8:
time: 402 us; the launch traced here: 400 us
  Pallas kernels  353 us (88%)
  between operations  14.5 us (4%)
  local copies, waits for them, and re-layouts  14.3 us (4%)
  matrix products  10.1 us (3%)
  other arithmetic  7.96 us (2%)
    pallas_call x1, Pallas kernels, run_backward(): pl.pallas_call(backward_kernel, out_shape=(jax.ShapeDtypeStruct((length,...  141 us
    pallas_call x1, Pallas kernels, run_expert(): pl.pallas_call(expert_kernel, out_shape=(jax.ShapeDtypeStruct((slots, mod...  77.5 us
    pallas_call x1, Pallas kernels, gather_plane(): pl.pallas_call(functools.partial(plane_kernel, count), out_shape=tuple((j...  56.3 us
    pallas_call x1, Pallas kernels, gather_line(): pl.pallas_call(line_kernel, out_shape=(jax.ShapeDtypeStruct((own_a.shape[...  39.4 us
    pallas_call x1, Pallas kernels, spread_tokens(): pl.pallas_call(spread_kernel, out_shape=(jax.ShapeDtypeStruct((8 * own_c....  33.5 us
  transfers between devices with their start and end apart: 2, of which 0 were waited for; matrix products, arithmetic and copies ran while one was open for 7% of the time, Pallas kernels for 58%

profile of v8, /device:TPU:0, one launch (start us, length us, event | category | flops | bytes accessed | tf_op | source)
XLA Modules:
  0.0 400.1 jit_solution(17174761219596195788)
XLA Ops:
  7.2 1.0 fusion.15
  8.3 1.3 pad_add_fusion.own_s
  9.6 1.7 concatenate.6.own_a
  11.3 39.4 %shard_map.229 = (bf16[192,2560]{1,0:T(8,128)(2,1)}, bf16[192,1536]{1,0:T(8,128)(2,1)}, bf16[4,8,16,256]{3,2,1,0:T(8,128)(2,1)}, bf16[2048,1536]{1,0:T(8,128)(2,1)}, bf16[384,2048]{1,0:T(8,128)(2,1)}) custom-call(bf16[192,640]{1,0:T(8,128)(2,1)} %concatenate.6.own_a, bf16[192,384]{1,0:T(8,128)(2,1)} %own_b.1, bf16[16,256]{1,0:T(8,128)(2,1)} %pad_add_fusion.own_s, ...), custom_call_target="tpu_custom_call" | custom-call | bytes 1000000 | tf_op jit(solution)/shard_map/pallas_call | solution.py:225
  50.7 0.9 convert_bitcast_fusion
  51.7 56.3 %shard_map.230 = (bf16[1536,2560]{1,0:T(8,128)(2,1)}, bf16[1536,1536]{1,0:T(8,128)(2,1)}) custom-call(bf16[192,2560]{1,0:T(8,128)(2,1)} %get-tuple-element.47.refs_0_, bf16[192,1536]{1,0:T(8,128)(2,1)} %get-tuple-element.48.refs_1_), custom_call_target="tpu_custom_call" | custom-call | bytes 1000000 | tf_op jit(solution)/shard_map/pallas_call | solution.py:283
  108.6 0.9 copy-done.5
  109.4 5.5 %convolution_convert_fusion.qkv_hbm = bf16[256,2560]{1,0:T(8,128)(2,1)S(1)} fusion(bf16[256,1536]{1,0:T(8,128)(2,1)S(1)} %fusion.5.normed_hbm, bf16[1536,2560]{1,0:T(8,128)(2,1)} %get-tuple-element.49.full_a_hbm), kind=kOutput, calls=%fused_computation.5 | convolution fusion | flops 2013921280 | bytes 9961472 | tf_op jit(solution)/shard_map/dot_general | solution.py:1154
  114.9 0.3 reshape.186
  115.3 1.2 slice.74
  116.4 1.0 fusion.14
  117.4 1.1 copy.56
  118.6 1.5 copy.70
  120.5 0.9 slice_bitcast_fusion
  121.6 1.1 fusion.1
  122.7 1.4 fusion
  124.1 1.8 fusion.6
  125.9 0.4 slice-done.1
  126.3 1.5 multiply_reduce_fusion
  128.7 0.6 select_bitcast_fusion.own_g
  129.3 33.5 %shard_map.231 = (bf16[2048,1536]{1,0:T(8,128)(2,1)}, f32[8,8,256]{2,1,0:T(8,128)}) custom-call(bf16[256,1536]{1,0:T(8,128)(2,1)} %copy-done.2, f32[8,256]{1,0:T(8,128)} %select_bitcast_fusion.own_g), custom_call_target="tpu_custom_call" | custom-call | bytes 1000000 | tf_op jit(solution)/shard_map/pallas_call | solution.py:324
  162.8 0.9 compare_convert_fusion
  163.6 0.6 reduce-window.16
  164.6 0.6 compare_select_fusion.key
  165.2 77.5 %shard_map.232 = (bf16[1024,1536]{1,0:T(8,128)(2,1)}, bf16[1024,1536]{1,0:T(8,128)(2,1)}, f32[8,1,128]{2,1,0:T(1,128)}, bf16[1536,2048]{1,0:T(8,128)(2,1)}, f32[...) custom-call(s32[8,1,256]{2,1,0:T(1,128)} %compare_select_fusion.key, f32[8,1,256]{2,1,0:T(1,128)} %copy-done.7, ...), custom_call_target="tpu_custom_call" | custom-call | bytes 1000000 | tf_op jit(solution)/shard_map/pallas_call | solution.py:682
  243.0 0.6 add.89.lse
  243.7 0.6 reduce-window.14
  244.5 0.7 convert_element_type.82.gains
  245.2 0.8 pad.19.router_p
  246.2 0.6 concatenate.7.table
  246.8 140.6 %shard_map.233 = (bf16[256,1536]{1,0:T(8,128)(2,1)}, f32[256,1536]{1,0:T(8,128)}, f32[192,384]{1,0:T(8,128)}, f32[192,128]{1,0:T(8,128)}, f32[192,128]{1,0:T(8,1...) custom-call(f32[8,256]{1,0:T(8,128)} %concatenate.7.table, bf16[1536,128]{1,0:T(8,128)(2,1)} %pad.19.router_p, ...), custom_call_target="tpu_custom_call" | custom-call | bytes 1000000 | tf_op jit(solution)/shard_map/pallas_call | solution.py:1114
  387.5 5.8 %shard_map.234 = (bf16[256,1536]{1,0:T(8,128)(2,1)}, f32[256,1536]{1,0:T(8,128)}, f32[192,384]{1,0:T(8,128)}, f32[192,128]{1,0:T(8,128)}, f32[192,128]{1,0:T(8,1...) custom-call(bf16[256,1536]{1,0:T(8,128)(2,1)} %get-tuple-element.59., ...), custom_call_target="tpu_custom_call" | custom-call | tf_op jit(solution)/shard_map/pallas_call | solution.py:385
  (71 shorter events, 3.1 us)
Async XLA Ops:
  7.2 158.0 %all-gather.2.cloned.1.call-start = ((), (), s32[]{:S(2)}) async-start(), calls=%async_computation.1 | async-start | bytes 7864320 | tf_op jit(solution)/shard_map/all_gather | solution.py:1317
  11.3 96.8 %copy-start.1 = (bf16[256,1536]{1,0:T(8,128)(2,1)S(1)}, bf16[256,1536]{1,0:T(8,128)(2,1)}, u32[]{:S(2)}) copy-start(bf16[256,1536]{1,0:T(8,128)(2,1)} %tokens_hbm.1) | copy-start | bytes 2359300
  50.7 336.8 %reduce-scatter.2.cloned.1.call-start = ((), (), s32[]{:S(2)}) async-start(), calls=%async_computation.2 | async-start | bytes 7864320 | tf_op jit(solution)/shard_map/reduce_scatter | solution.py:1372
  108.5 0.9 copy-start.5
  114.9 5.2 %copy-start.4 = (bf16[256,2560]{1,0:T(8,128)(2,1)}, bf16[256,2560]{1,0:T(8,128)(2,1)S(1)}, u32[]{:S(2)}) copy-start(bf16[256,2560]{1,0:T(8,128)(2,1)S(1)} %convolution_convert_fusion.qkv_hbm) | copy-start | bytes 3932164
  115.3 6.3 %copy-start.9 = (s32[1,256]{1,0:T(1,128)S(1)}, s32[1,256]{1,0:T(1,128)}, u32[]{:S(2)}) copy-start(s32[1,256]{1,0:T(1,128)} %param.25) | copy-start | bytes 3076
  117.4 2.8 copy-start.6
  122.7 3.2 slice-start
  124.1 2.2 slice-start.1
  125.9 1.9 copy-start.3
  127.8 114.9 %copy-start = (f32[256,1536]{1,0:T(8,128)}, f32[256,1536]{1,0:T(8,128)S(1)}, u32[]{:S(2)}) copy-start(f32[256,1536]{1,0:T(8,128)S(1)} %get-tuple-element.95.hidden_hbm) | copy-start | bytes 4718596
  127.8 0.7 copy-start.8
  128.1 1.2 copy-start.2
  163.6 1.6 copy-start.7
Sparse Core Ops, SparseCore 0:
  50.8 113.9 all-gather.1
  242.9 134.8 reduce-scatter.1
